TPU v7x, 32 devices: a whole 2x2x4 slice. The times are simulated.
32 devices in a mesh: groups: 2 (over y), gx: 4 (over z), gy: 4 (over x, core).
Axes of the slice: x: 2, y: 2, z: 4, core: 2. Of those that a mesh axis runs over, the one named last changes fastest.
Arguments:
- courant: float32 [32, 256, 128], P('gx', 'gy'), may hold values from 0.04 to 0.16
- state_prev: float32 [64, 256, 128], P(('groups', 'gx'), 'gy'), parts along dimension 0, may hold values from -6 to 6
- state_now: float32 [64, 256, 128], P(('groups', 'gx'), 'gy'), parts along dimension 0, may hold values from -6 to 6
- adjoint_now: float32 [64, 256, 128], P(('groups', 'gx'), 'gy'), parts along dimension 0, may hold values from -6 to 6
- adjoint_next: float32 [64, 256, 128], P(('groups', 'gx'), 'gy'), parts along dimension 0, may hold values from -6 to 6
- source_cell: int32 [32], P('groups'), parts along dimension 0, may hold values from 0 to 1048575
- wavelet: float32 [12, 32], P(None, 'groups'), parts along dimension 1, may hold values from -24 to 24
- observed: float32 [24, 4, 4, 4, 128], P('groups', 'gx', 'gy'), parts along dimension 0, may hold values from -6 to 6
- receiver_cell: int32 [4, 4, 4, 128], P('gx', 'gy'), may hold values from 0 to 65535
- receiver_count: int32 [4, 4, 4], P('gx', 'gy'), may hold values from 0 to 128, as said below
Outputs:
- gradient: float32 [64, 256, 128], P(('groups', 'gx'), 'gy'), parts along dimension 0
- trace_residual: float32 [24, 4, 4, 4, 128], P('groups', 'gx', 'gy'), parts along dimension 0
There are 2 independent parts, one for each index of `groups`. A program takes and returns all parts, laid end to end along the dimension named above; an argument that names none is the same for every part. Nothing has to cross between parts.
Inputs may be any that keep to these rules, and one draw needn't show every extreme that they name: receiver_count[k, j, i] counts the used slots that trace tile (i, j) holds for slab k; in every draw one slab k takes 128 from every tile i of strip 0.
All inputs are finite; a program needn't handle non-finite values.
Results may differ from a plain program's by a relative error of at most 0.00002.
Values sent between devices are 32-bit elements; how exact they have to be, the bound alone decides.
No kernel may reach another device: no remote copies, remote signals or barrier semaphores. Data moves between devices by JAX's collectives and lax.ppermute only.
A program may use at most 64 MiB of HBM per device.

v0:
```python
import functools

import jax
import jax.numpy as jnp
from jax import lax
from jax.experimental import pallas as pl
from jax.experimental.pallas import tpu as pltpu
from jax.sharding import PartitionSpec as P

STEPS = 12
SPONGE = 8
REACH = 4
DEPTH = 4
LANES = 128
ROWS = 8


stencil = (-205.0 / 72.0, 8.0 / 5.0, -1.0 / 5.0, 8.0 / 315.0, -1.0 / 560.0)
damping_peak = 0.3


class Layout:
    def __init__(self, count_x, count_y, width_x, width_y):
        self.count_x, self.count_y = count_x, count_y
        self.width_x, self.width_y = width_x, width_y
        self.chunk = width_y // count_x
        self.wide = width_x * count_x
        self.tiles = self.wide // ROWS
        self.whole_y = width_y * count_y
        self.margin = REACH * DEPTH
        self.extent = self.chunk + 2 * self.margin
        self.stride = self.tiles * 2 * ROWS
        self.padded_rows = self.extent * self.stride + ROWS
        self.kept = self.margin - REACH
        self.inner = self.extent - 2 * REACH
        self.rows = self.chunk * self.wide
        self.cells = self.chunk * width_x
        self.near = self.chunk + 2 * REACH
        self.state_rows = (self.chunk + self.near) * self.wide
        self.lacking = range(REACH, self.chunk - REACH)
        self.send_rows = (self.chunk + len(self.lacking)) * self.wide

    def at(self, place):
        pair, rest = divmod(place, 2 * self.count_x)
        chip, core = divmod(rest, 2)
        slab = chip if pair % 2 == 0 else self.count_x - 1 - chip
        return slab * self.count_y + 2 * pair + core

    def to_chunks(self, turn):
        moves = []
        for slab in range(self.count_x):
            for strip in range(self.count_y):
                moves.append((slab * self.count_y + strip, self.at(strip * self.count_x + (slab ^ turn))))
        return moves

    def to_slabs(self, turn):
        return [(target, source) for source, target in self.to_chunks(turn)]

    def swaps(self, first):
        moves = []
        for place in range(first, self.count_x * self.count_y - 1, 2):
            moves += [(self.at(place), self.at(place + 1)), (self.at(place + 1), self.at(place))]
        return moves


def fits(count_x, count_y, width_x, width_y, depth_z):
    return (
        count_x & (count_x - 1) == 0
        and count_y % 2 == 0
        and width_x == ROWS
        and width_x * count_x == ROWS * REACH
        and depth_z == LANES
        and width_y == count_x * REACH * DEPTH
    )


def f32(*shape):
    return jax.ShapeDtypeStruct(shape, jnp.float32)


def call(
    kernel, ints, arrays, outs, scratch=(), cost=1_000_000, space=pltpu.VMEM, aliases=None, limit=32 * 1024 * 1024
):
    return pl.pallas_call(
        kernel,
        out_shape=tuple(outs),
        in_specs=[pl.BlockSpec(memory_space=pltpu.SMEM)] * len(ints)
        + [pl.BlockSpec(memory_space=space)] * len(arrays),
        out_specs=tuple(pl.BlockSpec(memory_space=pltpu.VMEM) for _ in outs),
        scratch_shapes=list(scratch),
        input_output_aliases=aliases or {},
        compiler_params=pltpu.CompilerParams(vmem_limit_bytes=limit),
        cost_estimate=pl.CostEstimate(flops=cost, bytes_accessed=cost, transcendentals=0),
    )(*ints, *arrays)


def aligned(value, to=ROWS):
    return pl.multiple_of(value, to)


def cut_blocks(lay, slab_ref, count_ref, *refs):
    inputs, refs = refs[:7], refs[7:]
    sends, back_sends = refs[: lay.count_x], refs[lay.count_x : 2 * lay.count_x]
    held, held_cell, held_traces, done = refs[2 * lay.count_x :]
    targets = [held.at[index] for index in range(5)] + [held_cell, held_traces]
    copies = [
        pltpu.make_async_copy(source, target, done.at[index])
        for index, (source, target) in enumerate(zip(inputs, targets))
    ]
    for copy in copies:
        copy.start()
    for copy in copies:
        copy.wait()
    slab = slab_ref[0]
    slots = lax.broadcasted_iota(jnp.int32, (1, LANES), 1)
    used = []
    for tile in range(lay.count_x):
        cell = jnp.where(slots < count_ref[tile], held_cell[tile : tile + 1, :], -1)
        used.append(cell.astype(jnp.float32))
    for turn in range(lay.count_x):
        start = (slab ^ turn) * lay.chunk
        for index in range(5):
            target, first = (sends[turn], index) if index < 3 else (back_sends[turn], index - 3)
            for y in range(lay.chunk):
                row = (first * lay.chunk + y) * ROWS
                target[row : row + ROWS, :] = held[index, pl.ds(start + y, ROWS, stride=lay.width_y), :]
        for tile in range(lay.count_x):
            row = 3 * lay.cells + tile
            sends[turn][row : row + 1, :] = used[tile]
        row = 2 * lay.cells
        back_sends[turn][row : row + held_traces.shape[0], :] = held_traces[...]


def join_fields(lay, own_slot, odd, pieces, joined, state, courant, send_next, send_twin):
    fields = joined.shape[0]
    for turn, piece in enumerate(pieces):
        start_x = (own_slot ^ turn) * ROWS
        for field in range(fields):
            for y in range(lay.chunk):
                row = (field * lay.chunk + y) * ROWS
                joined[field, pl.ds(aligned(y * lay.wide + start_x), ROWS), :] = piece[row : row + ROWS, :]
    kept_rows = lay.kept * lay.wide
    for field in range(fields):
        target, first = (state, 0) if field == 0 else (state, (lay.chunk + REACH) * lay.wide)
        if field == 2:
            target, first = courant, 0
        for y in range(lay.chunk):
            for tile in range(lay.tiles):
                values = joined[field, pl.ds(y * lay.wide + tile, ROWS, stride=lay.tiles), :]
                row = y * lay.wide + tile * ROWS
                target[first + row : first + row + ROWS, :] = values
                if field == 0:
                    send_next[row : row + ROWS, :] = values
                    send_twin[row : row + ROWS, :] = values
    for field in range(1, fields):
        source, first = (state, (lay.chunk + REACH) * lay.wide) if field == 1 else (courant, 0)
        place = lay.rows + (field - 1) * kept_rows
        skipped = (lay.chunk - lay.kept) * lay.wide
        ahead = source[pl.ds(aligned(first + odd * skipped), kept_rows), :]
        send_next[place : place + kept_rows, :] = ahead
        behind = source[pl.ds(aligned(first + (1 - odd) * skipped), kept_rows), :]
        send_twin[place : place + kept_rows, :] = behind


def join_forward(lay, where_ref, *refs):
    pieces, (state, courant, send_next, send_twin, codes, joined) = refs[: lay.count_x], refs[lay.count_x :]
    own_slot = where_ref[0]
    join_fields(lay, own_slot, where_ref[1], pieces, joined, state, courant, send_next, send_twin)
    first = 3 * lay.cells
    strip_cells = lay.width_y * LANES
    slab_row = lax.broadcasted_iota(jnp.int32, codes.shape, 0)
    found = jnp.full(codes.shape, -1.0, jnp.float32)
    for turn, piece in enumerate(pieces):
        cell = piece[first : first + lay.count_x, :].astype(jnp.int32)
        used = cell >= 0
        cell = jnp.maximum(cell, 0)
        x = lax.div(cell, jnp.int32(strip_cells))
        y = lax.rem(lax.div(cell, jnp.int32(LANES)), jnp.int32(lay.width_y)) - own_slot * lay.chunk
        inside = used & (y >= 0) & (y < lay.chunk)
        code = jnp.where(inside, (y * ROWS + x) * LANES + lax.rem(cell, jnp.int32(LANES)), -1)
        code = code.astype(jnp.float32)
        line = jnp.concatenate([code[tile : tile + 1, :] for tile in range(lay.count_x)], axis=1)
        found = jnp.where(slab_row == (own_slot ^ turn), jnp.broadcast_to(line, codes.shape), found)
    codes[...] = found


def join_adjoint(lay, where_ref, *refs):
    pieces, (tie, state, send_next, send_twin, joined) = refs[: lay.count_x], refs[lay.count_x :]
    join_fields(lay, where_ref[0], where_ref[1], pieces, joined, state, None, send_next, send_twin)


def load_state(lay, odd, first, now, prev, state, from_next, from_twin):
    def put(buffer, layer, ref, source):
        for tile in range(lay.tiles):
            row = layer * lay.stride + (2 * tile + 1) * ROWS
            values = ref[source * lay.wide + tile * ROWS : source * lay.wide + (tile + 1) * ROWS, :]
            buffer[pl.ds(row if isinstance(row, int) else aligned(row), ROWS), :] = values

    ahead = lay.margin + lay.chunk
    for y in range(lay.chunk):
        put(now, lay.margin + y, state, y)
        put(now, odd * ahead + y, from_next, y)
        put(now, (1 - odd) * ahead + y, from_twin, y)
    if first:
        for y in range(lay.chunk):
            put(prev, lay.margin + y, state, lay.chunk + REACH + y)
        for y in range(lay.kept):
            put(prev, odd * ahead + (1 - odd) * REACH + y, from_next, lay.chunk + y)
            put(prev, (1 - odd) * ahead + odd * REACH + y, from_twin, lay.chunk + y)
        return
    for y in range(lay.near):
        put(prev, lay.margin - REACH + y, state, lay.chunk + y)
    for index, y in enumerate(lay.lacking):
        put(prev, odd * ahead + y, from_next, lay.chunk + index)
        put(prev, (1 - odd) * ahead + y, from_twin, lay.chunk + index)


def store_state(lay, now, prev, state, send):
    def put(refs, target, buffer, layer):
        for tile in range(lay.tiles):
            row = layer * lay.stride + (2 * tile + 1) * ROWS
            values = buffer[row : row + ROWS, :]
            for ref, place in refs:
                ref[place * lay.wide + tile * ROWS : place * lay.wide + (tile + 1) * ROWS, :] = values

    for y in range(lay.chunk):
        put([(state, y), (send, y)], y, now, lay.margin + y)
    for y in range(lay.near):
        refs = [(state, lay.chunk + y)]
        if y - REACH in lay.lacking:
            refs.append((send, lay.chunk + y - REACH - lay.lacking[0]))
        put(refs, y, prev, lay.margin - REACH + y)


def split(values):
    high = values.astype(jnp.bfloat16)
    rest = values - high.astype(jnp.float32)
    middle = rest.astype(jnp.bfloat16)
    low = (rest - middle.astype(jnp.float32)).astype(jnp.bfloat16)
    return high, middle, low


def fill_band(band):
    apart = lax.broadcasted_iota(jnp.int32, (LANES, LANES), 0) - lax.broadcasted_iota(
        jnp.int32, (LANES, LANES), 1
    )
    weights = jnp.where(apart == 0, 3.0 * stencil[0], 0.0).astype(jnp.float32)
    for k in range(1, REACH + 1):
        weights = jnp.where(jnp.abs(apart) == k, stencil[k], weights)
    high, middle, low = split(weights)
    for index, part in enumerate((high, high, high, middle, middle, low)):
        band[index * LANES : (index + 1) * LANES, :] = part


def sweep(lay, step, now, prev, following, half, gain, band, inject=None):
    first_layer = REACH * (step + 1)
    group = 8
    reach_rows = REACH * lay.stride

    def layers(block, carry):
        start = first_layer + group * block
        base = aligned((start - REACH) * lay.stride)
        around = now.at[pl.ds(base, (group + 2 * REACH) * lay.stride)]
        middle_rows = pl.ds(aligned(base + reach_rows), group * lay.stride)
        former_rows, target = prev.at[middle_rows], following.at[middle_rows]
        flat = aligned((start - REACH) * lay.wide)
        flat_rows = pl.ds(flat, group * lay.wide)
        half_rows, gain_rows = half.at[flat_rows], gain.at[flat_rows]
        added = None if inject is None else inject.at[step, flat_rows]

        def place(y, tile):
            return (y * lay.tiles + tile) * 2 * ROWS + ROWS

        def at(y, tile):
            row = place(y + REACH, tile)
            return around[row : row + ROWS, :]

        def beside(y, tile, shift):
            return now[pl.ds(base + (place(y + REACH, tile) + shift), ROWS), :]

        centers = [[at(y, tile) for tile in range(lay.tiles)] for y in range(group)]
        high, middle, low = split(jnp.concatenate([tile for layer in centers for tile in layer], axis=0))
        along_z = jnp.dot(
            jnp.concatenate([high, middle, low, high, middle, high], axis=1),
            band[...],
            preferred_element_type=jnp.float32,
        )
        for y in range(group):
            lower = [beside(y, tile, -1) for tile in range(lay.tiles)]
            upper = [beside(y, tile, 1) for tile in range(lay.tiles)]
            line = lower + centers[y] + upper
            for tile in range(lay.tiles):
                flat_at = (y * lay.tiles + tile) * ROWS
                total = along_z[flat_at : flat_at + ROWS, :]
                for k in range(1, REACH + 1):
                    pair = line[lay.tiles + tile - k] + line[lay.tiles + tile + k]
                    total = total + stencil[k] * (pair + (at(y - k, tile) + at(y + k, tile)))
                if added is not None:
                    total = total + added[pl.ds(y * lay.wide + tile, ROWS, stride=lay.tiles), :]
                row = place(y, tile)
                former = former_rows[row : row + ROWS, :]
                change = (centers[y][tile] - former) + half_rows[flat_at : flat_at + ROWS, :] * total
                target[row : row + ROWS, :] = former + gain_rows[flat_at : flat_at + ROWS, :] * change
        return carry

    lax.fori_loop(0, (lay.extent - 2 * first_layer) // group, layers, 0)


def zero_between(lay, step, buffer):
    zeros = jnp.zeros((ROWS, LANES), jnp.float32)
    first = REACH * (step + 1)
    for row in range(first * lay.stride, (lay.extent - first) * lay.stride + 1, 2 * ROWS):
        buffer[row : row + ROWS, :] = zeros


def zero_buffers(lay, now, prev, following):
    zero_between(lay, 0, now)
    zero_between(lay, 1, following)
    zero_between(lay, 2, prev)


def keep_own(lay, step, following, history):
    for y in range(lay.chunk):
        for tile in range(lay.tiles):
            row = (lay.margin + y) * lay.stride + (2 * tile + 1) * ROWS
            place = step * lay.rows + y * lay.wide + tile * ROWS
            history[place : place + ROWS, :] = following[row : row + ROWS, :]


def forward(lay, phase, sources, ints, state, from_next, from_twin, courant, gain, drive, *refs):
    first, last = phase == 0, phase == STEPS // DEPTH - 1
    refs = list(refs)
    history = refs.pop(0)
    half = refs.pop(0) if first else courant
    if not last:
        state_out, send, tie = [refs.pop(0) for _ in range(3)]
        tie[...] = jnp.zeros_like(tie)
    now, prev, following, band, pulse = refs
    odd = ints[0]

    fill_band(band)
    load_state(lay, odd, first, now, prev, state, from_next, from_twin)
    zero_buffers(lay, now, prev, following)
    if first:
        tail = (lay.chunk + lay.kept) * lay.wide
        part = lay.kept * lay.wide
        half[part : part + lay.rows, :] = 0.5 * courant[...]
        ahead = part + lay.rows
        half[pl.ds(aligned(odd * ahead), part), :] = 0.5 * from_next[tail : tail + part, :]
        half[pl.ds(aligned((1 - odd) * ahead), part), :] = 0.5 * from_twin[tail : tail + part, :]
    for source in range(sources):
        flat = pl.ds(ints[1 + sources + source], 1)
        pulse[source : source + 1, :] = half[flat, :] * gain[flat, :]

    for step in range(DEPTH):
        sweep(lay, step, now, prev, following, half, gain, band)
        added = pulse[...] * drive[phase * DEPTH + step]
        places = [pl.ds(ints[1 + source], 1) for source in range(sources)]
        lines = [following[place, :] for place in places]
        for source, (place, line) in enumerate(zip(places, lines)):
            following[place, :] = line + added[source : source + 1, :]
        keep_own(lay, step, following, history)
        now, prev, following = following, now, prev

    if not last:
        store_state(lay, now, prev, state_out, send)


def slot_rows(codes, slab):
    code = codes[slab : slab + 1, :].astype(jnp.int32)
    row = jnp.where(code >= 0, lax.shift_right_arithmetic(code, 7), -1)
    return row, jnp.where(code >= 0, code & (LANES - 1), -1)


def record_slots(lay, history, codes, plain, record):
    for step in range(DEPTH):
        for y in range(lay.chunk):
            for tile in range(lay.tiles):
                row = step * lay.rows + y * lay.wide
                values = history[row + tile * ROWS : row + (tile + 1) * ROWS, :]
                plain[pl.ds(row + tile, ROWS, stride=lay.tiles), :] = values
    slots = codes.shape[1]
    width = 2 * LANES
    for slab in range(lay.count_x):
        cell_row, cell_z = slot_rows(codes, slab)
        tiles = []
        for step in range(DEPTH):
            for y in range(lay.chunk):
                row = step * lay.rows + y * lay.wide + slab * ROWS
                tiles.append(plain[row : row + ROWS, :])
        parts = jnp.concatenate(split(jnp.concatenate(tiles, axis=0)), axis=1)
        for start in range(0, slots, width):
            here = slice(start, start + width)
            z = lax.broadcasted_iota(jnp.int32, (LANES, width), 0)
            pick = jnp.where(z == cell_z[:, here], 1.0, 0.0).astype(jnp.bfloat16)
            found = jnp.dot(parts, jnp.concatenate([pick] * 3, axis=0), preferred_element_type=jnp.float32)
            wanted = lax.broadcasted_iota(jnp.int32, (lay.cells, width), 0) == cell_row[:, here]
            for step in range(DEPTH):
                part = jnp.where(wanted, found[step * lay.cells : (step + 1) * lay.cells, :], 0.0)
                row = step * lay.count_x + slab
                record[row : row + 1, here] = jnp.sum(part, axis=0, keepdims=True)


def record_phase(lay, history, codes, record, plain):
    record_slots(lay, history, codes, plain, record)


def record_last(lay, phases, where_ref, history, codes, *refs):
    earlier, refs = refs[: phases - 1], refs[phases - 1 :]
    observed, (misfit, plain, record) = refs[: lay.count_x], refs[lay.count_x :]
    record_slots(lay, history, codes, plain, record)
    block = DEPTH * lay.count_x
    for index, part in enumerate(list(earlier) + [record]):
        misfit[index * block : (index + 1) * block, :] = part[...]
    total = STEPS * lay.count_x
    for slab in range(lay.count_x):
        misfit[total + slab : total + slab + 1, :] = codes[slab : slab + 1, :]
    for turn, piece in enumerate(observed):
        place = pl.ds(aligned((where_ref[0] ^ turn) * LANES, LANES), LANES)
        used = jnp.concatenate([codes[:, place]] * STEPS, axis=0) >= 0
        seen = piece[2 * lay.cells : 2 * lay.cells + total, :]
        misfit[0:total, place] = jnp.where(used, misfit[0:total, place] - seen, 0.0)


def spread(lay, phase, side, misfit, inject):
    codes = misfit[STEPS * lay.count_x : (STEPS + 1) * lay.count_x, :]
    for slab in range(lay.count_x):
        cell_row, cell_z = slot_rows(codes, slab)
        slots = cell_row.shape[1]
        z = lax.broadcasted_iota(jnp.int32, (LANES, slots), 0)
        pick = jnp.where(z == cell_z, 1.0, 0.0).astype(jnp.bfloat16)
        hit = lax.broadcasted_iota(jnp.int32, (lay.cells, slots), 0) == cell_row
        hit = jnp.where(hit, 1.0, 0.0).astype(jnp.bfloat16)
        left, spans = [], []
        for step in range(DEPTH):
            low, high = 0, lay.chunk
            if side < 0:
                low = REACH * (step + 1) - lay.margin + lay.chunk
            if side > 0:
                high = lay.margin - REACH * (step + 1)
            if low >= high:
                continue
            row = (STEPS - 1 - phase * DEPTH - step) * lay.count_x + slab
            parts = split(misfit[row : row + 1, :])
            left.append(jnp.concatenate([hit[low * ROWS : high * ROWS, :] * part for part in parts], axis=1))
            spans.append((step, low, high))
        placed = lax.dot_general(
            jnp.concatenate(left, axis=0),
            jnp.concatenate([pick] * 3, axis=1),
            (((1,), (1,)), ((), ())),
            preferred_element_type=jnp.float32,
        )
        at = 0
        for step, low, high in spans:
            for y in range(low, high):
                layer = lay.margin + side * lay.chunk + y - REACH
                target = layer * lay.wide + slab * ROWS
                inject[step, target : target + ROWS, :] = placed[at : at + ROWS, :]
                at += ROWS


def spread_own(lay, phase, misfit, inject):
    spread(lay, phase, 0, misfit, inject)


def spread_sides(lay, phase, where_ref, own, misfit_next, misfit_twin, inject):
    odd = where_ref[1]

    @pl.when(odd == 1)
    def ahead_is_next():
        spread(lay, phase, 1, misfit_next, inject)
        spread(lay, phase, -1, misfit_twin, inject)

    @pl.when(odd == 0)
    def behind_is_next():
        spread(lay, phase, -1, misfit_next, inject)
        spread(lay, phase, 1, misfit_twin, inject)


def backward(lay, phase, where_ref, state, from_next, from_twin, half, gain, inject, *refs):
    first, last = phase == 0, phase == STEPS // DEPTH - 1
    refs = list(refs)
    history = refs.pop(0)
    if not last:
        state_out, send = refs.pop(0), refs.pop(0)
    now, prev, following, band = refs

    fill_band(band)
    load_state(lay, where_ref[1], first, now, prev, state, from_next, from_twin)
    zero_buffers(lay, now, prev, following)
    for step in range(DEPTH):
        sweep(lay, step, now, prev, following, half, gain, band, inject)
        keep_own(lay, step, following, history)
        now, prev, following = following, now, prev
    if not last:
        store_state(lay, now, prev, state_out, send)


def add_gradient(lay, before, adjoint, history, state, gradient):
    def layer(y, carry):
        place = aligned(y * lay.wide)
        own = pl.ds(place, lay.wide)
        fields = [state[pl.ds(aligned(place + (lay.chunk + REACH) * lay.wide), lay.wide), :], state[own, :]]
        fields += [history[pl.ds(aligned(place + step * lay.rows), lay.wide), :] for step in range(DEPTH)]
        total = None if before is None else before[own, :]
        for step in range(DEPTH):
            index = DEPTH - 1 - step
            accel = (fields[index + 2] - fields[index + 1]) - (fields[index + 1] - fields[index])
            term = adjoint[pl.ds(aligned(place + step * lay.rows), lay.wide), :] * accel
            total = term if total is None else total + term
        gradient[own, :] = total
        return carry

    lax.fori_loop(0, lay.chunk, layer, 0)


def gradient_first(lay, adjoint, history, state, gradient):
    add_gradient(lay, None, adjoint, history, state, gradient)


def gradient_later(lay, adjoint, history, state, before, gradient):
    add_gradient(lay, before, adjoint, history, state, gradient)


def gradient_last(lay, where_ref, adjoint, history, state, before, misfit, *refs):
    sends, (gradient, plain) = refs[: lay.count_x], refs[lay.count_x :]
    add_gradient(lay, before, adjoint, history, state, gradient)
    for y in range(lay.chunk):
        for tile in range(lay.tiles):
            row = y * lay.wide + tile * ROWS
            plain[pl.ds(y * lay.wide + tile, ROWS, stride=lay.tiles), :] = gradient[row : row + ROWS, :]
    total = STEPS * lay.count_x
    for turn, send in enumerate(sends):
        other = where_ref[0] ^ turn
        for y in range(lay.chunk):
            source = pl.ds(aligned(y * lay.wide + other * ROWS), ROWS)
            send[y * ROWS : (y + 1) * ROWS, :] = plain[source, :]
        tile = pl.ds(aligned(other * LANES, LANES), LANES)
        send[lay.cells : lay.cells + total, :] = misfit[0:total, tile]


def finish(lay, slab_ref, *refs):
    pieces, (gradient, residual) = refs[: lay.count_x], refs[lay.count_x :]
    total = None
    for turn, piece in enumerate(pieces):
        start = (slab_ref[0] ^ turn) * lay.chunk
        for x in range(ROWS):
            target = pl.ds(aligned(x * lay.width_y + start), lay.chunk)
            gradient[target, :] = piece[pl.ds(x, lay.chunk, stride=ROWS), :]
        part = piece[lay.cells : lay.cells + residual.shape[0], :]
        total = part if total is None else total + part
    residual[...] = total


def gain_rows(lay, first_y):
    x = jnp.arange(ROWS)[None, :] * lay.tiles + jnp.arange(lay.tiles)[:, None]
    y = first_y + REACH + jnp.arange(lay.inner)

    def ramp(position, count):
        gap = jnp.minimum(position, count - 1 - position)
        profile = jnp.maximum(SPONGE - gap, 0).astype(jnp.float32) / SPONGE
        return profile * profile

    damping = damping_peak * (ramp(x, lay.wide)[None] + ramp(y, lay.whole_y)[:, None, None])
    gain = (2.0 / (1.0 + damping)).reshape(lay.inner * lay.wide, 1)
    return jnp.broadcast_to(gain, (lay.inner * lay.wide, LANES))


def source_rows(lay, first_y, source_cell, wavelet):
    x = source_cell // (lay.whole_y * LANES)
    y = source_cell // LANES % lay.whole_y - first_y
    z = source_cell % LANES
    inside = (y >= REACH) & (y < lay.extent - REACH)
    tile, row = x % lay.tiles, x // lay.tiles
    padded = jnp.where(inside, y * lay.stride + (2 * tile + 1) * ROWS + row, ROWS // 2)
    flat = jnp.where(inside, (y - REACH) * lay.wide + tile * ROWS + row, 0)
    same = (padded[:, None] == padded[None, :]) & inside[None, :]
    spot = (z[:, None] == jnp.arange(LANES)[None, :]).astype(jnp.float32)
    lines = jnp.where(same[None, :, :, None], wavelet[:, None, :, None] * spot[None, None], 0.0)
    return padded, flat, jnp.sum(lines, axis=2)


def local_tiles(
    lay,
    courant,
    state_prev,
    state_now,
    adjoint_now,
    adjoint_next,
    source_cell,
    wavelet,
    observed,
    receiver_cell,
    receiver_count,
):
    axes = ("gx", "gy")
    slab = lax.axis_index("gx")
    strip = lax.axis_index("gy")
    pair = strip // 2
    chip = jnp.where(pair % 2 == 0, slab, lay.count_x - 1 - slab)
    place = (pair * lay.count_x + chip) * 2 + strip % 2
    odd = strip % 2
    first_y = place * lay.chunk - lay.margin
    slab_int = slab.reshape(1).astype(jnp.int32)
    where = jnp.stack([place % lay.count_x, odd]).astype(jnp.int32)

    count = lay.count_x
    sources = source_cell.shape[0]
    slots = count * receiver_cell.shape[3]
    flat = lambda values: values.reshape(-1, LANES)
    part = functools.partial

    def swap(to_next, to_twin):
        return (
            lax.ppermute(to_next, axes, lay.swaps(1)),
            lax.ppermute(to_twin, axes, lay.swaps(0)),
        )

    def after(value, others):
        return lax.optimization_barrier((value, others))[0]

    padded, flat_row, drive = source_rows(lay, first_y, source_cell, wavelet)
    gain = gain_rows(lay, first_y)
    ints = jnp.concatenate([odd.reshape(1), padded, flat_row]).astype(jnp.int32)

    traces = flat(observed)
    forward_rows = 3 * lay.cells + -(-count // ROWS) * ROWS
    back_rows = 2 * lay.cells + traces.shape[0]
    cuts = call(
        part(cut_blocks, lay),
        (slab_int, receiver_count.reshape(-1)),
        [flat(field) for field in (state_now, state_prev, courant, adjoint_now, adjoint_next)]
        + [receiver_cell.reshape(count, LANES), traces],
        [f32(forward_rows, LANES)] * count + [f32(back_rows, LANES)] * count,
        [
            pltpu.VMEM((5, lay.width_x * lay.width_y, LANES), jnp.float32),
            pltpu.VMEM((count, LANES), jnp.int32),
            pltpu.VMEM(traces.shape, jnp.float32),
            pltpu.SemaphoreType.DMA((7,)),
        ],
        space=pltpu.HBM,
        limit=60 * 1024 * 1024,
    )
    cuts, back_cuts = cuts[:count], cuts[count:]
    pieces = [lax.ppermute(cut, axes, lay.to_chunks(turn)) for turn, cut in enumerate(cuts)]
    pieces, ints, gain, drive = lax.optimization_barrier((pieces, ints, gain, drive))
    kept_rows = lay.kept * lay.wide
    tie_shape = f32(ROWS, LANES)
    state, own_courant, to_next, to_twin, codes = call(
        part(join_forward, lay),
        (where,),
        pieces,
        [f32(lay.state_rows, LANES), f32(lay.rows, LANES)]
        + [f32(lay.rows + 2 * kept_rows, LANES)] * 2
        + [f32(count, slots)],
        [pltpu.VMEM((3, lay.rows, LANES), jnp.float32)],
    )
    from_next, from_twin = swap(to_next, to_twin)

    back_pieces = []

    def move_adjoint(turns, tie):
        for turn in turns:
            back_pieces.append(lax.ppermute(after(back_cuts[turn], tie), axes, lay.to_chunks(turn)))

    move_adjoint(range(count // 2), codes)

    phases = STEPS // DEPTH
    step_cost = 8_000_000
    side_cost = 4_000_000
    history_shape = f32(DEPTH * lay.rows, LANES)
    state_shapes = [f32(lay.state_rows, LANES), f32(lay.send_rows, LANES)]
    buffers = [pltpu.VMEM((lay.padded_rows, LANES), jnp.float32)] * 3
    buffers += [pltpu.VMEM((6 * LANES, LANES), jnp.bfloat16)]
    record_scratch = [pltpu.VMEM((DEPTH * lay.rows, LANES), jnp.float32)]
    record_shape = (DEPTH * count, slots)
    histories, states, records = [], [], []
    half = own_courant
    for phase in range(phases):
        first, last = phase == 0, phase == phases - 1
        outs = [history_shape]
        if first:
            outs.append(f32(lay.inner * lay.wide, LANES))
        if not last:
            outs += state_shapes + [tie_shape]
        results = list(
            call(
                part(forward, lay, phase, sources),
                (ints,),
                [state, from_next, from_twin, half, gain, drive],
                outs,
                buffers + [pltpu.VMEM((sources, LANES), jnp.float32)],
                cost=step_cost,
            )
        )
        histories.append(results.pop(0))
        states.append(state)
        if first:
            half = results.pop(0)
        if last:
            continue
        state, send, tie = results
        send = after(send, back_pieces[-(count // 2) :])
        from_next, from_twin = swap(send, send)
        if first:
            move_adjoint(range(count // 2, count), tie)
    back_state, to_next, to_twin = call(
        part(join_adjoint, lay),
        (where,),
        back_pieces + [tie],
        [f32(lay.state_rows, LANES)] + [f32(lay.rows + kept_rows, LANES)] * 2,
        [pltpu.VMEM((2, lay.rows, LANES), jnp.float32)],
    )
    for history in histories[:-1]:
        records += call(
            part(record_phase, lay),
            (),
            [history, codes],
            [f32(*record_shape)],
            record_scratch,
            cost=side_cost,
        )
    arrived = (from_next, from_twin, records)
    back_from_next, back_from_twin = swap(after(to_next, arrived), after(to_twin, arrived))
    (misfit,) = call(
        part(record_last, lay, phases),
        (where,),
        [histories[-1], codes] + records + back_pieces,
        [f32(-(-(STEPS + 1) * count // ROWS) * ROWS, slots)],
        record_scratch + [pltpu.VMEM(record_shape, jnp.float32)],
        cost=side_cost,
    )

    misfit = after(misfit, [back_from_next, back_from_twin])
    misfit_next, misfit_twin = swap(misfit, misfit)
    state, from_next, from_twin = back_state, back_from_next, back_from_twin
    gradient = None
    inject_shape = f32(DEPTH, lay.inner * lay.wide, LANES)
    for phase in range(phases):
        first, last = phase == 0, phase == phases - 1
        (inject,) = call(part(spread_own, lay, phase), (), [misfit], [inject_shape], cost=side_cost)
        (inject,) = call(
            part(spread_sides, lay, phase),
            (where,),
            [inject, misfit_next, misfit_twin],
            [inject_shape],
            cost=side_cost,
            aliases={1: 0},
        )
        results = call(
            part(backward, lay, phase),
            (where,),
            [state, from_next, from_twin, half, gain, inject],
            [history_shape] + ([] if last else state_shapes),
            buffers,
            cost=step_cost,
        )
        arrays = [results[0], histories[phases - 1 - phase], states[phases - 1 - phase]]
        if last:
            sends = call(
                part(gradient_last, lay),
                (where,),
                arrays + [gradient, misfit],
                [f32(lay.cells + traces.shape[0], LANES)] * count,
                [pltpu.VMEM((lay.rows, LANES), jnp.float32)] * 2,
            )
            continue
        _, state, send = results
        from_next, from_twin = swap(send, send)
        kernel = gradient_first if first else gradient_later
        (gradient,) = call(
            part(kernel, lay), (), arrays + ([] if first else [gradient]), [f32(lay.rows, LANES)], cost=side_cost
        )
    pieces = [lax.ppermute(send, axes, lay.to_slabs(turn)) for turn, send in enumerate(sends)]
    gradient, residual = call(
        part(finish, lay),
        (slab_int,),
        pieces,
        [f32(lay.width_x * lay.width_y, LANES), f32(*traces.shape)],
    )
    return gradient.reshape(courant.shape), residual.reshape(observed.shape)


def local(courant, *rest):
    width_x, width_y, depth_z = courant.shape
    count_x, count_y = lax.axis_size("gx"), lax.axis_size("gy")
    if fits(count_x, count_y, width_x, width_y, depth_z):
        return local_tiles(Layout(count_x, count_y, width_x, width_y), courant, *rest)
    return local_blocks(courant, *rest)


def padded_2(cells, sides, width):
    for axis, dim in sides:
        count = lax.axis_size(axis)
        ends = count - 1
        head = lax.slice_in_dim(cells, 0, width, axis=dim)
        tail = lax.slice_in_dim(cells, cells.shape[dim] - width, cells.shape[dim], axis=dim)
        cells = jnp.concatenate(
            [
                lax.ppermute(tail, axis, [(i, (i + 1) % count) for i in range(ends)]),
                cells,
                lax.ppermute(head, axis, [((i + 1) % count, i) for i in range(ends)]),
            ],
            axis=dim,
        )
    return cells


def laplace(values):
    width_x, width_y, depth_z = values.shape
    padded = padded_2(values, (("gx", 0), ("gy", 1)), 4)
    z_padded = jnp.pad(values, ((0, 0), (0, 0), (4, 4)))
    summed = 3.0 * stencil[0] * values
    for offset in range(1, 5):
        paired = (
            padded[4 + offset : 4 + offset + width_x, 4 : 4 + width_y]
            + padded[4 - offset : 4 - offset + width_x, 4 : 4 + width_y]
        )
        paired = (
            paired
            + padded[4 : 4 + width_x, 4 + offset : 4 + offset + width_y]
            + padded[4 : 4 + width_x, 4 - offset : 4 - offset + width_y]
        )
        paired = (
            paired
            + z_padded[:, :, 4 + offset : 4 + offset + depth_z]
            + z_padded[:, :, 4 - offset : 4 - offset + depth_z]
        )
        summed = summed + stencil[offset] * paired
    return summed


def sponge(start, count, whole):
    position = start + jnp.arange(count, dtype=jnp.int32)
    edge_gap = jnp.minimum(position, whole - 1 - position)
    profile = jnp.maximum(SPONGE - edge_gap, 0).astype(jnp.float32) / SPONGE
    return profile * profile


def place_sum(indices, amounts, shape):
    flat = jnp.zeros((shape[0] * shape[1] * shape[2],), jnp.float32).at[indices].add(amounts)
    return flat.reshape(shape)


def local_blocks(
    courant,
    state_prev,
    state_now,
    adjoint_now,
    adjoint_next,
    source_cell,
    wavelet,
    observed,
    receiver_cell,
    receiver_count,
):
    shape = courant.shape
    width_x, width_y, depth_z = shape
    slab = lax.axis_index("gx")
    strip = lax.axis_index("gy")
    whole_x = width_x * lax.axis_size("gx")
    whole_y = width_y * lax.axis_size("gy")
    damping = damping_peak * (
        sponge(slab * width_x, width_x, whole_x)[:, None, None]
        + sponge(strip * width_y, width_y, whole_y)[None, :, None]
    )
    source_x = source_cell // (whole_y * depth_z) - slab * width_x
    source_y = source_cell // depth_z % whole_y - strip * width_y
    source_z = source_cell % depth_z
    inside = (source_x >= 0) & (source_x < width_x) & (source_y >= 0) & (source_y < width_y)
    source_flat = jnp.where(inside, (source_x * width_y + source_y) * depth_z + source_z, 0)
    source_weight = wavelet * inside.astype(jnp.float32)[None, :]
    senders = receiver_cell.shape[2]
    slots = receiver_cell.shape[3]
    cells = receiver_cell.reshape(-1)
    active = (
        jnp.arange(slots, dtype=jnp.int32)[None, :] < receiver_count.reshape(senders, 1)
    ).astype(jnp.float32)
    active_flat = active.reshape(-1)

    def advance(carry, weights):
        former, current = carry
        drive = laplace(current) + place_sum(source_flat, weights, shape)
        following = (2.0 * current - (1.0 - damping) * former + courant * drive) / (1.0 + damping)
        return (
            (current, following),
            (following - 2.0 * current + former, following.reshape(-1)[cells] * active_flat),
        )

    final_states, (accels, recorded) = lax.scan(advance, (state_prev, state_now), source_weight)
    recorded_tiles = recorded.reshape(STEPS, senders, 1, 1, slots)
    active_tiles = active.reshape(1, senders, 1, 1, slots)
    synthetic, mask_back = (
        lax.all_to_all(recorded_tiles, "gx", split_axis=1, concat_axis=3, tiled=True),
        lax.all_to_all(active_tiles, "gx", split_axis=1, concat_axis=3, tiled=True),
    )
    trace_residual = mask_back * (synthetic - observed)
    misfit = lax.all_to_all(trace_residual, "gx", split_axis=3, concat_axis=1, tiled=True)
    misfit_rows = misfit.reshape(STEPS, senders * slots)

    def retreat(carry, inputs):
        later, current, gradient = carry
        acceleration, residual_row = inputs
        drive = laplace(current) + place_sum(cells, residual_row, shape)
        earlier = (2.0 * current - (1.0 - damping) * later + courant * drive) / (1.0 + damping)
        return ((current, earlier, gradient + earlier * acceleration), None)

    start_gradient = jnp.zeros(shape, jnp.float32)
    (last_later, last_current, gradient), unused = lax.scan(
        retreat, (adjoint_next, adjoint_now, start_gradient), (accels, misfit_rows), reverse=True
    )
    return (gradient, trace_residual)


def solution(mesh):
    placed = (
        P("gx", "gy", None),
        P(("groups", "gx"), "gy", None),
        P(("groups", "gx"), "gy", None),
        P(("groups", "gx"), "gy", None),
        P(("groups", "gx"), "gy", None),
        P("groups"),
        P(None, "groups"),
        P("groups", "gx", "gy", None, None),
        P("gx", "gy", None, None),
        P("gx", "gy", None),
    )
    return jax.shard_map(
        local,
        mesh=mesh,
        in_specs=placed,
        out_specs=(P(("groups", "gx"), "gy", None), P("groups", "gx", "gy", None, None)),
        check_vma=False,
    )
```

profile of v0, /device:TPU:0, one launch (start us, length us, event | category | flops | bytes accessed | tf_op | source)
XLA Modules:
  0.0 143.3 jit_solution(18097279965961521523)
XLA Ops:
  0.6 3.7 %shard_map.113 = (f32[392,128]{1,0:T(8,128)}, f32[392,128]{1,0:T(8,128)}, f32[392,128]{1,0:T(8,128)}, f32[392,128]{1,0:T(8,128)}, f32[304,128]{1,0:T(8,128)}, /*...) custom-call(s32[1]{0:T(128)} %bitcast.slab_ref, s32[4]{0:T(128)} %bitcast.22, f32[512,128]{1,0:T(8,128)} %bitcast.15, ...), custom_call_target="tpu_custom_call" | custom-call | flops 1000000 | bytes 1000000 | tf_op jit(solution)/shard_map/pallas_call | solution.py:84
  6.1 4.5 %collective-permute-start.1 = (f32[392,128]{1,0:T(8,128)}, f32[392,128]{1,0:T(8,128)S(1)}, u32[]{:S(2)}, u32[]{:S(2)}) collective-permute-start(f32[392,128]{1,0:T(8,128)} %get-tuple-element.57), channel_id=1, source_target_pairs={{0,1},{1,9},{2,15},{3,7},{4,0},{5,8},{6,14},{7,6},{8,5},{9,13},{10... | collective-permute-start | bytes 602120 | tf_op jit(solution)/shard_map/ppermute | solution.py:645
  10.7 3.2 %collective-permute-start.3 = (f32[392,128]{1,0:T(8,128)}, f32[392,128]{1,0:T(8,128)S(1)}, u32[]{:S(2)}, u32[]{:S(2)}) collective-permute-start(f32[392,128]{1,0:T(8,128)} %get-tuple-element.59), channel_id=1, source_target_pairs={{0,5},{1,13},{2,11},{3,3},{4,4},{5,12},{6,10},{7,2},{8,1},{9,9},{1... | collective-permute-start | bytes 602120 | tf_op jit(solution)/shard_map/ppermute | solution.py:645
  17.2 10.6 %collective-permute-done.2.refs_2_ = f32[392,128]{1,0:T(8,128)S(1)} collective-permute-done((f32[392,128]{1,0:T(8,128)}, f32[392,128]{1,0:T(8,128)S(1)}, u32[]{:S(2)}, u32[]{:S(2)}) %collective-permute-start.2) | collective-permute-done | bytes 200736 | tf_op jit(solution)/shard_map/ppermute | solution.py:645
  29.4 3.2 %collective-permute-start.7 = (f32[1280,128]{1,0:T(8,128)S(1)}, f32[1280,128]{1,0:T(8,128)S(1)}, u32[]{:S(2)}, u32[]{:S(2)}) collective-permute-start(f32[1280,128]{1,0:T(8,128)S(1)} %get-tuple-element.72), channel_id=1, source_target_pairs={{0,1},{1,0},{4,5},{5,4},{8,9},{9,8},{12,13},{13,12},{14,15},{15,14... | collective-permute-start | bytes 1966088 | tf_op jit(solution)/shard_map/ppermute | solution.py:616
  34.6 5.7 %shard_map.115 = (f32[2048,128]{1,0:T(8,128)S(1)}, f32[1280,128]{1,0:T(8,128)S(1)}, f32[1280,128]{1,0:T(8,128)S(1)}, f32[768,128]{1,0:T(8,128)S(1)}, f32[8,128]{1,0:T(8,128)}) custom-call(s32[33]{0:T(128)S(1)} %pad_add_fusion.1.ints, f32[1280,128]{1,0:T(8,128)S(1)} %get-tuple-element.70.state, f32[1280,128]{1,0:T(8,128)S(1)} %collective-permute-done.6.from_next, ...), custom_call_target="tpu_custom_call" | custom-call | flops 8000000 | bytes 8000000 | tf_op jit(solution)/shard_map/pallas_call | solution.py:84
  40.4 4.1 %collective-permute-done.5.refs_1_.refs_3_ = f32[304,128]{1,0:T(8,128)S(1)} collective-permute-done((f32[304,128]{1,0:T(8,128)}, f32[304,128]{1,0:T(8,128)S(1)}, u32[]{:S(2)}, u32[]{:S(2)}) %collective-permute-start.5) | collective-permute-done | bytes 155680 | tf_op jit(solution)/shard_map/ppermute | solution.py:664
  45.1 5.3 %collective-permute-start.11 = (f32[768,128]{1,0:T(8,128)S(1)}, f32[768,128]{1,0:T(8,128)S(1)}, u32[]{:S(2)}, u32[]{:S(2)}) collective-permute-start(f32[768,128]{1,0:T(8,128)S(1)} %get-tuple-element.82), channel_id=1, source_target_pairs={{0,1},{1,0},{4,5},{5,4},{8,9},{9,8},{12,13},{13,12},{14,15},{15,14... | collective-permute-start | bytes 1179656 | tf_op jit(solution)/shard_map/ppermute | solution.py:616
  50.5 3.5 %collective-permute-start.9 = (f32[304,128]{1,0:T(8,128)S(1)}, f32[304,128]{1,0:T(8,128)S(1)}, u32[]{:S(2)}, u32[]{:S(2)}) collective-permute-start(f32[304,128]{1,0:T(8,128)S(1)} %copy-done.1), channel_id=1, source_target_pairs={{0,5},{1,13},{2,11},{3,3},{4,4},{5,12},{6,10},{7,2},{8,1},{9,9},{1... | collective-permute-start | bytes 466952 | tf_op jit(solution)/shard_map/ppermute | solution.py:664
  54.1 5.1 %shard_map.116 = (f32[2048,128]{1,0:T(8,128)S(1)}, f32[1280,128]{1,0:T(8,128)S(1)}, f32[768,128]{1,0:T(8,128)S(1)}, f32[8,128]{1,0:T(8,128)S(1)}) custom-call(s32[33]{0:T(128)S(1)} %pad_add_fusion.1.ints, f32[1280,128]{1,0:T(8,128)S(1)} %get-tuple-element.80.state, f32[768,128]{1,0:T(8,128)S(1)} %collective-permute-done.10.from_next, ...), custom_call_target="tpu_custom_call" | custom-call | flops 8000000 | bytes 8000000 | tf_op jit(solution)/shard_map/pallas_call | solution.py:84
  59.2 2.3 %collective-permute-done.9.refs_3_.refs_5_ = f32[304,128]{1,0:T(8,128)S(1)} collective-permute-done((f32[304,128]{1,0:T(8,128)S(1)}, f32[304,128]{1,0:T(8,128)S(1)}, u32[]{:S(2)}, u32[]{:S(2)}) %collective-permute-start.9) | collective-permute-done | bytes 155680 | tf_op jit(solution)/shard_map/ppermute | solution.py:664
  62.6 8.1 %collective-permute-start.13 = (f32[768,128]{1,0:T(8,128)S(1)}, f32[768,128]{1,0:T(8,128)S(1)}, u32[]{:S(2)}, u32[]{:S(2)}) collective-permute-start(f32[768,128]{1,0:T(8,128)S(1)} %get-tuple-element.88), channel_id=1, source_target_pairs={{0,1},{1,0},{4,5},{5,4},{8,9},{9,8},{12,13},{13,12},{14,15},{15,14... | collective-permute-start | bytes 1179656 | tf_op jit(solution)/shard_map/ppermute | solution.py:616
  74.2 3.6 %collective-permute-start.15 = (f32[896,128]{1,0:T(8,128)S(1)}, f32[896,128]{1,0:T(8,128)S(1)}, u32[]{:S(2)}, u32[]{:S(2)}) collective-permute-start(f32[896,128]{1,0:T(8,128)S(1)} %get-tuple-element.93), channel_id=1, source_target_pairs={{0,1},{1,0},{4,5},{5,4},{8,9},{9,8},{12,13},{13,12},{14,15},{15,14... | collective-permute-start | bytes 1376264 | tf_op jit(solution)/shard_map/ppermute | solution.py:616
  78.5 5.1 %shard_map.120.history = f32[2048,128]{1,0:T(8,128)S(1)} custom-call(s32[33]{0:T(128)S(1)} %pad_add_fusion.1.ints, f32[1280,128]{1,0:T(8,128)S(1)} %get-tuple-element.94.state, f32[768,128]{1,0:T(8,128)S(1)} %collective-permute-done.12.from_next, f32[768,128]{1,0:T(8,128)S(1)} %collective-permute-done.13.from_twin, ...), custom_call_target="tpu_custom_call" | custom-call | flops 8000000 | bytes 8000000 | tf_op jit(solution)/shard_map/pallas_call | solution.py:84
  86.4 4.3 %collective-permute-start.17 = (f32[56,512]{1,0:T(8,128)S(1)}, f32[56,512]{1,0:T(8,128)S(1)}, u32[]{:S(2)}, u32[]{:S(2)}) collective-permute-start(f32[56,512]{1,0:T(8,128)S(1)} %shard_map.121.misfit), channel_id=1, source_target_pairs={{0,1},{1,0},{4,5},{5,4},{8,9},{9,8},{12,13},{13,12},{14,15},{15,14... | collective-permute-start | bytes 344072 | tf_op jit(solution)/shard_map/ppermute | solution.py:616
  94.6 5.0 %shard_map.124 = (f32[2048,128]{1,0:T(8,128)S(1)}, f32[1280,128]{1,0:T(8,128)S(1)}, f32[768,128]{1,0:T(8,128)S(1)}) custom-call(s32[2]{0:T(128)S(1)} %pad_add_fusion.where_ref, f32[1280,128]{1,0:T(8,128)S(1)} %get-tuple-element.85.state, f32[896,128]{1,0:T(8,128)S(1)} %collective-permute-done.14.from_next, f32[896,128]{1,0:T(8,128)S(1)} %collective-permute-done.15.from_twin, ...), custom_call_target="tpu_custom_call" | custom-call | flops 8000000 | bytes 8000000 | tf_op jit(solution)/shard_map/pallas_call | solution.py:84
  100.3 3.4 %collective-permute-start.19 = (f32[768,128]{1,0:T(8,128)S(1)}, f32[768,128]{1,0:T(8,128)S(1)}, u32[]{:S(2)}, u32[]{:S(2)}) collective-permute-start(f32[768,128]{1,0:T(8,128)S(1)} %get-tuple-element.97), channel_id=1, source_target_pairs={{0,1},{1,0},{4,5},{5,4},{8,9},{9,8},{12,13},{13,12},{14,15},{15,14... | collective-permute-start | bytes 1179656 | tf_op jit(solution)/shard_map/ppermute | solution.py:616
  107.6 5.0 %shard_map.127 = (f32[2048,128]{1,0:T(8,128)S(1)}, f32[1280,128]{1,0:T(8,128)S(1)}, f32[768,128]{1,0:T(8,128)S(1)}) custom-call(s32[2]{0:T(128)S(1)} %pad_add_fusion.where_ref, f32[1280,128]{1,0:T(8,128)S(1)} %get-tuple-element.96.state, f32[768,128]{1,0:T(8,128)S(1)} %collective-permute-done.18.from_next, f32[768,128]{1,0:T(8,128)S(1)} %collective-permute-done.19.from_twin, ...), custom_call_target="tpu_custom_call" | custom-call | flops 8000000 | bytes 8000000 | tf_op jit(solution)/shard_map/pallas_call | solution.py:84
  113.5 4.5 %collective-permute-start.21 = (f32[768,128]{1,0:T(8,128)S(1)}, f32[768,128]{1,0:T(8,128)S(1)}, u32[]{:S(2)}, u32[]{:S(2)}) collective-permute-start(f32[768,128]{1,0:T(8,128)S(1)} %get-tuple-element.99), channel_id=1, source_target_pairs={{0,1},{1,0},{4,5},{5,4},{8,9},{9,8},{12,13},{13,12},{14,15},{15,14... | collective-permute-start | bytes 1179656 | tf_op jit(solution)/shard_map/ppermute | solution.py:616
  122.5 5.0 %shard_map.130.adjoint = f32[2048,128]{1,0:T(8,128)S(1)} custom-call(s32[2]{0:T(128)S(1)} %pad_add_fusion.where_ref, f32[1280,128]{1,0:T(8,128)S(1)} %get-tuple-element.98.state, f32[768,128]{1,0:T(8,128)S(1)} %collective-permute-done.20.from_next, f32[768,128]{1,0:T(8,128)S(1)} %collective-permute-done.21.from_twin, ...), custom_call_target="tpu_custom_call" | custom-call | flops 8000000 | bytes 8000000 | tf_op jit(solution)/shard_map/pallas_call | solution.py:84
  129.0 4.1 %collective-permute-start.23 = (f32[176,128]{1,0:T(8,128)S(1)}, f32[176,128]{1,0:T(8,128)S(1)}, u32[]{:S(2)}, u32[]{:S(2)}) collective-permute-start(f32[176,128]{1,0:T(8,128)S(1)} %get-tuple-element.103), channel_id=1, source_target_pairs={{1,0},{9,1},{15,2},{7,3},{0,4},{8,5},{14,6},{6,7},{5,8},{13,9},{11... | collective-permute-start | bytes 270344 | tf_op jit(solution)/shard_map/ppermute | solution.py:774
  133.1 2.7 %collective-permute-start.24 = (f32[176,128]{1,0:T(8,128)S(1)}, f32[176,128]{1,0:T(8,128)S(1)}, u32[]{:S(2)}, u32[]{:S(2)}) collective-permute-start(f32[176,128]{1,0:T(8,128)S(1)} %get-tuple-element.104), channel_id=1, source_target_pairs={{4,0},{12,1},{10,2},{2,3},{5,4},{13,5},{11,6},{3,7},{0,8},{8,9},{1... | collective-permute-start | bytes 270344 | tf_op jit(solution)/shard_map/ppermute | solution.py:774
  135.8 2.4 %collective-permute-start.25 = (f32[176,128]{1,0:T(8,128)S(1)}, f32[176,128]{1,0:T(8,128)S(1)}, u32[]{:S(2)}, u32[]{:S(2)}) collective-permute-start(f32[176,128]{1,0:T(8,128)S(1)} %get-tuple-element.105), channel_id=1, source_target_pairs={{5,0},{13,1},{11,2},{3,3},{4,4},{12,5},{10,6},{2,7},{1,8},{9,9},{1... | collective-permute-start | bytes 270344 | tf_op jit(solution)/shard_map/ppermute | solution.py:774
  139.4 3.1 %collective-permute-done.25.refs_3_ = f32[176,128]{1,0:T(8,128)S(1)} collective-permute-done((f32[176,128]{1,0:T(8,128)S(1)}, f32[176,128]{1,0:T(8,128)S(1)}, u32[]{:S(2)}, u32[]{:S(2)}) %collective-permute-start.25) | collective-permute-done | bytes 90144 | tf_op jit(solution)/shard_map/ppermute | solution.py:774
  (70 shorter events, 34.4 us)
Async XLA Ops:
  4.4 12.7 %collective-permute-start = (f32[392,128]{1,0:T(8,128)}, f32[392,128]{1,0:T(8,128)S(1)}, u32[]{:S(2)}, u32[]{:S(2)}) collective-permute-start(f32[392,128]{1,0:T(8,128)} %get-tuple-element.56), channel_id=1, source_target_pairs={{0,0},{1,8},{2,14},{3,6},{4,1},{5,9},{6,15},{7,7},{8,4},{9,12},{10... | collective-permute-start | bytes 602120 | tf_op jit(solution)/shard_map/ppermute | solution.py:645
  6.1 11.0 %collective-permute-start.1 = (f32[392,128]{1,0:T(8,128)}, f32[392,128]{1,0:T(8,128)S(1)}, u32[]{:S(2)}, u32[]{:S(2)}) collective-permute-start(f32[392,128]{1,0:T(8,128)} %get-tuple-element.57), channel_id=1, source_target_pairs={{0,1},{1,9},{2,15},{3,7},{4,0},{5,8},{6,14},{7,6},{8,5},{9,13},{10... | collective-permute-start | bytes 602120 | tf_op jit(solution)/shard_map/ppermute | solution.py:645
  10.6 17.1 %collective-permute-start.2 = (f32[392,128]{1,0:T(8,128)}, f32[392,128]{1,0:T(8,128)S(1)}, u32[]{:S(2)}, u32[]{:S(2)}) collective-permute-start(f32[392,128]{1,0:T(8,128)} %get-tuple-element.58), channel_id=1, source_target_pairs={{0,4},{1,12},{2,10},{3,2},{4,5},{5,13},{6,11},{7,3},{8,0},{9,8},{1... | collective-permute-start | bytes 602120 | tf_op jit(solution)/shard_map/ppermute | solution.py:645
  10.7 17.1 %collective-permute-start.3 = (f32[392,128]{1,0:T(8,128)}, f32[392,128]{1,0:T(8,128)S(1)}, u32[]{:S(2)}, u32[]{:S(2)}) collective-permute-start(f32[392,128]{1,0:T(8,128)} %get-tuple-element.59), channel_id=1, source_target_pairs={{0,5},{1,13},{2,11},{3,3},{4,4},{5,12},{6,10},{7,2},{8,1},{9,9},{1... | collective-permute-start | bytes 602120 | tf_op jit(solution)/shard_map/ppermute | solution.py:645
  32.7 11.8 %collective-permute-start.5 = (f32[304,128]{1,0:T(8,128)}, f32[304,128]{1,0:T(8,128)S(1)}, u32[]{:S(2)}, u32[]{:S(2)}) collective-permute-start(f32[304,128]{1,0:T(8,128)} %get-tuple-element.67), channel_id=1, source_target_pairs={{0,1},{1,9},{2,15},{3,7},{4,0},{5,8},{6,14},{7,6},{8,5},{9,13},{10... | collective-permute-start | bytes 466952 | tf_op jit(solution)/shard_map/ppermute | solution.py:664
  32.8 11.7 %collective-permute-start.4 = (f32[304,128]{1,0:T(8,128)}, f32[304,128]{1,0:T(8,128)S(1)}, u32[]{:S(2)}, u32[]{:S(2)}) collective-permute-start(f32[304,128]{1,0:T(8,128)} %get-tuple-element.65), channel_id=1, source_target_pairs={{0,0},{1,8},{2,14},{3,6},{4,1},{5,9},{6,15},{7,7},{8,4},{9,12},{10... | collective-permute-start | bytes 466952 | tf_op jit(solution)/shard_map/ppermute | solution.py:664
  44.5 9.6 %collective-permute-start.10 = (f32[768,128]{1,0:T(8,128)S(1)}, f32[768,128]{1,0:T(8,128)S(1)}, u32[]{:S(2)}, u32[]{:S(2)}) collective-permute-start(f32[768,128]{1,0:T(8,128)S(1)} %get-tuple-element.82), channel_id=1, source_target_pairs={{1,4},{4,1},{5,8},{8,5},{9,12},{12,9},{13,14},{14,13},{15,10},{10,... | collective-permute-start | bytes 1179656 | tf_op jit(solution)/shard_map/ppermute | solution.py:615
  45.1 8.9 %collective-permute-start.11 = (f32[768,128]{1,0:T(8,128)S(1)}, f32[768,128]{1,0:T(8,128)S(1)}, u32[]{:S(2)}, u32[]{:S(2)}) collective-permute-start(f32[768,128]{1,0:T(8,128)S(1)} %get-tuple-element.82), channel_id=1, source_target_pairs={{0,1},{1,0},{4,5},{5,4},{8,9},{9,8},{12,13},{13,12},{14,15},{15,14... | collective-permute-start | bytes 1179656 | tf_op jit(solution)/shard_map/ppermute | solution.py:616
  50.5 11.1 %collective-permute-start.9 = (f32[304,128]{1,0:T(8,128)S(1)}, f32[304,128]{1,0:T(8,128)S(1)}, u32[]{:S(2)}, u32[]{:S(2)}) collective-permute-start(f32[304,128]{1,0:T(8,128)S(1)} %copy-done.1), channel_id=1, source_target_pairs={{0,5},{1,13},{2,11},{3,3},{4,4},{5,12},{6,10},{7,2},{8,1},{9,9},{1... | collective-permute-start | bytes 466952 | tf_op jit(solution)/shard_map/ppermute | solution.py:664
  54.0 7.9 %collective-permute-start.8 = (f32[304,128]{1,0:T(8,128)S(1)}, f32[304,128]{1,0:T(8,128)S(1)}, u32[]{:S(2)}, u32[]{:S(2)}) collective-permute-start(f32[304,128]{1,0:T(8,128)S(1)} %copy-done), channel_id=1, source_target_pairs={{0,4},{1,12},{2,10},{3,2},{4,5},{5,13},{6,11},{7,3},{8,0},{9,8},{1... | collective-permute-start | bytes 466952 | tf_op jit(solution)/shard_map/ppermute | solution.py:664
  61.9 12.3 %collective-permute-start.12 = (f32[768,128]{1,0:T(8,128)S(1)}, f32[768,128]{1,0:T(8,128)S(1)}, u32[]{:S(2)}, u32[]{:S(2)}) collective-permute-start(f32[768,128]{1,0:T(8,128)S(1)} %get-tuple-element.88), channel_id=1, source_target_pairs={{1,4},{4,1},{5,8},{8,5},{9,12},{12,9},{13,14},{14,13},{15,10},{10,... | collective-permute-start | bytes 1179656 | tf_op jit(solution)/shard_map/ppermute | solution.py:615
  62.6 11.6 %collective-permute-start.13 = (f32[768,128]{1,0:T(8,128)S(1)}, f32[768,128]{1,0:T(8,128)S(1)}, u32[]{:S(2)}, u32[]{:S(2)}) collective-permute-start(f32[768,128]{1,0:T(8,128)S(1)} %get-tuple-element.88), channel_id=1, source_target_pairs={{0,1},{1,0},{4,5},{5,4},{8,9},{9,8},{12,13},{13,12},{14,15},{15,14... | collective-permute-start | bytes 1179656 | tf_op jit(solution)/shard_map/ppermute | solution.py:616
  74.2 11.3 %collective-permute-start.15 = (f32[896,128]{1,0:T(8,128)S(1)}, f32[896,128]{1,0:T(8,128)S(1)}, u32[]{:S(2)}, u32[]{:S(2)}) collective-permute-start(f32[896,128]{1,0:T(8,128)S(1)} %get-tuple-element.93), channel_id=1, source_target_pairs={{0,1},{1,0},{4,5},{5,4},{8,9},{9,8},{12,13},{13,12},{14,15},{15,14... | collective-permute-start | bytes 1376264 | tf_op jit(solution)/shard_map/ppermute | solution.py:616
  77.8 7.8 %collective-permute-start.14 = (f32[896,128]{1,0:T(8,128)S(1)}, f32[896,128]{1,0:T(8,128)S(1)}, u32[]{:S(2)}, u32[]{:S(2)}) collective-permute-start(f32[896,128]{1,0:T(8,128)S(1)} %get-tuple-element.91), channel_id=1, source_target_pairs={{1,4},{4,1},{5,8},{8,5},{9,12},{12,9},{13,14},{14,13},{15,10},{10,... | collective-permute-start | bytes 1376264 | tf_op jit(solution)/shard_map/ppermute | solution.py:615
  85.6 6.9 %collective-permute-start.16 = (f32[56,512]{1,0:T(8,128)S(1)}, f32[56,512]{1,0:T(8,128)S(1)}, u32[]{:S(2)}, u32[]{:S(2)}) collective-permute-start(f32[56,512]{1,0:T(8,128)S(1)} %shard_map.121.misfit), channel_id=1, source_target_pairs={{1,4},{4,1},{5,8},{8,5},{9,12},{12,9},{13,14},{14,13},{15,10},{10,... | collective-permute-start | bytes 344072 | tf_op jit(solution)/shard_map/ppermute | solution.py:615
  86.4 6.1 %collective-permute-start.17 = (f32[56,512]{1,0:T(8,128)S(1)}, f32[56,512]{1,0:T(8,128)S(1)}, u32[]{:S(2)}, u32[]{:S(2)}) collective-permute-start(f32[56,512]{1,0:T(8,128)S(1)} %shard_map.121.misfit), channel_id=1, source_target_pairs={{0,1},{1,0},{4,5},{5,4},{8,9},{9,8},{12,13},{13,12},{14,15},{15,14... | collective-permute-start | bytes 344072 | tf_op jit(solution)/shard_map/ppermute | solution.py:616
  99.6 7.9 %collective-permute-start.18 = (f32[768,128]{1,0:T(8,128)S(1)}, f32[768,128]{1,0:T(8,128)S(1)}, u32[]{:S(2)}, u32[]{:S(2)}) collective-permute-start(f32[768,128]{1,0:T(8,128)S(1)} %get-tuple-element.97), channel_id=1, source_target_pairs={{1,4},{4,1},{5,8},{8,5},{9,12},{12,9},{13,14},{14,13},{15,10},{10,... | collective-permute-start | bytes 1179656 | tf_op jit(solution)/shard_map/ppermute | solution.py:615
  100.3 7.3 %collective-permute-start.19 = (f32[768,128]{1,0:T(8,128)S(1)}, f32[768,128]{1,0:T(8,128)S(1)}, u32[]{:S(2)}, u32[]{:S(2)}) collective-permute-start(f32[768,128]{1,0:T(8,128)S(1)} %get-tuple-element.97), channel_id=1, source_target_pairs={{0,1},{1,0},{4,5},{5,4},{8,9},{9,8},{12,13},{13,12},{14,15},{15,14... | collective-permute-start | bytes 1179656 | tf_op jit(solution)/shard_map/ppermute | solution.py:616
  112.6 9.8 %collective-permute-start.20 = (f32[768,128]{1,0:T(8,128)S(1)}, f32[768,128]{1,0:T(8,128)S(1)}, u32[]{:S(2)}, u32[]{:S(2)}) collective-permute-start(f32[768,128]{1,0:T(8,128)S(1)} %get-tuple-element.99), channel_id=1, source_target_pairs={{1,4},{4,1},{5,8},{8,5},{9,12},{12,9},{13,14},{14,13},{15,10},{10,... | collective-permute-start | bytes 1179656 | tf_op jit(solution)/shard_map/ppermute | solution.py:615
  113.5 8.9 %collective-permute-start.21 = (f32[768,128]{1,0:T(8,128)S(1)}, f32[768,128]{1,0:T(8,128)S(1)}, u32[]{:S(2)}, u32[]{:S(2)}) collective-permute-start(f32[768,128]{1,0:T(8,128)S(1)} %get-tuple-element.99), channel_id=1, source_target_pairs={{0,1},{1,0},{4,5},{5,4},{8,9},{9,8},{12,13},{13,12},{14,15},{15,14... | collective-permute-start | bytes 1179656 | tf_op jit(solution)/shard_map/ppermute | solution.py:616
  128.3 9.9 %collective-permute-start.22 = (f32[176,128]{1,0:T(8,128)S(1)}, f32[176,128]{1,0:T(8,128)S(1)}, u32[]{:S(2)}, u32[]{:S(2)}) collective-permute-start(f32[176,128]{1,0:T(8,128)S(1)} %get-tuple-element.102), channel_id=1, source_target_pairs={{0,0},{8,1},{14,2},{6,3},{1,4},{9,5},{15,6},{7,7},{4,8},{12,9},{10... | collective-permute-start | bytes 270344 | tf_op jit(solution)/shard_map/ppermute | solution.py:774
  129.0 9.2 %collective-permute-start.23 = (f32[176,128]{1,0:T(8,128)S(1)}, f32[176,128]{1,0:T(8,128)S(1)}, u32[]{:S(2)}, u32[]{:S(2)}) collective-permute-start(f32[176,128]{1,0:T(8,128)S(1)} %get-tuple-element.103), channel_id=1, source_target_pairs={{1,0},{9,1},{15,2},{7,3},{0,4},{8,5},{14,6},{6,7},{5,8},{13,9},{11... | collective-permute-start | bytes 270344 | tf_op jit(solution)/shard_map/ppermute | solution.py:774
  133.1 6.4 %collective-permute-start.24 = (f32[176,128]{1,0:T(8,128)S(1)}, f32[176,128]{1,0:T(8,128)S(1)}, u32[]{:S(2)}, u32[]{:S(2)}) collective-permute-start(f32[176,128]{1,0:T(8,128)S(1)} %get-tuple-element.104), channel_id=1, source_target_pairs={{4,0},{12,1},{10,2},{2,3},{5,4},{13,5},{11,6},{3,7},{0,8},{8,9},{1... | collective-permute-start | bytes 270344 | tf_op jit(solution)/shard_map/ppermute | solution.py:774
  135.8 6.8 %collective-permute-start.25 = (f32[176,128]{1,0:T(8,128)S(1)}, f32[176,128]{1,0:T(8,128)S(1)}, u32[]{:S(2)}, u32[]{:S(2)}) collective-permute-start(f32[176,128]{1,0:T(8,128)S(1)} %get-tuple-element.105), channel_id=1, source_target_pairs={{5,0},{13,1},{11,2},{3,3},{4,4},{12,5},{10,6},{2,7},{1,8},{9,9},{1... | collective-permute-start | bytes 270344 | tf_op jit(solution)/shard_map/ppermute | solution.py:774
  (4 other events, 106.5 us)
where the time goes:
time: 144 us; the launch traced here: 143 us
  starting transfers between devices  62.2 us (43%)
  Pallas kernels  54.6 us (38%)
  waiting for transfers between devices  21.9 us (15%)
  other arithmetic  2.92 us (2%)
    pallas_call x22, Pallas kernels, call(): pl.pallas_call(kernel, out_shape=tuple(outs), in_specs=[pl.BlockSpec(memo...  54.6 us
    ppermute x7, starting transfers between devices, swap(): lax.ppermute(to_twin, axes, lay.swaps(0))  32.5 us
    ppermute x4, waiting for transfers between devices, local_tiles(): lax.ppermute(cut, axes, lay.to_chunks(turn))  10.6 us
    ppermute x4, starting transfers between devices, local_tiles(): lax.ppermute(send, axes, lay.to_slabs(turn))  9.87 us
    ppermute x4, starting transfers between devices, local_tiles(): lax.ppermute(cut, axes, lay.to_chunks(turn))  9.46 us
    ppermute x4, waiting for transfers between devices, move_adjoint(): lax.ppermute(after(back_cuts[turn], tie), axes, lay.to_chunks(turn))  6.74 us
    ppermute x4, starting transfers between devices, move_adjoint(): lax.ppermute(after(back_cuts[turn], tie), axes, lay.to_chunks(turn))  5.2 us
    ppermute x7, starting transfers between devices, swap(): lax.ppermute(to_next, axes, lay.swaps(1))  5.17 us
  transfers between devices with their start and end apart: 26, of which 7 were waited for; matrix products, arithmetic and copies ran while one was open for 2% of the time, Pallas kernels for 22%

commit v1 on v0

--- a/solution.py
+++ b/solution.py
@@ -17,6 +17,8 @@
 
 stencil = (-205.0 / 72.0, 8.0 / 5.0, -1.0 / 5.0, 8.0 / 315.0, -1.0 / 560.0)
 damping_peak = 0.3
+scale = 5040.0
+weights = (3.0 * -14350.0, 8064.0, -1008.0, 128.0, -9.0)
 
 
 class Layout:
@@ -98,37 +100,42 @@
     return pl.multiple_of(value, to)
 
 
-def cut_blocks(lay, slab_ref, count_ref, *refs):
-    inputs, refs = refs[:7], refs[7:]
-    sends, back_sends = refs[: lay.count_x], refs[lay.count_x : 2 * lay.count_x]
-    held, held_cell, held_traces, done = refs[2 * lay.count_x :]
-    targets = [held.at[index] for index in range(5)] + [held_cell, held_traces]
+def cut_chunk(lay, slab, turn, fields, target):
+    start = (slab ^ turn) * lay.chunk
+    for index, field in enumerate(fields):
+        for y in range(lay.chunk):
+            row = (index * lay.chunk + y) * ROWS
+            target[row : row + ROWS, :] = field[pl.ds(start + y, ROWS, stride=lay.width_y), :]
+
+
+def cut_forward(lay, slab_ref, count_ref, *refs):
+    inputs, sends, (held, held_cell, done) = refs[:4], refs[4 : 4 + lay.count_x], refs[4 + lay.count_x :]
+    fields = [held.at[index] for index in range(3)]
     copies = [
         pltpu.make_async_copy(source, target, done.at[index])
-        for index, (source, target) in enumerate(zip(inputs, targets))
+        for index, (source, target) in enumerate(zip(inputs, fields + [held_cell]))
     ]
     for copy in copies:
         copy.start()
     for copy in copies:
         copy.wait()
-    slab = slab_ref[0]
     slots = lax.broadcasted_iota(jnp.int32, (1, LANES), 1)
     used = []
     for tile in range(lay.count_x):
         cell = jnp.where(slots < count_ref[tile], held_cell[tile : tile + 1, :], -1)
         used.append(cell.astype(jnp.float32))
-    for turn in range(lay.count_x):
-        start = (slab ^ turn) * lay.chunk
-        for index in range(5):
-            target, first = (sends[turn], index) if index < 3 else (back_sends[turn], index - 3)
-            for y in range(lay.chunk):
-                row = (first * lay.chunk + y) * ROWS
-                target[row : row + ROWS, :] = held[index, pl.ds(start + y, ROWS, stride=lay.width_y), :]
+    for turn, send in enumerate(sends):
+        cut_chunk(lay, slab_ref[0], turn, fields, send)
         for tile in range(lay.count_x):
             row = 3 * lay.cells + tile
-            sends[turn][row : row + 1, :] = used[tile]
+            send[row : row + 1, :] = used[tile]
+
+
+def cut_adjoint(lay, slab_ref, now, prev, observed, *sends):
+    for turn, send in enumerate(sends):
+        cut_chunk(lay, slab_ref[0], turn, (now, prev), send)
         row = 2 * lay.cells
-        back_sends[turn][row : row + held_traces.shape[0], :] = held_traces[...]
+        send[row : row + observed.shape[0], :] = observed[...]
 
 
 def join_fields(lay, own_slot, odd, pieces, joined, state, courant, send_next, send_twin):
@@ -185,7 +192,7 @@
 
 
 def join_adjoint(lay, where_ref, *refs):
-    pieces, (tie, state, send_next, send_twin, joined) = refs[: lay.count_x], refs[lay.count_x :]
+    pieces, (state, send_next, send_twin, joined) = refs[: lay.count_x], refs[lay.count_x :]
     join_fields(lay, where_ref[0], where_ref[1], pieces, joined, state, None, send_next, send_twin)
 
 
@@ -241,21 +248,36 @@
 
 
 def fill_band(band):
-    apart = lax.broadcasted_iota(jnp.int32, (LANES, LANES), 0) - lax.broadcasted_iota(
-        jnp.int32, (LANES, LANES), 1
-    )
-    weights = jnp.where(apart == 0, 3.0 * stencil[0], 0.0).astype(jnp.float32)
+    row = lax.broadcasted_iota(jnp.int32, (2 * LANES, 2 * LANES), 0)
+    column = lax.broadcasted_iota(jnp.int32, (2 * LANES, 2 * LANES), 1)
+    apart = jnp.where((row < LANES) == (column < LANES), jnp.abs(row - column), 0)
+    values = jnp.zeros((2 * LANES, 2 * LANES), jnp.float32)
     for k in range(1, REACH + 1):
-        weights = jnp.where(jnp.abs(apart) == k, stencil[k], weights)
-    high, middle, low = split(weights)
-    for index, part in enumerate((high, high, high, middle, middle, low)):
-        band[index * LANES : (index + 1) * LANES, :] = part
-
-
-def sweep(lay, step, now, prev, following, half, gain, band, inject=None):
+        values = jnp.where(apart == k, weights[k], values)
+    values = values.astype(jnp.bfloat16)
+    for part in range(3):
+        band[part * 2 * LANES : (part + 1) * 2 * LANES, :] = values
+
+
+def multiply_z(lay, first_layer, count, now, band, along_z):
+    tiles = []
+    for y in range(count):
+        for tile in range(lay.tiles):
+            row = (first_layer + y) * lay.stride + (2 * tile + 1) * ROWS
+            tiles.append(now[row : row + ROWS, :])
+    half = len(tiles) // 2
+    parts = [split(jnp.concatenate(group, axis=0)) for group in (tiles[:half], tiles[half:])]
+    both = [side[part] for part in range(3) for side in parts]
+    found = jnp.dot(jnp.concatenate(both, axis=1), band[...], preferred_element_type=jnp.float32)
+    along_z[0 : half * ROWS, :] = found[:, :LANES]
+    along_z[half * ROWS : 2 * half * ROWS, :] = found[:, LANES:]
+
+
+def sweep(lay, step, now, prev, following, half, gain, band, along_z, inject=None):
     first_layer = REACH * (step + 1)
     group = 8
     reach_rows = REACH * lay.stride
+    multiply_z(lay, first_layer, lay.extent - 2 * first_layer, now, band, along_z)
 
     def layers(block, carry):
         start = first_layer + group * block
@@ -278,28 +300,23 @@
         def beside(y, tile, shift):
             return now[pl.ds(base + (place(y + REACH, tile) + shift), ROWS), :]
 
-        centers = [[at(y, tile) for tile in range(lay.tiles)] for y in range(group)]
-        high, middle, low = split(jnp.concatenate([tile for layer in centers for tile in layer], axis=0))
-        along_z = jnp.dot(
-            jnp.concatenate([high, middle, low, high, middle, high], axis=1),
-            band[...],
-            preferred_element_type=jnp.float32,
-        )
+        z_rows = along_z.at[pl.ds(aligned(block * group * lay.wide), group * lay.wide)]
         for y in range(group):
+            center = [at(y, tile) for tile in range(lay.tiles)]
             lower = [beside(y, tile, -1) for tile in range(lay.tiles)]
             upper = [beside(y, tile, 1) for tile in range(lay.tiles)]
-            line = lower + centers[y] + upper
+            line = lower + center + upper
             for tile in range(lay.tiles):
                 flat_at = (y * lay.tiles + tile) * ROWS
-                total = along_z[flat_at : flat_at + ROWS, :]
+                total = z_rows[flat_at : flat_at + ROWS, :] + weights[0] * center[tile]
                 for k in range(1, REACH + 1):
                     pair = line[lay.tiles + tile - k] + line[lay.tiles + tile + k]
-                    total = total + stencil[k] * (pair + (at(y - k, tile) + at(y + k, tile)))
+                    total = total + weights[k] * (pair + (at(y - k, tile) + at(y + k, tile)))
                 if added is not None:
                     total = total + added[pl.ds(y * lay.wide + tile, ROWS, stride=lay.tiles), :]
                 row = place(y, tile)
                 former = former_rows[row : row + ROWS, :]
-                change = (centers[y][tile] - former) + half_rows[flat_at : flat_at + ROWS, :] * total
+                change = (center[tile] - former) + half_rows[flat_at : flat_at + ROWS, :] * total
                 target[row : row + ROWS, :] = former + gain_rows[flat_at : flat_at + ROWS, :] * change
         return carry
 
@@ -335,7 +352,7 @@
     if not last:
         state_out, send, tie = [refs.pop(0) for _ in range(3)]
         tie[...] = jnp.zeros_like(tie)
-    now, prev, following, band, pulse = refs
+    now, prev, following, band, along_z, pulse = refs
     odd = ints[0]
 
     fill_band(band)
@@ -344,16 +361,16 @@
     if first:
         tail = (lay.chunk + lay.kept) * lay.wide
         part = lay.kept * lay.wide
-        half[part : part + lay.rows, :] = 0.5 * courant[...]
+        half[part : part + lay.rows, :] = (0.5 / scale) * courant[...]
         ahead = part + lay.rows
-        half[pl.ds(aligned(odd * ahead), part), :] = 0.5 * from_next[tail : tail + part, :]
-        half[pl.ds(aligned((1 - odd) * ahead), part), :] = 0.5 * from_twin[tail : tail + part, :]
+        half[pl.ds(aligned(odd * ahead), part), :] = (0.5 / scale) * from_next[tail : tail + part, :]
+        half[pl.ds(aligned((1 - odd) * ahead), part), :] = (0.5 / scale) * from_twin[tail : tail + part, :]
     for source in range(sources):
         flat = pl.ds(ints[1 + sources + source], 1)
-        pulse[source : source + 1, :] = half[flat, :] * gain[flat, :]
+        pulse[source : source + 1, :] = scale * (half[flat, :] * gain[flat, :])
 
     for step in range(DEPTH):
-        sweep(lay, step, now, prev, following, half, gain, band)
+        sweep(lay, step, now, prev, following, half, gain, band, along_z)
         added = pulse[...] * drive[phase * DEPTH + step]
         places = [pl.ds(ints[1 + source], 1) for source in range(sources)]
         lines = [following[place, :] for place in places]
@@ -441,22 +458,26 @@
             if low >= high:
                 continue
             row = (STEPS - 1 - phase * DEPTH - step) * lay.count_x + slab
-            parts = split(misfit[row : row + 1, :])
-            left.append(jnp.concatenate([hit[low * ROWS : high * ROWS, :] * part for part in parts], axis=1))
+            parts = split(scale * misfit[row : row + 1, :])
+            left += [hit[low * ROWS : high * ROWS, :] * part for part in parts]
             spans.append((step, low, high))
         placed = lax.dot_general(
             jnp.concatenate(left, axis=0),
-            jnp.concatenate([pick] * 3, axis=1),
+            pick,
             (((1,), (1,)), ((), ())),
             preferred_element_type=jnp.float32,
         )
         at = 0
         for step, low, high in spans:
+            rows = (high - low) * ROWS
+            total = placed[at : at + rows, :]
+            for part in (1, 2):
+                total = total + placed[at + part * rows : at + (part + 1) * rows, :]
             for y in range(low, high):
                 layer = lay.margin + side * lay.chunk + y - REACH
                 target = layer * lay.wide + slab * ROWS
-                inject[step, target : target + ROWS, :] = placed[at : at + ROWS, :]
-                at += ROWS
+                inject[step, target : target + ROWS, :] = total[(y - low) * ROWS : (y - low + 1) * ROWS, :]
+            at += 3 * rows
 
 
 def spread_own(lay, phase, misfit, inject):
@@ -483,13 +504,13 @@
     history = refs.pop(0)
     if not last:
         state_out, send = refs.pop(0), refs.pop(0)
-    now, prev, following, band = refs
+    now, prev, following, band, along_z = refs
 
     fill_band(band)
     load_state(lay, where_ref[1], first, now, prev, state, from_next, from_twin)
     zero_buffers(lay, now, prev, following)
     for step in range(DEPTH):
-        sweep(lay, step, now, prev, following, half, gain, band, inject)
+        sweep(lay, step, now, prev, following, half, gain, band, along_z, inject)
         keep_own(lay, step, following, history)
         now, prev, following = following, now, prev
     if not last:
@@ -627,23 +648,26 @@
     forward_rows = 3 * lay.cells + -(-count // ROWS) * ROWS
     back_rows = 2 * lay.cells + traces.shape[0]
     cuts = call(
-        part(cut_blocks, lay),
+        part(cut_forward, lay),
         (slab_int, receiver_count.reshape(-1)),
-        [flat(field) for field in (state_now, state_prev, courant, adjoint_now, adjoint_next)]
-        + [receiver_cell.reshape(count, LANES), traces],
-        [f32(forward_rows, LANES)] * count + [f32(back_rows, LANES)] * count,
+        [flat(field) for field in (state_now, state_prev, courant)] + [receiver_cell.reshape(count, LANES)],
+        [f32(forward_rows, LANES)] * count,
         [
-            pltpu.VMEM((5, lay.width_x * lay.width_y, LANES), jnp.float32),
+            pltpu.VMEM((3, lay.width_x * lay.width_y, LANES), jnp.float32),
             pltpu.VMEM((count, LANES), jnp.int32),
-            pltpu.VMEM(traces.shape, jnp.float32),
-            pltpu.SemaphoreType.DMA((7,)),
+            pltpu.SemaphoreType.DMA((4,)),
         ],
         space=pltpu.HBM,
         limit=60 * 1024 * 1024,
     )
-    cuts, back_cuts = cuts[:count], cuts[count:]
+    back_cuts = call(
+        part(cut_adjoint, lay),
+        (slab_int,),
+        [flat(adjoint_now), flat(adjoint_next), traces],
+        [f32(back_rows, LANES)] * count,
+    )
     pieces = [lax.ppermute(cut, axes, lay.to_chunks(turn)) for turn, cut in enumerate(cuts)]
-    pieces, ints, gain, drive = lax.optimization_barrier((pieces, ints, gain, drive))
+    pieces, ints, gain, drive, back_cuts = lax.optimization_barrier((pieces, ints, gain, drive, back_cuts))
     kept_rows = lay.kept * lay.wide
     tie_shape = f32(ROWS, LANES)
     state, own_courant, to_next, to_twin, codes = call(
@@ -663,7 +687,7 @@
         for turn in turns:
             back_pieces.append(lax.ppermute(after(back_cuts[turn], tie), axes, lay.to_chunks(turn)))
 
-    move_adjoint(range(count // 2), codes)
+    move_adjoint(range(count), codes)
 
     phases = STEPS // DEPTH
     step_cost = 8_000_000
@@ -671,7 +695,8 @@
     history_shape = f32(DEPTH * lay.rows, LANES)
     state_shapes = [f32(lay.state_rows, LANES), f32(lay.send_rows, LANES)]
     buffers = [pltpu.VMEM((lay.padded_rows, LANES), jnp.float32)] * 3
-    buffers += [pltpu.VMEM((6 * LANES, LANES), jnp.bfloat16)]
+    buffers += [pltpu.VMEM((6 * LANES, 2 * LANES), jnp.bfloat16)]
+    buffers += [pltpu.VMEM((lay.inner * lay.wide, LANES), jnp.float32)]
     record_scratch = [pltpu.VMEM((DEPTH * lay.rows, LANES), jnp.float32)]
     record_shape = (DEPTH * count, slots)
     histories, states, records = [], [], []
@@ -700,17 +725,9 @@
         if last:
             continue
         state, send, tie = results
-        send = after(send, back_pieces[-(count // 2) :])
+        if first:
+            send = after(send, back_pieces)
         from_next, from_twin = swap(send, send)
-        if first:
-            move_adjoint(range(count // 2, count), tie)
-    back_state, to_next, to_twin = call(
-        part(join_adjoint, lay),
-        (where,),
-        back_pieces + [tie],
-        [f32(lay.state_rows, LANES)] + [f32(lay.rows + kept_rows, LANES)] * 2,
-        [pltpu.VMEM((2, lay.rows, LANES), jnp.float32)],
-    )
     for history in histories[:-1]:
         records += call(
             part(record_phase, lay),
@@ -720,8 +737,14 @@
             record_scratch,
             cost=side_cost,
         )
-    arrived = (from_next, from_twin, records)
-    back_from_next, back_from_twin = swap(after(to_next, arrived), after(to_twin, arrived))
+    back_state, to_next, to_twin = call(
+        part(join_adjoint, lay),
+        (where,),
+        back_pieces,
+        [f32(lay.state_rows, LANES)] + [f32(lay.rows + kept_rows, LANES)] * 2,
+        [pltpu.VMEM((2, lay.rows, LANES), jnp.float32)],
+    )
+    back_from_next, back_from_twin = swap(to_next, to_twin)
     (misfit,) = call(
         part(record_last, lay, phases),
         (where,),

time: 144 us -> 140 us (0.972); the launches traced: 143 us -> 138 us
  waiting for transfers between devices: 21.9 us -> 16.9 us
  local copies, waits for them, and re-layouts: 0.44 us -> 3.07 us
  starting transfers between devices: 62.2 us -> 60.5 us
    ppermute x7, starting transfers between devices: 32.5 us -> 29.2 us  [swap(): lax.ppermute(to_twin, axes, lay.swaps(0))]
    ppermute x4, waiting for transfers between devices: 10.6 us -> 7.61 us  [local_tiles(): lax.ppermute(cut, axes, lay.to_chunks(turn))]
    unnamed x4 -> x6, local copies, waits for them, and re-layouts: 0.01 us -> 2.64 us
    ppermute x4, waiting for transfers between devices: 4.31 us -> 2.85 us  [local_tiles(): lax.ppermute(send, axes, lay.to_slabs(turn))]
    pallas_call x22 -> x23, Pallas kernels: 54.6 us -> 53.3 us  [call(): pl.pallas_call(kernel, out_shape=tuple(outs), in_specs=[pl.BlockSpec(memo...]
  transfers between devices with their start and end apart: 26 -> 26, of which waited for: 7 -> 5; matrix products, arithmetic and copies ran while one was open for 2% -> 2% of each run, Pallas kernels for 22% -> 23%
where the time goes in v1:
time: 140 us; the launch traced here: 138 us
  starting transfers between devices  60.5 us (43%)
  Pallas kernels  53.3 us (38%)
  waiting for transfers between devices  16.9 us (12%)
  local copies, waits for them, and re-layouts  3.07 us (2%)
  other arithmetic  2.92 us (2%)
    pallas_call x23, Pallas kernels, call(): pl.pallas_call(kernel, out_shape=tuple(outs), in_specs=[pl.BlockSpec(memo...  53.3 us
    ppermute x7, starting transfers between devices, swap(): lax.ppermute(to_twin, axes, lay.swaps(0))  29.2 us
    ppermute x4, starting transfers between devices, local_tiles(): lax.ppermute(send, axes, lay.to_slabs(turn))  10.2 us
    ppermute x4, starting transfers between devices, local_tiles(): lax.ppermute(cut, axes, lay.to_chunks(turn))  9.33 us
    ppermute x4, waiting for transfers between devices, local_tiles(): lax.ppermute(cut, axes, lay.to_chunks(turn))  7.61 us
    ppermute x4, starting transfers between devices, move_adjoint(): lax.ppermute(after(back_cuts[turn], tie), axes, lay.to_chunks(turn))  6.55 us
    ppermute x4, waiting for transfers between devices, move_adjoint(): lax.ppermute(after(back_cuts[turn], tie), axes, lay.to_chunks(turn))  6.4 us
    ppermute x7, starting transfers between devices, swap(): lax.ppermute(to_next, axes, lay.swaps(1))  5.18 us
  transfers between devices with their start and end apart: 26, of which 5 were waited for; matrix products, arithmetic and copies ran while one was open for 2% of the time, Pallas kernels for 23%

profile of v1, /device:TPU:0, one launch (start us, length us, event | category | flops | bytes accessed | tf_op | source)
XLA Modules:
  0.0 137.8 jit_solution(4975527958434655894)
XLA Ops:
  0.6 3.1 %shard_map.113 = (f32[392,128]{1,0:T(8,128)}, f32[392,128]{1,0:T(8,128)}, f32[392,128]{1,0:T(8,128)}, f32[392,128]{1,0:T(8,128)}) custom-call(s32[1]{0:T(128)} %bitcast.slab_ref, s32[4]{0:T(128)} %bitcast.22, f32[512,128]{1,0:T(8,128)} %bitcast.18, f32[512,128]{1,0:T(8,128)} %bitcast.19, f32[512,128]{1,0:T(8,128)} %bitcast.20, s32[4,128]{1,0:T(4,128)} %bitcast.21), custom_call_target="tpu_custom_call" | custom-call | flops 1000000 | bytes 1000000 | tf_op jit(solution)/shard_map/pallas_call | solution.py:86
  5.3 4.5 %collective-permute-start.1 = (f32[392,128]{1,0:T(8,128)}, f32[392,128]{1,0:T(8,128)S(1)}, u32[]{:S(2)}, u32[]{:S(2)}) collective-permute-start(f32[392,128]{1,0:T(8,128)} %get-tuple-element.55), channel_id=1, source_target_pairs={{0,1},{1,9},{2,15},{3,7},{4,0},{5,8},{6,14},{7,6},{8,5},{9,13},{10... | collective-permute-start | bytes 602120 | tf_op jit(solution)/shard_map/ppermute | solution.py:669
  9.9 3.2 %collective-permute-start.3 = (f32[392,128]{1,0:T(8,128)}, f32[392,128]{1,0:T(8,128)S(1)}, u32[]{:S(2)}, u32[]{:S(2)}) collective-permute-start(f32[392,128]{1,0:T(8,128)} %get-tuple-element.57), channel_id=1, source_target_pairs={{0,5},{1,13},{2,11},{3,3},{4,4},{5,12},{6,10},{7,2},{8,1},{9,9},{1... | collective-permute-start | bytes 602120 | tf_op jit(solution)/shard_map/ppermute | solution.py:669
  19.3 7.6 %collective-permute-done.2.refs_2_ = f32[392,128]{1,0:T(8,128)S(1)} collective-permute-done((f32[392,128]{1,0:T(8,128)}, f32[392,128]{1,0:T(8,128)S(1)}, u32[]{:S(2)}, u32[]{:S(2)}) %collective-permute-start.2) | collective-permute-done | bytes 200736 | tf_op jit(solution)/shard_map/ppermute | solution.py:669
  28.6 3.2 %collective-permute-start.11 = (f32[1280,128]{1,0:T(8,128)S(1)}, f32[1280,128]{1,0:T(8,128)S(1)}, u32[]{:S(2)}, u32[]{:S(2)}) collective-permute-start(f32[1280,128]{1,0:T(8,128)S(1)} %get-tuple-element.81), channel_id=1, source_target_pairs={{0,1},{1,0},{4,5},{5,4},{8,9},{9,8},{12,13},{13,12},{14,15},{15,14... | collective-permute-start | bytes 1966088 | tf_op jit(solution)/shard_map/ppermute | solution.py:637
  31.9 3.6 %collective-permute-start.7 = (f32[304,128]{1,0:T(8,128)S(1)}, f32[304,128]{1,0:T(8,128)S(1)}, u32[]{:S(2)}, u32[]{:S(2)}) collective-permute-start(f32[304,128]{1,0:T(8,128)S(1)} %get-tuple-element.74), channel_id=1, source_target_pairs={{0,5},{1,13},{2,11},{3,3},{4,4},{5,12},{6,10},{7,2},{8,1},{9,9},{1... | collective-permute-start | bytes 466952 | tf_op jit(solution)/shard_map/ppermute | solution.py:688
  35.6 2.2 %collective-permute-start.5 = (f32[304,128]{1,0:T(8,128)S(1)}, f32[304,128]{1,0:T(8,128)S(1)}, u32[]{:S(2)}, u32[]{:S(2)}) collective-permute-start(f32[304,128]{1,0:T(8,128)S(1)} %get-tuple-element.70), channel_id=1, source_target_pairs={{0,1},{1,9},{2,15},{3,7},{4,0},{5,8},{6,14},{7,6},{8,5},{9,13},{10... | collective-permute-start | bytes 466952 | tf_op jit(solution)/shard_map/ppermute | solution.py:688
  38.5 5.4 %shard_map.117 = (f32[2048,128]{1,0:T(8,128)S(1)}, f32[1280,128]{1,0:T(8,128)S(1)}, f32[1280,128]{1,0:T(8,128)S(1)}, f32[768,128]{1,0:T(8,128)S(1)}, f32[8,128]{1,0:T(8,128)}) custom-call(s32[33]{0:T(128)S(1)} %pad_add_fusion.1.ints, f32[1280,128]{1,0:T(8,128)S(1)} %get-tuple-element.79.state, f32[1280,128]{1,0:T(8,128)S(1)} %collective-permute-done.10.from_next, ...), custom_call_target="tpu_custom_call" | custom-call | flops 8000000 | bytes 8000000 | tf_op jit(solution)/shard_map/pallas_call | solution.py:86
  43.9 3.1 %collective-permute-done.7.refs_3_.refs_5_ = f32[304,128]{1,0:T(8,128)S(1)} collective-permute-done((f32[304,128]{1,0:T(8,128)S(1)}, f32[304,128]{1,0:T(8,128)S(1)}, u32[]{:S(2)}, u32[]{:S(2)}) %collective-permute-start.7) | collective-permute-done | bytes 155680 | tf_op jit(solution)/shard_map/ppermute | solution.py:688
  47.0 3.3 %collective-permute-done.5.refs_1_.refs_3_ = f32[304,128]{1,0:T(8,128)S(1)} collective-permute-done((f32[304,128]{1,0:T(8,128)S(1)}, f32[304,128]{1,0:T(8,128)S(1)}, u32[]{:S(2)}, u32[]{:S(2)}) %collective-permute-start.5) | collective-permute-done | bytes 155680 | tf_op jit(solution)/shard_map/ppermute | solution.py:688
  51.0 5.5 %collective-permute-start.13 = (f32[768,128]{1,0:T(8,128)S(1)}, f32[768,128]{1,0:T(8,128)S(1)}, u32[]{:S(2)}, u32[]{:S(2)}) collective-permute-start(f32[768,128]{1,0:T(8,128)S(1)} %get-tuple-element.88), channel_id=1, source_target_pairs={{0,1},{1,0},{4,5},{5,4},{8,9},{9,8},{12,13},{13,12},{14,15},{15,14... | collective-permute-start | bytes 1179656 | tf_op jit(solution)/shard_map/ppermute | solution.py:637
  59.3 5.4 %shard_map.118 = (f32[2048,128]{1,0:T(8,128)S(1)}, f32[1280,128]{1,0:T(8,128)S(1)}, f32[768,128]{1,0:T(8,128)S(1)}, f32[8,128]{1,0:T(8,128)}) custom-call(s32[33]{0:T(128)S(1)} %pad_add_fusion.1.ints, f32[1280,128]{1,0:T(8,128)S(1)} %get-tuple-element.86.state, f32[768,128]{1,0:T(8,128)S(1)} %collective-permute-done.12.from_next, ...), custom_call_target="tpu_custom_call" | custom-call | flops 8000000 | bytes 8000000 | tf_op jit(solution)/shard_map/pallas_call | solution.py:86
  65.5 5.7 %collective-permute-start.15 = (f32[768,128]{1,0:T(8,128)S(1)}, f32[768,128]{1,0:T(8,128)S(1)}, u32[]{:S(2)}, u32[]{:S(2)}) collective-permute-start(f32[768,128]{1,0:T(8,128)S(1)} %get-tuple-element.90), channel_id=1, source_target_pairs={{0,1},{1,0},{4,5},{5,4},{8,9},{9,8},{12,13},{13,12},{14,15},{15,14... | collective-permute-start | bytes 1179656 | tf_op jit(solution)/shard_map/ppermute | solution.py:637
  74.0 4.8 %shard_map.119.history = f32[2048,128]{1,0:T(8,128)S(1)} custom-call(s32[33]{0:T(128)S(1)} %pad_add_fusion.1.ints, f32[1280,128]{1,0:T(8,128)S(1)} %get-tuple-element.89.state, f32[768,128]{1,0:T(8,128)S(1)} %collective-permute-done.14.from_next, f32[768,128]{1,0:T(8,128)S(1)} %collective-permute-done.15.from_twin, ...), custom_call_target="tpu_custom_call" | custom-call | flops 8000000 | bytes 8000000 | tf_op jit(solution)/shard_map/pallas_call | solution.py:86
  81.4 5.4 %collective-permute-start.17 = (f32[56,512]{1,0:T(8,128)S(1)}, f32[56,512]{1,0:T(8,128)S(1)}, u32[]{:S(2)}, u32[]{:S(2)}) collective-permute-start(f32[56,512]{1,0:T(8,128)S(1)} %shard_map.122.misfit), channel_id=1, source_target_pairs={{0,1},{1,0},{4,5},{5,4},{8,9},{9,8},{12,13},{13,12},{14,15},{15,14... | collective-permute-start | bytes 344072 | tf_op jit(solution)/shard_map/ppermute | solution.py:637
  90.6 4.9 %shard_map.125 = (f32[2048,128]{1,0:T(8,128)S(1)}, f32[1280,128]{1,0:T(8,128)S(1)}, f32[768,128]{1,0:T(8,128)S(1)}) custom-call(s32[2]{0:T(128)S(1)} %pad_add_fusion.where_ref, f32[1280,128]{1,0:T(8,128)S(1)} %get-tuple-element.75.state, f32[896,128]{1,0:T(8,128)S(1)} %collective-permute-done.8.from_next, f32[896,128]{1,0:T(8,128)S(1)} %collective-permute-done.9.from_twin, ...), custom_call_target="tpu_custom_call" | custom-call | flops 8000000 | bytes 8000000 | tf_op jit(solution)/shard_map/pallas_call | solution.py:86
  96.5 3.6 %collective-permute-start.19 = (f32[768,128]{1,0:T(8,128)S(1)}, f32[768,128]{1,0:T(8,128)S(1)}, u32[]{:S(2)}, u32[]{:S(2)}) collective-permute-start(f32[768,128]{1,0:T(8,128)S(1)} %get-tuple-element.95), channel_id=1, source_target_pairs={{0,1},{1,0},{4,5},{5,4},{8,9},{9,8},{12,13},{13,12},{14,15},{15,14... | collective-permute-start | bytes 1179656 | tf_op jit(solution)/shard_map/ppermute | solution.py:637
  103.8 4.9 %shard_map.128 = (f32[2048,128]{1,0:T(8,128)S(1)}, f32[1280,128]{1,0:T(8,128)S(1)}, f32[768,128]{1,0:T(8,128)S(1)}) custom-call(s32[2]{0:T(128)S(1)} %pad_add_fusion.where_ref, f32[1280,128]{1,0:T(8,128)S(1)} %get-tuple-element.94.state, f32[768,128]{1,0:T(8,128)S(1)} %collective-permute-done.18.from_next, f32[768,128]{1,0:T(8,128)S(1)} %collective-permute-done.19.from_twin, ...), custom_call_target="tpu_custom_call" | custom-call | flops 8000000 | bytes 8000000 | tf_op jit(solution)/shard_map/pallas_call | solution.py:86
  109.5 4.4 %collective-permute-start.21 = (f32[768,128]{1,0:T(8,128)S(1)}, f32[768,128]{1,0:T(8,128)S(1)}, u32[]{:S(2)}, u32[]{:S(2)}) collective-permute-start(f32[768,128]{1,0:T(8,128)S(1)} %get-tuple-element.97), channel_id=1, source_target_pairs={{0,1},{1,0},{4,5},{5,4},{8,9},{9,8},{12,13},{13,12},{14,15},{15,14... | collective-permute-start | bytes 1179656 | tf_op jit(solution)/shard_map/ppermute | solution.py:637
  118.2 4.9 %shard_map.131.adjoint = f32[2048,128]{1,0:T(8,128)S(1)} custom-call(s32[2]{0:T(128)S(1)} %pad_add_fusion.where_ref, f32[1280,128]{1,0:T(8,128)S(1)} %get-tuple-element.96.state, f32[768,128]{1,0:T(8,128)S(1)} %collective-permute-done.20.from_next, f32[768,128]{1,0:T(8,128)S(1)} %collective-permute-done.21.from_twin, ...), custom_call_target="tpu_custom_call" | custom-call | flops 8000000 | bytes 8000000 | tf_op jit(solution)/shard_map/pallas_call | solution.py:86
  124.6 4.0 %collective-permute-start.23 = (f32[176,128]{1,0:T(8,128)S(1)}, f32[176,128]{1,0:T(8,128)S(1)}, u32[]{:S(2)}, u32[]{:S(2)}) collective-permute-start(f32[176,128]{1,0:T(8,128)S(1)} %get-tuple-element.101), channel_id=1, source_target_pairs={{1,0},{9,1},{15,2},{7,3},{0,4},{8,5},{14,6},{6,7},{5,8},{13,9},{11... | collective-permute-start | bytes 270344 | tf_op jit(solution)/shard_map/ppermute | solution.py:797
  128.6 2.2 %collective-permute-start.24 = (f32[176,128]{1,0:T(8,128)S(1)}, f32[176,128]{1,0:T(8,128)S(1)}, u32[]{:S(2)}, u32[]{:S(2)}) collective-permute-start(f32[176,128]{1,0:T(8,128)S(1)} %get-tuple-element.102), channel_id=1, source_target_pairs={{4,0},{12,1},{10,2},{2,3},{5,4},{13,5},{11,6},{3,7},{0,8},{8,9},{1... | collective-permute-start | bytes 270344 | tf_op jit(solution)/shard_map/ppermute | solution.py:797
  130.9 3.3 %collective-permute-start.25 = (f32[176,128]{1,0:T(8,128)S(1)}, f32[176,128]{1,0:T(8,128)S(1)}, u32[]{:S(2)}, u32[]{:S(2)}) collective-permute-start(f32[176,128]{1,0:T(8,128)S(1)} %get-tuple-element.103), channel_id=1, source_target_pairs={{5,0},{13,1},{11,2},{3,3},{4,4},{12,5},{10,6},{2,7},{1,8},{9,9},{1... | collective-permute-start | bytes 270344 | tf_op jit(solution)/shard_map/ppermute | solution.py:797
  134.5 2.5 %collective-permute-done.25.refs_3_ = f32[176,128]{1,0:T(8,128)S(1)} collective-permute-done((f32[176,128]{1,0:T(8,128)S(1)}, f32[176,128]{1,0:T(8,128)S(1)}, u32[]{:S(2)}, u32[]{:S(2)}) %collective-permute-start.25) | collective-permute-done | bytes 90144 | tf_op jit(solution)/shard_map/ppermute | solution.py:797
  (73 shorter events, 35.8 us)
Async XLA Ops:
  3.7 15.6 %collective-permute-start = (f32[392,128]{1,0:T(8,128)}, f32[392,128]{1,0:T(8,128)S(1)}, u32[]{:S(2)}, u32[]{:S(2)}) collective-permute-start(f32[392,128]{1,0:T(8,128)} %get-tuple-element.54), channel_id=1, source_target_pairs={{0,0},{1,8},{2,14},{3,6},{4,1},{5,9},{6,15},{7,7},{8,4},{9,12},{10... | collective-permute-start | bytes 602120 | tf_op jit(solution)/shard_map/ppermute | solution.py:669
  5.3 14.0 %collective-permute-start.1 = (f32[392,128]{1,0:T(8,128)}, f32[392,128]{1,0:T(8,128)S(1)}, u32[]{:S(2)}, u32[]{:S(2)}) collective-permute-start(f32[392,128]{1,0:T(8,128)} %get-tuple-element.55), channel_id=1, source_target_pairs={{0,1},{1,9},{2,15},{3,7},{4,0},{5,8},{6,14},{7,6},{8,5},{9,13},{10... | collective-permute-start | bytes 602120 | tf_op jit(solution)/shard_map/ppermute | solution.py:669
  9.9 17.1 %collective-permute-start.2 = (f32[392,128]{1,0:T(8,128)}, f32[392,128]{1,0:T(8,128)S(1)}, u32[]{:S(2)}, u32[]{:S(2)}) collective-permute-start(f32[392,128]{1,0:T(8,128)} %get-tuple-element.56), channel_id=1, source_target_pairs={{0,4},{1,12},{2,10},{3,2},{4,5},{5,13},{6,11},{7,3},{8,0},{9,8},{1... | collective-permute-start | bytes 602120 | tf_op jit(solution)/shard_map/ppermute | solution.py:669
  9.9 17.1 %collective-permute-start.3 = (f32[392,128]{1,0:T(8,128)}, f32[392,128]{1,0:T(8,128)S(1)}, u32[]{:S(2)}, u32[]{:S(2)}) collective-permute-start(f32[392,128]{1,0:T(8,128)} %get-tuple-element.57), channel_id=1, source_target_pairs={{0,5},{1,13},{2,11},{3,3},{4,4},{5,12},{6,10},{7,2},{8,1},{9,9},{1... | collective-permute-start | bytes 602120 | tf_op jit(solution)/shard_map/ppermute | solution.py:669
  27.9 9.9 %collective-permute-start.10 = (f32[1280,128]{1,0:T(8,128)S(1)}, f32[1280,128]{1,0:T(8,128)S(1)}, u32[]{:S(2)}, u32[]{:S(2)}) collective-permute-start(f32[1280,128]{1,0:T(8,128)S(1)} %get-tuple-element.80), channel_id=1, source_target_pairs={{1,4},{4,1},{5,8},{8,5},{9,12},{12,9},{13,14},{14,13},{15,10},{10,... | collective-permute-start | bytes 1966088 | tf_op jit(solution)/shard_map/ppermute | solution.py:636
  28.6 9.8 %collective-permute-start.11 = (f32[1280,128]{1,0:T(8,128)S(1)}, f32[1280,128]{1,0:T(8,128)S(1)}, u32[]{:S(2)}, u32[]{:S(2)}) collective-permute-start(f32[1280,128]{1,0:T(8,128)S(1)} %get-tuple-element.81), channel_id=1, source_target_pairs={{0,1},{1,0},{4,5},{5,4},{8,9},{9,8},{12,13},{13,12},{14,15},{15,14... | collective-permute-start | bytes 1966088 | tf_op jit(solution)/shard_map/ppermute | solution.py:637
  31.9 15.1 %collective-permute-start.7 = (f32[304,128]{1,0:T(8,128)S(1)}, f32[304,128]{1,0:T(8,128)S(1)}, u32[]{:S(2)}, u32[]{:S(2)}) collective-permute-start(f32[304,128]{1,0:T(8,128)S(1)} %get-tuple-element.74), channel_id=1, source_target_pairs={{0,5},{1,13},{2,11},{3,3},{4,4},{5,12},{6,10},{7,2},{8,1},{9,9},{1... | collective-permute-start | bytes 466952 | tf_op jit(solution)/shard_map/ppermute | solution.py:688
  35.5 11.5 %collective-permute-start.6 = (f32[304,128]{1,0:T(8,128)S(1)}, f32[304,128]{1,0:T(8,128)S(1)}, u32[]{:S(2)}, u32[]{:S(2)}) collective-permute-start(f32[304,128]{1,0:T(8,128)S(1)} %get-tuple-element.72), channel_id=1, source_target_pairs={{0,4},{1,12},{2,10},{3,2},{4,5},{5,13},{6,11},{7,3},{8,0},{9,8},{1... | collective-permute-start | bytes 466952 | tf_op jit(solution)/shard_map/ppermute | solution.py:688
  35.6 14.7 %collective-permute-start.5 = (f32[304,128]{1,0:T(8,128)S(1)}, f32[304,128]{1,0:T(8,128)S(1)}, u32[]{:S(2)}, u32[]{:S(2)}) collective-permute-start(f32[304,128]{1,0:T(8,128)S(1)} %get-tuple-element.70), channel_id=1, source_target_pairs={{0,1},{1,9},{2,15},{3,7},{4,0},{5,8},{6,14},{7,6},{8,5},{9,13},{10... | collective-permute-start | bytes 466952 | tf_op jit(solution)/shard_map/ppermute | solution.py:688
  37.8 12.5 %collective-permute-start.4 = (f32[304,128]{1,0:T(8,128)S(1)}, f32[304,128]{1,0:T(8,128)S(1)}, u32[]{:S(2)}, u32[]{:S(2)}) collective-permute-start(f32[304,128]{1,0:T(8,128)S(1)} %get-tuple-element.68), channel_id=1, source_target_pairs={{0,0},{1,8},{2,14},{3,6},{4,1},{5,9},{6,15},{7,7},{8,4},{9,12},{10... | collective-permute-start | bytes 466952 | tf_op jit(solution)/shard_map/ppermute | solution.py:688
  50.3 9.0 %collective-permute-start.12 = (f32[768,128]{1,0:T(8,128)S(1)}, f32[768,128]{1,0:T(8,128)S(1)}, u32[]{:S(2)}, u32[]{:S(2)}) collective-permute-start(f32[768,128]{1,0:T(8,128)S(1)} %get-tuple-element.88), channel_id=1, source_target_pairs={{1,4},{4,1},{5,8},{8,5},{9,12},{12,9},{13,14},{14,13},{15,10},{10,... | collective-permute-start | bytes 1179656 | tf_op jit(solution)/shard_map/ppermute | solution.py:636
  51.0 8.3 %collective-permute-start.13 = (f32[768,128]{1,0:T(8,128)S(1)}, f32[768,128]{1,0:T(8,128)S(1)}, u32[]{:S(2)}, u32[]{:S(2)}) collective-permute-start(f32[768,128]{1,0:T(8,128)S(1)} %get-tuple-element.88), channel_id=1, source_target_pairs={{0,1},{1,0},{4,5},{5,4},{8,9},{9,8},{12,13},{13,12},{14,15},{15,14... | collective-permute-start | bytes 1179656 | tf_op jit(solution)/shard_map/ppermute | solution.py:637
  57.3 23.5 %collective-permute-start.8 = (f32[896,128]{1,0:T(8,128)S(1)}, f32[896,128]{1,0:T(8,128)S(1)}, u32[]{:S(2)}, u32[]{:S(2)}) collective-permute-start(f32[896,128]{1,0:T(8,128)S(1)} %get-tuple-element.76), channel_id=1, source_target_pairs={{1,4},{4,1},{5,8},{8,5},{9,12},{12,9},{13,14},{14,13},{15,10},{10,... | collective-permute-start | bytes 1376264 | tf_op jit(solution)/shard_map/ppermute | solution.py:636
  58.0 22.8 %collective-permute-start.9 = (f32[896,128]{1,0:T(8,128)S(1)}, f32[896,128]{1,0:T(8,128)S(1)}, u32[]{:S(2)}, u32[]{:S(2)}) collective-permute-start(f32[896,128]{1,0:T(8,128)S(1)} %get-tuple-element.77), channel_id=1, source_target_pairs={{0,1},{1,0},{4,5},{5,4},{8,9},{9,8},{12,13},{13,12},{14,15},{15,14... | collective-permute-start | bytes 1376264 | tf_op jit(solution)/shard_map/ppermute | solution.py:637
  64.6 9.3 %collective-permute-start.14 = (f32[768,128]{1,0:T(8,128)S(1)}, f32[768,128]{1,0:T(8,128)S(1)}, u32[]{:S(2)}, u32[]{:S(2)}) collective-permute-start(f32[768,128]{1,0:T(8,128)S(1)} %get-tuple-element.90), channel_id=1, source_target_pairs={{1,4},{4,1},{5,8},{8,5},{9,12},{12,9},{13,14},{14,13},{15,10},{10,... | collective-permute-start | bytes 1179656 | tf_op jit(solution)/shard_map/ppermute | solution.py:636
  65.5 8.5 %collective-permute-start.15 = (f32[768,128]{1,0:T(8,128)S(1)}, f32[768,128]{1,0:T(8,128)S(1)}, u32[]{:S(2)}, u32[]{:S(2)}) collective-permute-start(f32[768,128]{1,0:T(8,128)S(1)} %get-tuple-element.90), channel_id=1, source_target_pairs={{0,1},{1,0},{4,5},{5,4},{8,9},{9,8},{12,13},{13,12},{14,15},{15,14... | collective-permute-start | bytes 1179656 | tf_op jit(solution)/shard_map/ppermute | solution.py:637
  80.8 7.9 %collective-permute-start.16 = (f32[56,512]{1,0:T(8,128)S(1)}, f32[56,512]{1,0:T(8,128)S(1)}, u32[]{:S(2)}, u32[]{:S(2)}) collective-permute-start(f32[56,512]{1,0:T(8,128)S(1)} %shard_map.122.misfit), channel_id=1, source_target_pairs={{1,4},{4,1},{5,8},{8,5},{9,12},{12,9},{13,14},{14,13},{15,10},{10,... | collective-permute-start | bytes 344072 | tf_op jit(solution)/shard_map/ppermute | solution.py:636
  81.4 7.2 %collective-permute-start.17 = (f32[56,512]{1,0:T(8,128)S(1)}, f32[56,512]{1,0:T(8,128)S(1)}, u32[]{:S(2)}, u32[]{:S(2)}) collective-permute-start(f32[56,512]{1,0:T(8,128)S(1)} %shard_map.122.misfit), channel_id=1, source_target_pairs={{0,1},{1,0},{4,5},{5,4},{8,9},{9,8},{12,13},{13,12},{14,15},{15,14... | collective-permute-start | bytes 344072 | tf_op jit(solution)/shard_map/ppermute | solution.py:637
  95.6 8.3 %collective-permute-start.18 = (f32[768,128]{1,0:T(8,128)S(1)}, f32[768,128]{1,0:T(8,128)S(1)}, u32[]{:S(2)}, u32[]{:S(2)}) collective-permute-start(f32[768,128]{1,0:T(8,128)S(1)} %get-tuple-element.95), channel_id=1, source_target_pairs={{1,4},{4,1},{5,8},{8,5},{9,12},{12,9},{13,14},{14,13},{15,10},{10,... | collective-permute-start | bytes 1179656 | tf_op jit(solution)/shard_map/ppermute | solution.py:636
  96.5 7.4 %collective-permute-start.19 = (f32[768,128]{1,0:T(8,128)S(1)}, f32[768,128]{1,0:T(8,128)S(1)}, u32[]{:S(2)}, u32[]{:S(2)}) collective-permute-start(f32[768,128]{1,0:T(8,128)S(1)} %get-tuple-element.95), channel_id=1, source_target_pairs={{0,1},{1,0},{4,5},{5,4},{8,9},{9,8},{12,13},{13,12},{14,15},{15,14... | collective-permute-start | bytes 1179656 | tf_op jit(solution)/shard_map/ppermute | solution.py:637
  108.8 9.4 %collective-permute-start.20 = (f32[768,128]{1,0:T(8,128)S(1)}, f32[768,128]{1,0:T(8,128)S(1)}, u32[]{:S(2)}, u32[]{:S(2)}) collective-permute-start(f32[768,128]{1,0:T(8,128)S(1)} %get-tuple-element.97), channel_id=1, source_target_pairs={{1,4},{4,1},{5,8},{8,5},{9,12},{12,9},{13,14},{14,13},{15,10},{10,... | collective-permute-start | bytes 1179656 | tf_op jit(solution)/shard_map/ppermute | solution.py:636
  109.5 8.7 %collective-permute-start.21 = (f32[768,128]{1,0:T(8,128)S(1)}, f32[768,128]{1,0:T(8,128)S(1)}, u32[]{:S(2)}, u32[]{:S(2)}) collective-permute-start(f32[768,128]{1,0:T(8,128)S(1)} %get-tuple-element.97), channel_id=1, source_target_pairs={{0,1},{1,0},{4,5},{5,4},{8,9},{9,8},{12,13},{13,12},{14,15},{15,14... | collective-permute-start | bytes 1179656 | tf_op jit(solution)/shard_map/ppermute | solution.py:637
  123.9 10.2 %collective-permute-start.22 = (f32[176,128]{1,0:T(8,128)S(1)}, f32[176,128]{1,0:T(8,128)S(1)}, u32[]{:S(2)}, u32[]{:S(2)}) collective-permute-start(f32[176,128]{1,0:T(8,128)S(1)} %get-tuple-element.100), channel_id=1, source_target_pairs={{0,0},{8,1},{14,2},{6,3},{1,4},{9,5},{15,6},{7,7},{4,8},{12,9},{10... | collective-permute-start | bytes 270344 | tf_op jit(solution)/shard_map/ppermute | solution.py:797
  124.6 9.6 %collective-permute-start.23 = (f32[176,128]{1,0:T(8,128)S(1)}, f32[176,128]{1,0:T(8,128)S(1)}, u32[]{:S(2)}, u32[]{:S(2)}) collective-permute-start(f32[176,128]{1,0:T(8,128)S(1)} %get-tuple-element.101), channel_id=1, source_target_pairs={{1,0},{9,1},{15,2},{7,3},{0,4},{8,5},{14,6},{6,7},{5,8},{13,9},{11... | collective-permute-start | bytes 270344 | tf_op jit(solution)/shard_map/ppermute | solution.py:797
  (5 other events, 14.7 us)

commit v2 on v1

--- a/solution.py
+++ b/solution.py
@@ -81,14 +81,15 @@
 
 
 def call(
-    kernel, ints, arrays, outs, scratch=(), cost=1_000_000, space=pltpu.VMEM, aliases=None, limit=32 * 1024 * 1024
+    kernel, ints, arrays, outs, scratch=(), cost=1_000_000, space=pltpu.VMEM, aliases=None,
+    out_space=pltpu.VMEM, limit=32 * 1024 * 1024
 ):
     return pl.pallas_call(
         kernel,
         out_shape=tuple(outs),
         in_specs=[pl.BlockSpec(memory_space=pltpu.SMEM)] * len(ints)
         + [pl.BlockSpec(memory_space=space)] * len(arrays),
-        out_specs=tuple(pl.BlockSpec(memory_space=pltpu.VMEM) for _ in outs),
+        out_specs=tuple(pl.BlockSpec(memory_space=out_space) for _ in outs),
         scratch_shapes=list(scratch),
         input_output_aliases=aliases or {},
         compiler_params=pltpu.CompilerParams(vmem_limit_bytes=limit),
@@ -100,42 +101,41 @@
     return pl.multiple_of(value, to)
 
 
-def cut_chunk(lay, slab, turn, fields, target):
-    start = (slab ^ turn) * lay.chunk
-    for index, field in enumerate(fields):
-        for y in range(lay.chunk):
-            row = (index * lay.chunk + y) * ROWS
-            target[row : row + ROWS, :] = field[pl.ds(start + y, ROWS, stride=lay.width_y), :]
-
-
 def cut_forward(lay, slab_ref, count_ref, *refs):
-    inputs, sends, (held, held_cell, done) = refs[:4], refs[4 : 4 + lay.count_x], refs[4 + lay.count_x :]
-    fields = [held.at[index] for index in range(3)]
-    copies = [
-        pltpu.make_async_copy(source, target, done.at[index])
-        for index, (source, target) in enumerate(zip(inputs, fields + [held_cell]))
-    ]
-    for copy in copies:
-        copy.start()
+    fields, cell, refs = refs[:3], refs[3], refs[4:]
+    sends, (held_cell, used, done, cells_done) = refs[: lay.count_x], refs[lay.count_x :]
+    copies = []
+    for turn, send in enumerate(sends):
+        chunk = pl.ds(aligned((slab_ref[0] ^ turn) * lay.chunk), lay.chunk)
+        for index, field in enumerate(fields):
+            source = field.at[:, chunk, :]
+            target = send.at[pl.ds(index * lay.width_x, lay.width_x)]
+            copies.append(pltpu.make_async_copy(source, target, done.at[turn, index]))
+            copies[-1].start()
+    loaded = pltpu.make_async_copy(cell, held_cell, cells_done.at[0])
+    loaded.start()
+    loaded.wait()
+    slots = lax.broadcasted_iota(jnp.int32, (1, LANES), 1)
+    used[...] = jnp.full(used.shape, -1.0, jnp.float32)
+    for tile in range(lay.count_x):
+        line = jnp.where(slots < count_ref[tile], held_cell[tile : tile + 1, :], -1)
+        used[tile : tile + 1, :] = line.astype(jnp.float32)
+    for turn, send in enumerate(sends):
+        target = send.at[3 * lay.width_x]
+        copies.append(pltpu.make_async_copy(used, target, done.at[turn, 3]))
+        copies[-1].start()
     for copy in copies:
         copy.wait()
-    slots = lax.broadcasted_iota(jnp.int32, (1, LANES), 1)
-    used = []
-    for tile in range(lay.count_x):
-        cell = jnp.where(slots < count_ref[tile], held_cell[tile : tile + 1, :], -1)
-        used.append(cell.astype(jnp.float32))
-    for turn, send in enumerate(sends):
-        cut_chunk(lay, slab_ref[0], turn, fields, send)
-        for tile in range(lay.count_x):
-            row = 3 * lay.cells + tile
-            send[row : row + 1, :] = used[tile]
 
 
 def cut_adjoint(lay, slab_ref, now, prev, observed, *sends):
     for turn, send in enumerate(sends):
-        cut_chunk(lay, slab_ref[0], turn, (now, prev), send)
-        row = 2 * lay.cells
-        send[row : row + observed.shape[0], :] = observed[...]
+        chunk = pl.ds(aligned((slab_ref[0] ^ turn) * lay.chunk), lay.chunk)
+        for index, field in enumerate((now, prev)):
+            send[index * lay.width_x : (index + 1) * lay.width_x] = field[:, chunk, :]
+        for index in range(observed.shape[0] // lay.chunk):
+            rows = observed[index * lay.chunk : (index + 1) * lay.chunk, :]
+            send[2 * lay.width_x + index] = rows
 
 
 def join_fields(lay, own_slot, odd, pieces, joined, state, courant, send_next, send_twin):
@@ -144,8 +144,8 @@
         start_x = (own_slot ^ turn) * ROWS
         for field in range(fields):
             for y in range(lay.chunk):
-                row = (field * lay.chunk + y) * ROWS
-                joined[field, pl.ds(aligned(y * lay.wide + start_x), ROWS), :] = piece[row : row + ROWS, :]
+                rows = pl.ds(field * lay.cells + y, ROWS, stride=lay.chunk)
+                joined[field, pl.ds(aligned(y * lay.wide + start_x), ROWS), :] = piece[rows, :]
     kept_rows = lay.kept * lay.wide
     for field in range(fields):
         target, first = (state, 0) if field == 0 else (state, (lay.chunk + REACH) * lay.wide)
@@ -275,7 +275,7 @@
 
 def sweep(lay, step, now, prev, following, half, gain, band, along_z, inject=None):
     first_layer = REACH * (step + 1)
-    group = 8
+    group, quad = 8, 4
     reach_rows = REACH * lay.stride
     multiply_z(lay, first_layer, lay.extent - 2 * first_layer, now, band, along_z)
 
@@ -290,6 +290,8 @@
         half_rows, gain_rows = half.at[flat_rows], gain.at[flat_rows]
         added = None if inject is None else inject.at[step, flat_rows]
 
+        z_rows = along_z.at[pl.ds(aligned(block * group * lay.wide), group * lay.wide)]
+
         def place(y, tile):
             return (y * lay.tiles + tile) * 2 * ROWS + ROWS
 
@@ -300,24 +302,38 @@
         def beside(y, tile, shift):
             return now[pl.ds(base + (place(y + REACH, tile) + shift), ROWS), :]
 
-        z_rows = along_z.at[pl.ds(aligned(block * group * lay.wide), group * lay.wide)]
-        for y in range(group):
-            center = [at(y, tile) for tile in range(lay.tiles)]
-            lower = [beside(y, tile, -1) for tile in range(lay.tiles)]
-            upper = [beside(y, tile, 1) for tile in range(lay.tiles)]
-            line = lower + center + upper
+        def layers_from(first):
+            inside = range(first, first + quad)
+            centers = {y: [] for y in inside}
+            totals = {y: [] for y in inside}
             for tile in range(lay.tiles):
-                flat_at = (y * lay.tiles + tile) * ROWS
-                total = z_rows[flat_at : flat_at + ROWS, :] + weights[0] * center[tile]
-                for k in range(1, REACH + 1):
-                    pair = line[lay.tiles + tile - k] + line[lay.tiles + tile + k]
-                    total = total + weights[k] * (pair + (at(y - k, tile) + at(y + k, tile)))
-                if added is not None:
-                    total = total + added[pl.ds(y * lay.wide + tile, ROWS, stride=lay.tiles), :]
-                row = place(y, tile)
-                former = former_rows[row : row + ROWS, :]
-                change = (center[tile] - former) + half_rows[flat_at : flat_at + ROWS, :] * total
-                target[row : row + ROWS, :] = former + gain_rows[flat_at : flat_at + ROWS, :] * change
+                column = {y: at(y, tile) for y in range(first - REACH, first + quad + REACH)}
+                for y in inside:
+                    total = weights[0] * column[y]
+                    for k in range(1, REACH + 1):
+                        total = total + weights[k] * (column[y - k] + column[y + k])
+                    centers[y].append(column[y])
+                    totals[y].append(total)
+            for y in inside:
+                lower = [beside(y, tile, -1) for tile in range(lay.tiles)]
+                upper = [beside(y, tile, 1) for tile in range(lay.tiles)]
+                line = lower + centers[y] + upper
+                for tile in range(lay.tiles):
+                    total = totals[y][tile]
+                    for k in range(1, REACH + 1):
+                        pair = line[lay.tiles + tile - k] + line[lay.tiles + tile + k]
+                        total = total + weights[k] * pair
+                    flat_at = (y * lay.tiles + tile) * ROWS
+                    total = total + z_rows[flat_at : flat_at + ROWS, :]
+                    if added is not None:
+                        total = total + added[pl.ds(y * lay.wide + tile, ROWS, stride=lay.tiles), :]
+                    row = place(y, tile)
+                    former = former_rows[row : row + ROWS, :]
+                    change = (centers[y][tile] - former) + half_rows[flat_at : flat_at + ROWS, :] * total
+                    target[row : row + ROWS, :] = former + gain_rows[flat_at : flat_at + ROWS, :] * change
+
+        for first in range(0, group, quad):
+            layers_from(first)
         return carry
 
     lax.fori_loop(0, (lay.extent - 2 * first_layer) // group, layers, 0)
@@ -350,8 +366,7 @@
     history = refs.pop(0)
     half = refs.pop(0) if first else courant
     if not last:
-        state_out, send, tie = [refs.pop(0) for _ in range(3)]
-        tie[...] = jnp.zeros_like(tie)
+        state_out, send = refs.pop(0), refs.pop(0)
     now, prev, following, band, along_z, pulse = refs
     odd = ints[0]
 
@@ -645,31 +660,32 @@
     ints = jnp.concatenate([odd.reshape(1), padded, flat_row]).astype(jnp.int32)
 
     traces = flat(observed)
-    forward_rows = 3 * lay.cells + -(-count // ROWS) * ROWS
-    back_rows = 2 * lay.cells + traces.shape[0]
+    forward_shape = f32(3 * lay.width_x + 1, lay.chunk, LANES)
+    back_shape = f32(2 * lay.width_x + traces.shape[0] // lay.chunk, lay.chunk, LANES)
     cuts = call(
         part(cut_forward, lay),
         (slab_int, receiver_count.reshape(-1)),
-        [flat(field) for field in (state_now, state_prev, courant)] + [receiver_cell.reshape(count, LANES)],
-        [f32(forward_rows, LANES)] * count,
+        [state_now, state_prev, courant, receiver_cell.reshape(count, LANES)],
+        [forward_shape] * count,
         [
-            pltpu.VMEM((3, lay.width_x * lay.width_y, LANES), jnp.float32),
             pltpu.VMEM((count, LANES), jnp.int32),
-            pltpu.SemaphoreType.DMA((4,)),
+            pltpu.VMEM((lay.chunk, LANES), jnp.float32),
+            pltpu.SemaphoreType.DMA((count, 4)),
+            pltpu.SemaphoreType.DMA((1,)),
         ],
         space=pltpu.HBM,
+        out_space=pltpu.HBM,
         limit=60 * 1024 * 1024,
     )
     back_cuts = call(
         part(cut_adjoint, lay),
         (slab_int,),
-        [flat(adjoint_now), flat(adjoint_next), traces],
-        [f32(back_rows, LANES)] * count,
-    )
-    pieces = [lax.ppermute(cut, axes, lay.to_chunks(turn)) for turn, cut in enumerate(cuts)]
+        [adjoint_now, adjoint_next, traces],
+        [back_shape] * count,
+    )
+    pieces = [flat(lax.ppermute(cut, axes, lay.to_chunks(turn))) for turn, cut in enumerate(cuts)]
     pieces, ints, gain, drive, back_cuts = lax.optimization_barrier((pieces, ints, gain, drive, back_cuts))
     kept_rows = lay.kept * lay.wide
-    tie_shape = f32(ROWS, LANES)
     state, own_courant, to_next, to_twin, codes = call(
         part(join_forward, lay),
         (where,),
@@ -683,11 +699,12 @@
 
     back_pieces = []
 
-    def move_adjoint(turns, tie):
+    def move_adjoint(turns, earlier):
         for turn in turns:
-            back_pieces.append(lax.ppermute(after(back_cuts[turn], tie), axes, lay.to_chunks(turn)))
-
-    move_adjoint(range(count), codes)
+            moved = lax.ppermute(after(back_cuts[turn], earlier), axes, lay.to_chunks(turn))
+            back_pieces.append(flat(moved))
+
+    move_adjoint(range(count - 2), codes)
 
     phases = STEPS // DEPTH
     step_cost = 8_000_000
@@ -703,11 +720,22 @@
     half = own_courant
     for phase in range(phases):
         first, last = phase == 0, phase == phases - 1
+        if last:
+            for history in histories:
+                records += call(
+                    part(record_phase, lay),
+                    (),
+                    [history, codes],
+                    [f32(*record_shape)],
+                    record_scratch,
+                    cost=side_cost,
+                )
+            state = after(state, records)
         outs = [history_shape]
         if first:
             outs.append(f32(lay.inner * lay.wide, LANES))
         if not last:
-            outs += state_shapes + [tie_shape]
+            outs += state_shapes
         results = list(
             call(
                 part(forward, lay, phase, sources),
@@ -724,19 +752,11 @@
             half = results.pop(0)
         if last:
             continue
-        state, send, tie = results
-        if first:
-            send = after(send, back_pieces)
+        state, send = results
+        send = after(send, back_pieces)
         from_next, from_twin = swap(send, send)
-    for history in histories[:-1]:
-        records += call(
-            part(record_phase, lay),
-            (),
-            [history, codes],
-            [f32(*record_shape)],
-            record_scratch,
-            cost=side_cost,
-        )
+        move_adjoint([count - 2 + phase], send)
+    back_pieces = after(back_pieces, histories[-1])
     back_state, to_next, to_twin = call(
         part(join_adjoint, lay),
         (where,),
@@ -754,7 +774,6 @@
         cost=side_cost,
     )
 
-    misfit = after(misfit, [back_from_next, back_from_twin])
     misfit_next, misfit_twin = swap(misfit, misfit)
     state, from_next, from_twin = back_state, back_from_next, back_from_twin
     gradient = None

time: 140 us -> 168 us (1.20)
  Pallas kernels: 53.3 us -> 76.3 us
  waiting for transfers between devices: 16.9 us -> 25 us
  starting transfers between devices: 60.5 us -> 57.9 us
    pallas_call x23, Pallas kernels: 53.3 us -> 76.3 us  [call(): pl.pallas_call(kernel, out_shape=tuple(outs), in_specs=[pl.BlockSpec(memo...]
    ppermute x4, waiting for transfers between devices: 6.4 us -> 13 us  [move_adjoint(): lax.ppermute(after(back_cuts[turn], earlier), axes, lay.to_chunks(turn))]
    ppermute x7, starting transfers between devices: 29.2 us -> 27.3 us  [swap(): lax.ppermute(to_twin, axes, lay.swaps(0))]
  transfers between devices with their start and end apart: 26 -> 26, of which waited for: 5 -> 7; matrix products, arithmetic and copies ran while one was open for 2% -> 2% of each run, Pallas kernels for 23% -> 19%
where the time goes in v2:
time: 168 us; the launch traced here: 166 us
  Pallas kernels  76.3 us (45%)
  starting transfers between devices  57.9 us (34%)
  waiting for transfers between devices  25 us (15%)
  local copies, waits for them, and re-layouts  3.07 us (2%)
  other arithmetic  2.92 us (2%)
    pallas_call x23, Pallas kernels, call(): pl.pallas_call(kernel, out_shape=tuple(outs), in_specs=[pl.BlockSpec(memo...  76.3 us
    ppermute x7, starting transfers between devices, swap(): lax.ppermute(to_twin, axes, lay.swaps(0))  27.3 us
    ppermute x4, waiting for transfers between devices, move_adjoint(): lax.ppermute(after(back_cuts[turn], earlier), axes, lay.to_chunks(turn))  13 us
    ppermute x4, starting transfers between devices, local_tiles(): lax.ppermute(send, axes, lay.to_slabs(turn))  9.95 us
    ppermute x4, starting transfers between devices, local_tiles(): lax.ppermute(cut, axes, lay.to_chunks(turn))  9.33 us
    ppermute x4, waiting for transfers between devices, local_tiles(): lax.ppermute(cut, axes, lay.to_chunks(turn))  8.18 us
    ppermute x4, starting transfers between devices, move_adjoint(): lax.ppermute(after(back_cuts[turn], earlier), axes, lay.to_chunks(turn))  6.52 us
    ppermute x7, starting transfers between devices, swap(): lax.ppermute(to_next, axes, lay.swaps(1))  4.78 us
  transfers between devices with their start and end apart: 26, of which 7 were waited for; matrix products, arithmetic and copies ran while one was open for 2% of the time, Pallas kernels for 19%

profile of v2, /device:TPU:0, one launch (start us, length us, event | category | flops | bytes accessed | tf_op | source)
XLA Modules:
  0.0 166.3 jit_solution(7830694481637746177)
XLA Ops:
  0.6 25.7 %shard_map.113 = (f32[25,16,128]{2,1,0:T(8,128)}, f32[25,16,128]{2,1,0:T(8,128)}, f32[25,16,128]{2,1,0:T(8,128)}, f32[25,16,128]{2,1,0:T(8,128)}) custom-call(s32[1]{0:T(128)} %bitcast.slab_ref, s32[4]{0:T(128)} %bitcast.32, f32[8,64,128]{2,1,0:T(8,128)} %refs_0_.1, f32[8,64,128]{2,1,0:T(8,128)} %refs_1_.1, f32[8,64,128]{2,1,0:T(8,128)} %refs_2_.1, ...), custom_call_target="tpu_custom_call" | custom-call | flops 1000000 | bytes 1000000 | tf_op jit(solution)/shard_map/pallas_call | solution.py:87
  28.0 4.5 %collective-permute-start.1 = (f32[25,16,128]{2,1,0:T(8,128)}, f32[25,16,128]{2,1,0:T(8,128)S(1)}, u32[]{:S(2)}, u32[]{:S(2)}) collective-permute-start(f32[25,16,128]{2,1,0:T(8,128)} %get-tuple-element.60), channel_id=1, source_target_pairs={{0,1},{1,9},{2,15},{3,7},{4,0},{5,8},{6,14},{7,6},{8,5},{9,13},{10... | collective-permute-start | bytes 614408 | tf_op jit(solution)/shard_map/ppermute | solution.py:686
  32.5 3.2 %collective-permute-start.3 = (f32[25,16,128]{2,1,0:T(8,128)}, f32[25,16,128]{2,1,0:T(8,128)S(1)}, u32[]{:S(2)}, u32[]{:S(2)}) collective-permute-start(f32[25,16,128]{2,1,0:T(8,128)} %get-tuple-element.62), channel_id=1, source_target_pairs={{0,5},{1,13},{2,11},{3,3},{4,4},{5,12},{6,10},{7,2},{8,1},{9,9},{1... | collective-permute-start | bytes 614408 | tf_op jit(solution)/shard_map/ppermute | solution.py:686
  41.7 8.2 %collective-permute-done.2 = f32[25,16,128]{2,1,0:T(8,128)S(1)} collective-permute-done((f32[25,16,128]{2,1,0:T(8,128)}, f32[25,16,128]{2,1,0:T(8,128)S(1)}, u32[]{:S(2)}, u32[]{:S(2)}) %collective-permute-start.2) | collective-permute-done | bytes 204832 | tf_op jit(solution)/shard_map/ppermute | solution.py:686
  51.8 3.3 %collective-permute-start.7 = (f32[1280,128]{1,0:T(8,128)S(1)}, f32[1280,128]{1,0:T(8,128)S(1)}, u32[]{:S(2)}, u32[]{:S(2)}) collective-permute-start(f32[1280,128]{1,0:T(8,128)S(1)} %get-tuple-element.80), channel_id=1, source_target_pairs={{0,1},{1,0},{4,5},{5,4},{8,9},{9,8},{12,13},{13,12},{14,15},{15,14... | collective-permute-start | bytes 1966088 | tf_op jit(solution)/shard_map/ppermute | solution.py:652
  56.8 5.1 %shard_map.116 = (f32[2048,128]{1,0:T(8,128)S(1)}, f32[1280,128]{1,0:T(8,128)S(1)}, f32[1280,128]{1,0:T(8,128)S(1)}, f32[768,128]{1,0:T(8,128)S(1)}) custom-call(s32[33]{0:T(128)S(1)} %pad_add_fusion.1.ints, f32[1280,128]{1,0:T(8,128)S(1)} %get-tuple-element.78.state, f32[1280,128]{1,0:T(8,128)S(1)} %collective-permute-done.6.from_next, ...), custom_call_target="tpu_custom_call" | custom-call | flops 8000000 | bytes 8000000 | tf_op jit(solution)/shard_map/pallas_call | solution.py:87
  61.9 5.0 %collective-permute-done.5 = f32[19,16,128]{2,1,0:T(8,128)S(1)} collective-permute-done((f32[19,16,128]{2,1,0:T(8,128)S(1)}, f32[19,16,128]{2,1,0:T(8,128)S(1)}, u32[]{:S(2)}, u32[]{:S(2)}) %collective-permute-start.5) | collective-permute-done | bytes 155680 | tf_op jit(solution)/shard_map/ppermute | solution.py:704
  66.8 3.3 %collective-permute-start.10 = (f32[768,128]{1,0:T(8,128)S(1)}, f32[768,128]{1,0:T(8,128)S(1)}, u32[]{:S(2)}, u32[]{:S(2)}) collective-permute-start(f32[768,128]{1,0:T(8,128)S(1)} %get-tuple-element.85), channel_id=1, source_target_pairs={{0,1},{1,0},{4,5},{5,4},{8,9},{9,8},{12,13},{13,12},{14,15},{15,14... | collective-permute-start | bytes 1179656 | tf_op jit(solution)/shard_map/ppermute | solution.py:652
  70.8 2.9 %collective-permute-start.8 = (f32[19,16,128]{2,1,0:T(8,128)S(1)}, f32[19,16,128]{2,1,0:T(8,128)S(1)}, u32[]{:S(2)}, u32[]{:S(2)}) collective-permute-start(f32[19,16,128]{2,1,0:T(8,128)S(1)} %get-tuple-element.86), channel_id=1, source_target_pairs={{0,4},{1,12},{2,10},{3,2},{4,5},{5,13},{6,11},{7,3},{8,0},{9,8},{1... | collective-permute-start | bytes 466952 | tf_op jit(solution)/shard_map/ppermute | solution.py:704
  73.7 5.0 %shard_map.117 = (f32[2048,128]{1,0:T(8,128)S(1)}, f32[1280,128]{1,0:T(8,128)S(1)}, f32[768,128]{1,0:T(8,128)S(1)}) custom-call(s32[33]{0:T(128)S(1)} %pad_add_fusion.1.ints, f32[1280,128]{1,0:T(8,128)S(1)} %get-tuple-element.88.state, f32[768,128]{1,0:T(8,128)S(1)} %collective-permute-done.9.from_next, f32[768,128]{1,0:T(8,128)S(1)} %collective-permute-done.10.from_twin, ...), custom_call_target="tpu_custom_call" | custom-call | flops 8000000 | bytes 8000000 | tf_op jit(solution)/shard_map/pallas_call | solution.py:87
  78.7 4.6 %collective-permute-done.8 = f32[19,16,128]{2,1,0:T(8,128)S(1)} collective-permute-done((f32[19,16,128]{2,1,0:T(8,128)S(1)}, f32[19,16,128]{2,1,0:T(8,128)S(1)}, u32[]{:S(2)}, u32[]{:S(2)}) %collective-permute-start.8) | collective-permute-done | bytes 155680 | tf_op jit(solution)/shard_map/ppermute | solution.py:704
  84.0 4.6 %collective-permute-start.13 = (f32[768,128]{1,0:T(8,128)S(1)}, f32[768,128]{1,0:T(8,128)S(1)}, u32[]{:S(2)}, u32[]{:S(2)}) collective-permute-start(f32[768,128]{1,0:T(8,128)S(1)} %get-tuple-element.91), channel_id=1, source_target_pairs={{0,1},{1,0},{4,5},{5,4},{8,9},{9,8},{12,13},{13,12},{14,15},{15,14... | collective-permute-start | bytes 1179656 | tf_op jit(solution)/shard_map/ppermute | solution.py:652
  88.6 2.9 %collective-permute-start.11 = (f32[19,16,128]{2,1,0:T(8,128)S(1)}, f32[19,16,128]{2,1,0:T(8,128)S(1)}, u32[]{:S(2)}, u32[]{:S(2)}) collective-permute-start(f32[19,16,128]{2,1,0:T(8,128)S(1)} %get-tuple-element.92), channel_id=1, source_target_pairs={{0,5},{1,13},{2,11},{3,3},{4,4},{5,12},{6,10},{7,2},{8,1},{9,9},{1... | collective-permute-start | bytes 466952 | tf_op jit(solution)/shard_map/ppermute | solution.py:704
  94.3 4.9 %shard_map.120.history = f32[2048,128]{1,0:T(8,128)S(1)} custom-call(s32[33]{0:T(128)S(1)} %pad_add_fusion.1.ints, f32[1280,128]{1,0:T(8,128)S(1)} %get-tuple-element.96.state, f32[768,128]{1,0:T(8,128)S(1)} %collective-permute-done.12.from_next, f32[768,128]{1,0:T(8,128)S(1)} %collective-permute-done.13.from_twin, ...), custom_call_target="tpu_custom_call" | custom-call | flops 8000000 | bytes 8000000 | tf_op jit(solution)/shard_map/pallas_call | solution.py:87
  99.2 3.4 %collective-permute-done.11 = f32[19,16,128]{2,1,0:T(8,128)S(1)} collective-permute-done((f32[19,16,128]{2,1,0:T(8,128)S(1)}, f32[19,16,128]{2,1,0:T(8,128)S(1)}, u32[]{:S(2)}, u32[]{:S(2)}) %collective-permute-start.11) | collective-permute-done | bytes 155680 | tf_op jit(solution)/shard_map/ppermute | solution.py:704
  104.2 4.8 %collective-permute-start.15 = (f32[896,128]{1,0:T(8,128)S(1)}, f32[896,128]{1,0:T(8,128)S(1)}, u32[]{:S(2)}, u32[]{:S(2)}) collective-permute-start(f32[896,128]{1,0:T(8,128)S(1)} %get-tuple-element.103), channel_id=1, source_target_pairs={{0,1},{1,0},{4,5},{5,4},{8,9},{9,8},{12,13},{13,12},{14,15},{15,14... | collective-permute-start | bytes 1376264 | tf_op jit(solution)/shard_map/ppermute | solution.py:652
  111.6 3.1 %collective-permute-start.17 = (f32[56,512]{1,0:T(8,128)S(1)}, f32[56,512]{1,0:T(8,128)S(1)}, u32[]{:S(2)}, u32[]{:S(2)}) collective-permute-start(f32[56,512]{1,0:T(8,128)S(1)} %shard_map.122.misfit), channel_id=1, source_target_pairs={{0,1},{1,0},{4,5},{5,4},{8,9},{9,8},{12,13},{13,12},{14,15},{15,14... | collective-permute-start | bytes 344072 | tf_op jit(solution)/shard_map/ppermute | solution.py:652
  118.6 5.1 %shard_map.125 = (f32[2048,128]{1,0:T(8,128)S(1)}, f32[1280,128]{1,0:T(8,128)S(1)}, f32[768,128]{1,0:T(8,128)S(1)}) custom-call(s32[2]{0:T(128)S(1)} %pad_add_fusion.where_ref, f32[1280,128]{1,0:T(8,128)S(1)} %get-tuple-element.101.state, f32[896,128]{1,0:T(8,128)S(1)} %collective-permute-done.14.from_next, ...), custom_call_target="tpu_custom_call" | custom-call | flops 8000000 | bytes 8000000 | tf_op jit(solution)/shard_map/pallas_call | solution.py:87
  124.4 3.6 %collective-permute-start.19 = (f32[768,128]{1,0:T(8,128)S(1)}, f32[768,128]{1,0:T(8,128)S(1)}, u32[]{:S(2)}, u32[]{:S(2)}) collective-permute-start(f32[768,128]{1,0:T(8,128)S(1)} %get-tuple-element.105), channel_id=1, source_target_pairs={{0,1},{1,0},{4,5},{5,4},{8,9},{9,8},{12,13},{13,12},{14,15},{15,14... | collective-permute-start | bytes 1179656 | tf_op jit(solution)/shard_map/ppermute | solution.py:652
  131.8 5.1 %shard_map.128 = (f32[2048,128]{1,0:T(8,128)S(1)}, f32[1280,128]{1,0:T(8,128)S(1)}, f32[768,128]{1,0:T(8,128)S(1)}) custom-call(s32[2]{0:T(128)S(1)} %pad_add_fusion.where_ref, f32[1280,128]{1,0:T(8,128)S(1)} %get-tuple-element.104.state, f32[768,128]{1,0:T(8,128)S(1)} %collective-permute-done.18.from_next, ...), custom_call_target="tpu_custom_call" | custom-call | flops 8000000 | bytes 8000000 | tf_op jit(solution)/shard_map/pallas_call | solution.py:87
  137.6 4.6 %collective-permute-start.21 = (f32[768,128]{1,0:T(8,128)S(1)}, f32[768,128]{1,0:T(8,128)S(1)}, u32[]{:S(2)}, u32[]{:S(2)}) collective-permute-start(f32[768,128]{1,0:T(8,128)S(1)} %get-tuple-element.107), channel_id=1, source_target_pairs={{0,1},{1,0},{4,5},{5,4},{8,9},{9,8},{12,13},{13,12},{14,15},{15,14... | collective-permute-start | bytes 1179656 | tf_op jit(solution)/shard_map/ppermute | solution.py:652
  146.8 5.0 %shard_map.131.adjoint = f32[2048,128]{1,0:T(8,128)S(1)} custom-call(s32[2]{0:T(128)S(1)} %pad_add_fusion.where_ref, f32[1280,128]{1,0:T(8,128)S(1)} %get-tuple-element.106.state, f32[768,128]{1,0:T(8,128)S(1)} %collective-permute-done.20.from_next, f32[768,128]{1,0:T(8,128)S(1)} %collective-permute-done.21.from_twin, ...), custom_call_target="tpu_custom_call" | custom-call | flops 8000000 | bytes 8000000 | tf_op jit(solution)/shard_map/pallas_call | solution.py:87
  153.4 4.7 %collective-permute-start.23 = (f32[176,128]{1,0:T(8,128)S(1)}, f32[176,128]{1,0:T(8,128)S(1)}, u32[]{:S(2)}, u32[]{:S(2)}) collective-permute-start(f32[176,128]{1,0:T(8,128)S(1)} %get-tuple-element.111), channel_id=1, source_target_pairs={{1,0},{9,1},{15,2},{7,3},{0,4},{8,5},{14,6},{6,7},{5,8},{13,9},{11... | collective-permute-start | bytes 270344 | tf_op jit(solution)/shard_map/ppermute | solution.py:816
  159.7 3.0 %collective-permute-start.25 = (f32[176,128]{1,0:T(8,128)S(1)}, f32[176,128]{1,0:T(8,128)S(1)}, u32[]{:S(2)}, u32[]{:S(2)}) collective-permute-start(f32[176,128]{1,0:T(8,128)S(1)} %get-tuple-element.113), channel_id=1, source_target_pairs={{5,0},{13,1},{11,2},{3,3},{4,4},{12,5},{10,6},{2,7},{1,8},{9,9},{1... | collective-permute-start | bytes 270344 | tf_op jit(solution)/shard_map/ppermute | solution.py:816
  (73 shorter events, 39.6 us)
Async XLA Ops:
  26.4 15.3 %collective-permute-start = (f32[25,16,128]{2,1,0:T(8,128)}, f32[25,16,128]{2,1,0:T(8,128)S(1)}, u32[]{:S(2)}, u32[]{:S(2)}) collective-permute-start(f32[25,16,128]{2,1,0:T(8,128)} %get-tuple-element.59), channel_id=1, source_target_pairs={{0,0},{1,8},{2,14},{3,6},{4,1},{5,9},{6,15},{7,7},{8,4},{9,12},{10... | collective-permute-start | bytes 614408 | tf_op jit(solution)/shard_map/ppermute | solution.py:686
  28.0 13.7 %collective-permute-start.1 = (f32[25,16,128]{2,1,0:T(8,128)}, f32[25,16,128]{2,1,0:T(8,128)S(1)}, u32[]{:S(2)}, u32[]{:S(2)}) collective-permute-start(f32[25,16,128]{2,1,0:T(8,128)} %get-tuple-element.60), channel_id=1, source_target_pairs={{0,1},{1,9},{2,15},{3,7},{4,0},{5,8},{6,14},{7,6},{8,5},{9,13},{10... | collective-permute-start | bytes 614408 | tf_op jit(solution)/shard_map/ppermute | solution.py:686
  32.5 17.4 %collective-permute-start.2 = (f32[25,16,128]{2,1,0:T(8,128)}, f32[25,16,128]{2,1,0:T(8,128)S(1)}, u32[]{:S(2)}, u32[]{:S(2)}) collective-permute-start(f32[25,16,128]{2,1,0:T(8,128)} %get-tuple-element.61), channel_id=1, source_target_pairs={{0,4},{1,12},{2,10},{3,2},{4,5},{5,13},{6,11},{7,3},{8,0},{9,8},{1... | collective-permute-start | bytes 614408 | tf_op jit(solution)/shard_map/ppermute | solution.py:686
  32.5 17.4 %collective-permute-start.3 = (f32[25,16,128]{2,1,0:T(8,128)}, f32[25,16,128]{2,1,0:T(8,128)S(1)}, u32[]{:S(2)}, u32[]{:S(2)}) collective-permute-start(f32[25,16,128]{2,1,0:T(8,128)} %get-tuple-element.62), channel_id=1, source_target_pairs={{0,5},{1,13},{2,11},{3,3},{4,4},{5,12},{6,10},{7,2},{8,1},{9,9},{1... | collective-permute-start | bytes 614408 | tf_op jit(solution)/shard_map/ppermute | solution.py:686
  51.8 5.0 %collective-permute-start.7 = (f32[1280,128]{1,0:T(8,128)S(1)}, f32[1280,128]{1,0:T(8,128)S(1)}, u32[]{:S(2)}, u32[]{:S(2)}) collective-permute-start(f32[1280,128]{1,0:T(8,128)S(1)} %get-tuple-element.80), channel_id=1, source_target_pairs={{0,1},{1,0},{4,5},{5,4},{8,9},{9,8},{12,13},{13,12},{14,15},{15,14... | collective-permute-start | bytes 1966088 | tf_op jit(solution)/shard_map/ppermute | solution.py:652
  55.1 11.8 %collective-permute-start.5 = (f32[19,16,128]{2,1,0:T(8,128)S(1)}, f32[19,16,128]{2,1,0:T(8,128)S(1)}, u32[]{:S(2)}, u32[]{:S(2)}) collective-permute-start(f32[19,16,128]{2,1,0:T(8,128)S(1)} %get-tuple-element.75), channel_id=1, source_target_pairs={{0,1},{1,9},{2,15},{3,7},{4,0},{5,8},{6,14},{7,6},{8,5},{9,13},{10... | collective-permute-start | bytes 466952 | tf_op jit(solution)/shard_map/ppermute | solution.py:704
  55.1 11.7 %collective-permute-start.4 = (f32[19,16,128]{2,1,0:T(8,128)S(1)}, f32[19,16,128]{2,1,0:T(8,128)S(1)}, u32[]{:S(2)}, u32[]{:S(2)}) collective-permute-start(f32[19,16,128]{2,1,0:T(8,128)S(1)} %get-tuple-element.73), channel_id=1, source_target_pairs={{0,0},{1,8},{2,14},{3,6},{4,1},{5,9},{6,15},{7,7},{8,4},{9,12},{10... | collective-permute-start | bytes 466952 | tf_op jit(solution)/shard_map/ppermute | solution.py:704
  66.8 6.9 %collective-permute-start.10 = (f32[768,128]{1,0:T(8,128)S(1)}, f32[768,128]{1,0:T(8,128)S(1)}, u32[]{:S(2)}, u32[]{:S(2)}) collective-permute-start(f32[768,128]{1,0:T(8,128)S(1)} %get-tuple-element.85), channel_id=1, source_target_pairs={{0,1},{1,0},{4,5},{5,4},{8,9},{9,8},{12,13},{13,12},{14,15},{15,14... | collective-permute-start | bytes 1179656 | tf_op jit(solution)/shard_map/ppermute | solution.py:652
  70.8 12.5 %collective-permute-start.8 = (f32[19,16,128]{2,1,0:T(8,128)S(1)}, f32[19,16,128]{2,1,0:T(8,128)S(1)}, u32[]{:S(2)}, u32[]{:S(2)}) collective-permute-start(f32[19,16,128]{2,1,0:T(8,128)S(1)} %get-tuple-element.86), channel_id=1, source_target_pairs={{0,4},{1,12},{2,10},{3,2},{4,5},{5,13},{6,11},{7,3},{8,0},{9,8},{1... | collective-permute-start | bytes 466952 | tf_op jit(solution)/shard_map/ppermute | solution.py:704
  83.3 11.0 %collective-permute-start.12 = (f32[768,128]{1,0:T(8,128)S(1)}, f32[768,128]{1,0:T(8,128)S(1)}, u32[]{:S(2)}, u32[]{:S(2)}) collective-permute-start(f32[768,128]{1,0:T(8,128)S(1)} %get-tuple-element.91), channel_id=1, source_target_pairs={{1,4},{4,1},{5,8},{8,5},{9,12},{12,9},{13,14},{14,13},{15,10},{10,... | collective-permute-start | bytes 1179656 | tf_op jit(solution)/shard_map/ppermute | solution.py:651
  84.0 10.3 %collective-permute-start.13 = (f32[768,128]{1,0:T(8,128)S(1)}, f32[768,128]{1,0:T(8,128)S(1)}, u32[]{:S(2)}, u32[]{:S(2)}) collective-permute-start(f32[768,128]{1,0:T(8,128)S(1)} %get-tuple-element.91), channel_id=1, source_target_pairs={{0,1},{1,0},{4,5},{5,4},{8,9},{9,8},{12,13},{13,12},{14,15},{15,14... | collective-permute-start | bytes 1179656 | tf_op jit(solution)/shard_map/ppermute | solution.py:652
  88.6 14.1 %collective-permute-start.11 = (f32[19,16,128]{2,1,0:T(8,128)S(1)}, f32[19,16,128]{2,1,0:T(8,128)S(1)}, u32[]{:S(2)}, u32[]{:S(2)}) collective-permute-start(f32[19,16,128]{2,1,0:T(8,128)S(1)} %get-tuple-element.92), channel_id=1, source_target_pairs={{0,5},{1,13},{2,11},{3,3},{4,4},{5,12},{6,10},{7,2},{8,1},{9,9},{1... | collective-permute-start | bytes 466952 | tf_op jit(solution)/shard_map/ppermute | solution.py:704
  103.5 15.2 %collective-permute-start.14 = (f32[896,128]{1,0:T(8,128)S(1)}, f32[896,128]{1,0:T(8,128)S(1)}, u32[]{:S(2)}, u32[]{:S(2)}) collective-permute-start(f32[896,128]{1,0:T(8,128)S(1)} %get-tuple-element.102), channel_id=1, source_target_pairs={{1,4},{4,1},{5,8},{8,5},{9,12},{12,9},{13,14},{14,13},{15,10},{10,... | collective-permute-start | bytes 1376264 | tf_op jit(solution)/shard_map/ppermute | solution.py:651
  104.2 14.5 %collective-permute-start.15 = (f32[896,128]{1,0:T(8,128)S(1)}, f32[896,128]{1,0:T(8,128)S(1)}, u32[]{:S(2)}, u32[]{:S(2)}) collective-permute-start(f32[896,128]{1,0:T(8,128)S(1)} %get-tuple-element.103), channel_id=1, source_target_pairs={{0,1},{1,0},{4,5},{5,4},{8,9},{9,8},{12,13},{13,12},{14,15},{15,14... | collective-permute-start | bytes 1376264 | tf_op jit(solution)/shard_map/ppermute | solution.py:652
  110.9 5.5 %collective-permute-start.16 = (f32[56,512]{1,0:T(8,128)S(1)}, f32[56,512]{1,0:T(8,128)S(1)}, u32[]{:S(2)}, u32[]{:S(2)}) collective-permute-start(f32[56,512]{1,0:T(8,128)S(1)} %shard_map.122.misfit), channel_id=1, source_target_pairs={{1,4},{4,1},{5,8},{8,5},{9,12},{12,9},{13,14},{14,13},{15,10},{10,... | collective-permute-start | bytes 344072 | tf_op jit(solution)/shard_map/ppermute | solution.py:651
  111.6 4.9 %collective-permute-start.17 = (f32[56,512]{1,0:T(8,128)S(1)}, f32[56,512]{1,0:T(8,128)S(1)}, u32[]{:S(2)}, u32[]{:S(2)}) collective-permute-start(f32[56,512]{1,0:T(8,128)S(1)} %shard_map.122.misfit), channel_id=1, source_target_pairs={{0,1},{1,0},{4,5},{5,4},{8,9},{9,8},{12,13},{13,12},{14,15},{15,14... | collective-permute-start | bytes 344072 | tf_op jit(solution)/shard_map/ppermute | solution.py:652
  123.7 8.0 %collective-permute-start.18 = (f32[768,128]{1,0:T(8,128)S(1)}, f32[768,128]{1,0:T(8,128)S(1)}, u32[]{:S(2)}, u32[]{:S(2)}) collective-permute-start(f32[768,128]{1,0:T(8,128)S(1)} %get-tuple-element.105), channel_id=1, source_target_pairs={{1,4},{4,1},{5,8},{8,5},{9,12},{12,9},{13,14},{14,13},{15,10},{10,... | collective-permute-start | bytes 1179656 | tf_op jit(solution)/shard_map/ppermute | solution.py:651
  124.4 7.3 %collective-permute-start.19 = (f32[768,128]{1,0:T(8,128)S(1)}, f32[768,128]{1,0:T(8,128)S(1)}, u32[]{:S(2)}, u32[]{:S(2)}) collective-permute-start(f32[768,128]{1,0:T(8,128)S(1)} %get-tuple-element.105), channel_id=1, source_target_pairs={{0,1},{1,0},{4,5},{5,4},{8,9},{9,8},{12,13},{13,12},{14,15},{15,14... | collective-permute-start | bytes 1179656 | tf_op jit(solution)/shard_map/ppermute | solution.py:652
  136.9 9.8 %collective-permute-start.20 = (f32[768,128]{1,0:T(8,128)S(1)}, f32[768,128]{1,0:T(8,128)S(1)}, u32[]{:S(2)}, u32[]{:S(2)}) collective-permute-start(f32[768,128]{1,0:T(8,128)S(1)} %get-tuple-element.107), channel_id=1, source_target_pairs={{1,4},{4,1},{5,8},{8,5},{9,12},{12,9},{13,14},{14,13},{15,10},{10,... | collective-permute-start | bytes 1179656 | tf_op jit(solution)/shard_map/ppermute | solution.py:651
  137.6 9.2 %collective-permute-start.21 = (f32[768,128]{1,0:T(8,128)S(1)}, f32[768,128]{1,0:T(8,128)S(1)}, u32[]{:S(2)}, u32[]{:S(2)}) collective-permute-start(f32[768,128]{1,0:T(8,128)S(1)} %get-tuple-element.107), channel_id=1, source_target_pairs={{0,1},{1,0},{4,5},{5,4},{8,9},{9,8},{12,13},{13,12},{14,15},{15,14... | collective-permute-start | bytes 1179656 | tf_op jit(solution)/shard_map/ppermute | solution.py:652
  152.7 10.0 %collective-permute-start.22 = (f32[176,128]{1,0:T(8,128)S(1)}, f32[176,128]{1,0:T(8,128)S(1)}, u32[]{:S(2)}, u32[]{:S(2)}) collective-permute-start(f32[176,128]{1,0:T(8,128)S(1)} %get-tuple-element.110), channel_id=1, source_target_pairs={{0,0},{8,1},{14,2},{6,3},{1,4},{9,5},{15,6},{7,7},{4,8},{12,9},{10... | collective-permute-start | bytes 270344 | tf_op jit(solution)/shard_map/ppermute | solution.py:816
  153.4 9.3 %collective-permute-start.23 = (f32[176,128]{1,0:T(8,128)S(1)}, f32[176,128]{1,0:T(8,128)S(1)}, u32[]{:S(2)}, u32[]{:S(2)}) collective-permute-start(f32[176,128]{1,0:T(8,128)S(1)} %get-tuple-element.111), channel_id=1, source_target_pairs={{1,0},{9,1},{15,2},{7,3},{0,4},{8,5},{14,6},{6,7},{5,8},{13,9},{11... | collective-permute-start | bytes 270344 | tf_op jit(solution)/shard_map/ppermute | solution.py:816
  158.1 6.3 %collective-permute-start.24 = (f32[176,128]{1,0:T(8,128)S(1)}, f32[176,128]{1,0:T(8,128)S(1)}, u32[]{:S(2)}, u32[]{:S(2)}) collective-permute-start(f32[176,128]{1,0:T(8,128)S(1)} %get-tuple-element.112), channel_id=1, source_target_pairs={{4,0},{12,1},{10,2},{2,3},{5,4},{13,5},{11,6},{3,7},{0,8},{8,9},{1... | collective-permute-start | bytes 270344 | tf_op jit(solution)/shard_map/ppermute | solution.py:816
  159.7 5.9 %collective-permute-start.25 = (f32[176,128]{1,0:T(8,128)S(1)}, f32[176,128]{1,0:T(8,128)S(1)}, u32[]{:S(2)}, u32[]{:S(2)}) collective-permute-start(f32[176,128]{1,0:T(8,128)S(1)} %get-tuple-element.113), channel_id=1, source_target_pairs={{5,0},{13,1},{11,2},{3,3},{4,4},{12,5},{10,6},{2,7},{1,8},{9,9},{1... | collective-permute-start | bytes 270344 | tf_op jit(solution)/shard_map/ppermute | solution.py:816
  (5 other events, 11.0 us)

commit v3 on v1

--- a/solution.py
+++ b/solution.py
@@ -31,8 +31,6 @@
         self.whole_y = width_y * count_y
         self.margin = REACH * DEPTH
         self.extent = self.chunk + 2 * self.margin
-        self.stride = self.tiles * 2 * ROWS
-        self.padded_rows = self.extent * self.stride + ROWS
         self.kept = self.margin - REACH
         self.inner = self.extent - 2 * REACH
         self.rows = self.chunk * self.wide
@@ -197,46 +195,36 @@
 
 
 def load_state(lay, odd, first, now, prev, state, from_next, from_twin):
-    def put(buffer, layer, ref, source):
-        for tile in range(lay.tiles):
-            row = layer * lay.stride + (2 * tile + 1) * ROWS
-            values = ref[source * lay.wide + tile * ROWS : source * lay.wide + (tile + 1) * ROWS, :]
-            buffer[pl.ds(row if isinstance(row, int) else aligned(row), ROWS), :] = values
+    wide = lay.wide
+
+    def put(buffer, layer, ref, source, count):
+        target = pl.ds(layer * wide if isinstance(layer, int) else aligned(layer * wide), count * wide)
+        buffer[target, :] = ref[source * wide : (source + count) * wide, :]
 
     ahead = lay.margin + lay.chunk
-    for y in range(lay.chunk):
-        put(now, lay.margin + y, state, y)
-        put(now, odd * ahead + y, from_next, y)
-        put(now, (1 - odd) * ahead + y, from_twin, y)
+    put(now, lay.margin, state, 0, lay.chunk)
+    put(now, odd * ahead, from_next, 0, lay.chunk)
+    put(now, (1 - odd) * ahead, from_twin, 0, lay.chunk)
     if first:
-        for y in range(lay.chunk):
-            put(prev, lay.margin + y, state, lay.chunk + REACH + y)
-        for y in range(lay.kept):
-            put(prev, odd * ahead + (1 - odd) * REACH + y, from_next, lay.chunk + y)
-            put(prev, (1 - odd) * ahead + odd * REACH + y, from_twin, lay.chunk + y)
+        put(prev, lay.margin, state, lay.chunk + REACH, lay.chunk)
+        put(prev, odd * ahead + (1 - odd) * REACH, from_next, lay.chunk, lay.kept)
+        put(prev, (1 - odd) * ahead + odd * REACH, from_twin, lay.chunk, lay.kept)
         return
-    for y in range(lay.near):
-        put(prev, lay.margin - REACH + y, state, lay.chunk + y)
-    for index, y in enumerate(lay.lacking):
-        put(prev, odd * ahead + y, from_next, lay.chunk + index)
-        put(prev, (1 - odd) * ahead + y, from_twin, lay.chunk + index)
+    put(prev, lay.margin - REACH, state, lay.chunk, lay.near)
+    put(prev, odd * ahead + lay.lacking[0], from_next, lay.chunk, len(lay.lacking))
+    put(prev, (1 - odd) * ahead + lay.lacking[0], from_twin, lay.chunk, len(lay.lacking))
 
 
 def store_state(lay, now, prev, state, send):
-    def put(refs, target, buffer, layer):
-        for tile in range(lay.tiles):
-            row = layer * lay.stride + (2 * tile + 1) * ROWS
-            values = buffer[row : row + ROWS, :]
-            for ref, place in refs:
-                ref[place * lay.wide + tile * ROWS : place * lay.wide + (tile + 1) * ROWS, :] = values
-
-    for y in range(lay.chunk):
-        put([(state, y), (send, y)], y, now, lay.margin + y)
-    for y in range(lay.near):
-        refs = [(state, lay.chunk + y)]
-        if y - REACH in lay.lacking:
-            refs.append((send, lay.chunk + y - REACH - lay.lacking[0]))
-        put(refs, y, prev, lay.margin - REACH + y)
+    wide = lay.wide
+
+    def put(ref, target, buffer, layer, count):
+        ref[target * wide : (target + count) * wide, :] = buffer[layer * wide : (layer + count) * wide, :]
+
+    put(state, 0, now, lay.margin, lay.chunk)
+    put(send, 0, now, lay.margin, lay.chunk)
+    put(state, lay.chunk, prev, lay.margin - REACH, lay.near)
+    put(send, lay.chunk, prev, lay.margin + lay.lacking[0], len(lay.lacking))
 
 
 def split(values):
@@ -260,88 +248,61 @@
 
 
 def multiply_z(lay, first_layer, count, now, band, along_z):
-    tiles = []
-    for y in range(count):
-        for tile in range(lay.tiles):
-            row = (first_layer + y) * lay.stride + (2 * tile + 1) * ROWS
-            tiles.append(now[row : row + ROWS, :])
-    half = len(tiles) // 2
-    parts = [split(jnp.concatenate(group, axis=0)) for group in (tiles[:half], tiles[half:])]
+    half = count * lay.wide // 2
+    first = first_layer * lay.wide
+    parts = [split(now[start : start + half, :]) for start in (first, first + half)]
     both = [side[part] for part in range(3) for side in parts]
     found = jnp.dot(jnp.concatenate(both, axis=1), band[...], preferred_element_type=jnp.float32)
-    along_z[0 : half * ROWS, :] = found[:, :LANES]
-    along_z[half * ROWS : 2 * half * ROWS, :] = found[:, LANES:]
+    along_z[0:half, :] = found[:, :LANES]
+    along_z[half : 2 * half, :] = found[:, LANES:]
 
 
 def sweep(lay, step, now, prev, following, half, gain, band, along_z, inject=None):
     first_layer = REACH * (step + 1)
     group = 8
-    reach_rows = REACH * lay.stride
     multiply_z(lay, first_layer, lay.extent - 2 * first_layer, now, band, along_z)
+    row = lax.broadcasted_iota(jnp.int32, (ROWS, LANES), 0)
+    top, bottom = row == 0, row == ROWS - 1
 
     def layers(block, carry):
         start = first_layer + group * block
-        base = aligned((start - REACH) * lay.stride)
-        around = now.at[pl.ds(base, (group + 2 * REACH) * lay.stride)]
-        middle_rows = pl.ds(aligned(base + reach_rows), group * lay.stride)
-        former_rows, target = prev.at[middle_rows], following.at[middle_rows]
-        flat = aligned((start - REACH) * lay.wide)
-        flat_rows = pl.ds(flat, group * lay.wide)
-        half_rows, gain_rows = half.at[flat_rows], gain.at[flat_rows]
-        added = None if inject is None else inject.at[step, flat_rows]
-
-        def place(y, tile):
-            return (y * lay.tiles + tile) * 2 * ROWS + ROWS
+        around = now.at[pl.ds(aligned((start - REACH) * lay.wide), (group + 2 * REACH) * lay.wide)]
+        here = pl.ds(aligned(start * lay.wide), group * lay.wide)
+        former_rows, target = prev.at[here], following.at[here]
+        inner = pl.ds(aligned((start - REACH) * lay.wide), group * lay.wide)
+        half_rows, gain_rows = half.at[inner], gain.at[inner]
+        added = None if inject is None else inject.at[step, inner]
+        z_rows = along_z.at[pl.ds(aligned(block * group * lay.wide), group * lay.wide)]
 
         def at(y, tile):
-            row = place(y + REACH, tile)
-            return around[row : row + ROWS, :]
-
-        def beside(y, tile, shift):
-            return now[pl.ds(base + (place(y + REACH, tile) + shift), ROWS), :]
-
-        z_rows = along_z.at[pl.ds(aligned(block * group * lay.wide), group * lay.wide)]
+            first = ((y + REACH) * lay.tiles + tile) * ROWS
+            return around[first : first + ROWS, :]
+
         for y in range(group):
             center = [at(y, tile) for tile in range(lay.tiles)]
-            lower = [beside(y, tile, -1) for tile in range(lay.tiles)]
-            upper = [beside(y, tile, 1) for tile in range(lay.tiles)]
+            lower = [jnp.where(top, 0.0, pltpu.roll(tile, 1, 0)) for tile in center]
+            upper = [jnp.where(bottom, 0.0, pltpu.roll(tile, ROWS - 1, 0)) for tile in center]
             line = lower + center + upper
             for tile in range(lay.tiles):
-                flat_at = (y * lay.tiles + tile) * ROWS
-                total = z_rows[flat_at : flat_at + ROWS, :] + weights[0] * center[tile]
+                place = (y * lay.tiles + tile) * ROWS
+                place = slice(place, place + ROWS)
+                total = z_rows[place, :] + weights[0] * center[tile]
                 for k in range(1, REACH + 1):
                     pair = line[lay.tiles + tile - k] + line[lay.tiles + tile + k]
                     total = total + weights[k] * (pair + (at(y - k, tile) + at(y + k, tile)))
                 if added is not None:
                     total = total + added[pl.ds(y * lay.wide + tile, ROWS, stride=lay.tiles), :]
-                row = place(y, tile)
-                former = former_rows[row : row + ROWS, :]
-                change = (center[tile] - former) + half_rows[flat_at : flat_at + ROWS, :] * total
-                target[row : row + ROWS, :] = former + gain_rows[flat_at : flat_at + ROWS, :] * change
+                former = former_rows[place, :]
+                change = (center[tile] - former) + half_rows[place, :] * total
+                target[place, :] = former + gain_rows[place, :] * change
         return carry
 
     lax.fori_loop(0, (lay.extent - 2 * first_layer) // group, layers, 0)
 
 
-def zero_between(lay, step, buffer):
-    zeros = jnp.zeros((ROWS, LANES), jnp.float32)
-    first = REACH * (step + 1)
-    for row in range(first * lay.stride, (lay.extent - first) * lay.stride + 1, 2 * ROWS):
-        buffer[row : row + ROWS, :] = zeros
-
-
-def zero_buffers(lay, now, prev, following):
-    zero_between(lay, 0, now)
-    zero_between(lay, 1, following)
-    zero_between(lay, 2, prev)
-
-
 def keep_own(lay, step, following, history):
-    for y in range(lay.chunk):
-        for tile in range(lay.tiles):
-            row = (lay.margin + y) * lay.stride + (2 * tile + 1) * ROWS
-            place = step * lay.rows + y * lay.wide + tile * ROWS
-            history[place : place + ROWS, :] = following[row : row + ROWS, :]
+    first = lay.margin * lay.wide
+    history[step * lay.rows : (step + 1) * lay.rows, :] = following[first : first + lay.rows, :]
 
 
 def forward(lay, phase, sources, ints, state, from_next, from_twin, courant, gain, drive, *refs):
@@ -350,14 +311,12 @@
     history = refs.pop(0)
     half = refs.pop(0) if first else courant
     if not last:
-        state_out, send, tie = [refs.pop(0) for _ in range(3)]
-        tie[...] = jnp.zeros_like(tie)
+        state_out, send = refs.pop(0), refs.pop(0)
     now, prev, following, band, along_z, pulse = refs
     odd = ints[0]
 
     fill_band(band)
     load_state(lay, odd, first, now, prev, state, from_next, from_twin)
-    zero_buffers(lay, now, prev, following)
     if first:
         tail = (lay.chunk + lay.kept) * lay.wide
         part = lay.kept * lay.wide
@@ -508,7 +467,6 @@
 
     fill_band(band)
     load_state(lay, where_ref[1], first, now, prev, state, from_next, from_twin)
-    zero_buffers(lay, now, prev, following)
     for step in range(DEPTH):
         sweep(lay, step, now, prev, following, half, gain, band, along_z, inject)
         keep_own(lay, step, following, history)
@@ -593,12 +551,12 @@
     z = source_cell % LANES
     inside = (y >= REACH) & (y < lay.extent - REACH)
     tile, row = x % lay.tiles, x // lay.tiles
-    padded = jnp.where(inside, y * lay.stride + (2 * tile + 1) * ROWS + row, ROWS // 2)
     flat = jnp.where(inside, (y - REACH) * lay.wide + tile * ROWS + row, 0)
-    same = (padded[:, None] == padded[None, :]) & inside[None, :]
+    buffer_row = jnp.where(inside, flat + REACH * lay.wide, 0)
+    same = (buffer_row[:, None] == buffer_row[None, :]) & inside[None, :]
     spot = (z[:, None] == jnp.arange(LANES)[None, :]).astype(jnp.float32)
     lines = jnp.where(same[None, :, :, None], wavelet[:, None, :, None] * spot[None, None], 0.0)
-    return padded, flat, jnp.sum(lines, axis=2)
+    return buffer_row, flat, jnp.sum(lines, axis=2)
 
 
 def local_tiles(
@@ -640,9 +598,9 @@
     def after(value, others):
         return lax.optimization_barrier((value, others))[0]
 
-    padded, flat_row, drive = source_rows(lay, first_y, source_cell, wavelet)
+    buffer_row, flat_row, drive = source_rows(lay, first_y, source_cell, wavelet)
     gain = gain_rows(lay, first_y)
-    ints = jnp.concatenate([odd.reshape(1), padded, flat_row]).astype(jnp.int32)
+    ints = jnp.concatenate([odd.reshape(1), buffer_row, flat_row]).astype(jnp.int32)
 
     traces = flat(observed)
     forward_rows = 3 * lay.cells + -(-count // ROWS) * ROWS
@@ -669,7 +627,6 @@
     pieces = [lax.ppermute(cut, axes, lay.to_chunks(turn)) for turn, cut in enumerate(cuts)]
     pieces, ints, gain, drive, back_cuts = lax.optimization_barrier((pieces, ints, gain, drive, back_cuts))
     kept_rows = lay.kept * lay.wide
-    tie_shape = f32(ROWS, LANES)
     state, own_courant, to_next, to_twin, codes = call(
         part(join_forward, lay),
         (where,),
@@ -681,20 +638,21 @@
     )
     from_next, from_twin = swap(to_next, to_twin)
 
-    back_pieces = []
-
-    def move_adjoint(turns, tie):
+    back_pieces = [None] * count
+
+    def move_adjoint(turns, earlier):
         for turn in turns:
-            back_pieces.append(lax.ppermute(after(back_cuts[turn], tie), axes, lay.to_chunks(turn)))
-
-    move_adjoint(range(count), codes)
+            back_pieces[turn] = lax.ppermute(after(back_cuts[turn], earlier), axes, lay.to_chunks(turn))
+
+    move_adjoint(range(1, count), codes)
+    move_adjoint(range(1), from_twin)
 
     phases = STEPS // DEPTH
     step_cost = 8_000_000
     side_cost = 4_000_000
     history_shape = f32(DEPTH * lay.rows, LANES)
     state_shapes = [f32(lay.state_rows, LANES), f32(lay.send_rows, LANES)]
-    buffers = [pltpu.VMEM((lay.padded_rows, LANES), jnp.float32)] * 3
+    buffers = [pltpu.VMEM((lay.extent * lay.wide, LANES), jnp.float32)] * 3
     buffers += [pltpu.VMEM((6 * LANES, 2 * LANES), jnp.bfloat16)]
     buffers += [pltpu.VMEM((lay.inner * lay.wide, LANES), jnp.float32)]
     record_scratch = [pltpu.VMEM((DEPTH * lay.rows, LANES), jnp.float32)]
@@ -707,7 +665,7 @@
         if first:
             outs.append(f32(lay.inner * lay.wide, LANES))
         if not last:
-            outs += state_shapes + [tie_shape]
+            outs += state_shapes
         results = list(
             call(
                 part(forward, lay, phase, sources),
@@ -724,7 +682,7 @@
             half = results.pop(0)
         if last:
             continue
-        state, send, tie = results
+        state, send = results
         if first:
             send = after(send, back_pieces)
         from_next, from_twin = swap(send, send)

time: 140 us -> 140 us (level); the launches traced: 138 us -> 139 us
  waiting for transfers between devices: 16.9 us -> 20.7 us
  Pallas kernels: 53.3 us -> 51.8 us
    ppermute x4, waiting for transfers between devices: 2.85 us -> 4.8 us  [local_tiles(): lax.ppermute(send, axes, lay.to_slabs(turn))]
    ppermute x4, waiting for transfers between devices: 6.4 us -> 8.26 us  [move_adjoint(): lax.ppermute(after(back_cuts[turn], earlier), axes, lay.to_chunks(turn))]
    pallas_call x23, Pallas kernels: 53.3 us -> 51.8 us  [call(): pl.pallas_call(kernel, out_shape=tuple(outs), in_specs=[pl.BlockSpec(memo...]
  transfers between devices with their start and end apart: 26 -> 26, of which waited for: 5 -> 5; matrix products, arithmetic and copies ran while one was open for 2% -> 2% of each run, Pallas kernels for 23% -> 21%
where the time goes in v3:
time: 140 us; the launch traced here: 139 us
  starting transfers between devices  59.5 us (42%)
  Pallas kernels  51.8 us (37%)
  waiting for transfers between devices  20.7 us (15%)
  local copies, waits for them, and re-layouts  3.07 us (2%)
  other arithmetic  2.9 us (2%)
    pallas_call x23, Pallas kernels, call(): pl.pallas_call(kernel, out_shape=tuple(outs), in_specs=[pl.BlockSpec(memo...  51.8 us
    ppermute x7, starting transfers between devices, swap(): lax.ppermute(to_twin, axes, lay.swaps(0))  27.8 us
    ppermute x4, starting transfers between devices, local_tiles(): lax.ppermute(send, axes, lay.to_slabs(turn))  10.6 us
    ppermute x4, starting transfers between devices, local_tiles(): lax.ppermute(cut, axes, lay.to_chunks(turn))  9.33 us
    ppermute x4, waiting for transfers between devices, move_adjoint(): lax.ppermute(after(back_cuts[turn], earlier), axes, lay.to_chunks(turn))  8.26 us
    ppermute x4, waiting for transfers between devices, local_tiles(): lax.ppermute(cut, axes, lay.to_chunks(turn))  7.62 us
    ppermute x4, starting transfers between devices, move_adjoint(): lax.ppermute(after(back_cuts[turn], earlier), axes, lay.to_chunks(turn))  6.57 us
    ppermute x7, starting transfers between devices, swap(): lax.ppermute(to_next, axes, lay.swaps(1))  5.18 us
  transfers between devices with their start and end apart: 26, of which 5 were waited for; matrix products, arithmetic and copies ran while one was open for 2% of the time, Pallas kernels for 21%

profile of v3, /device:TPU:0, one launch (start us, length us, event | category | flops | bytes accessed | tf_op | source)
XLA Modules:
  0.0 139.2 jit_solution(6741120759792049608)
XLA Ops:
  0.6 3.1 %shard_map.113 = (f32[392,128]{1,0:T(8,128)}, f32[392,128]{1,0:T(8,128)}, f32[392,128]{1,0:T(8,128)}, f32[392,128]{1,0:T(8,128)}) custom-call(s32[1]{0:T(128)} %bitcast.slab_ref, s32[4]{0:T(128)} %bitcast.22, f32[512,128]{1,0:T(8,128)} %bitcast.18, f32[512,128]{1,0:T(8,128)} %bitcast.19, f32[512,128]{1,0:T(8,128)} %bitcast.20, s32[4,128]{1,0:T(4,128)} %bitcast.21), custom_call_target="tpu_custom_call" | custom-call | flops 1000000 | bytes 1000000 | tf_op jit(solution)/shard_map/pallas_call | solution.py:84
  5.3 4.5 %collective-permute-start.1 = (f32[392,128]{1,0:T(8,128)}, f32[392,128]{1,0:T(8,128)S(1)}, u32[]{:S(2)}, u32[]{:S(2)}) collective-permute-start(f32[392,128]{1,0:T(8,128)} %get-tuple-element.55), channel_id=1, source_target_pairs={{0,1},{1,9},{2,15},{3,7},{4,0},{5,8},{6,14},{7,6},{8,5},{9,13},{10... | collective-permute-start | bytes 602120 | tf_op jit(solution)/shard_map/ppermute | solution.py:627
  9.9 3.2 %collective-permute-start.3 = (f32[392,128]{1,0:T(8,128)}, f32[392,128]{1,0:T(8,128)S(1)}, u32[]{:S(2)}, u32[]{:S(2)}) collective-permute-start(f32[392,128]{1,0:T(8,128)} %get-tuple-element.57), channel_id=1, source_target_pairs={{0,5},{1,13},{2,11},{3,3},{4,4},{5,12},{6,10},{7,2},{8,1},{9,9},{1... | collective-permute-start | bytes 602120 | tf_op jit(solution)/shard_map/ppermute | solution.py:627
  19.3 7.6 %collective-permute-done.2.refs_2_ = f32[392,128]{1,0:T(8,128)S(1)} collective-permute-done((f32[392,128]{1,0:T(8,128)}, f32[392,128]{1,0:T(8,128)S(1)}, u32[]{:S(2)}, u32[]{:S(2)}) %collective-permute-start.2) | collective-permute-done | bytes 200736 | tf_op jit(solution)/shard_map/ppermute | solution.py:627
  27.9 2.0 %collective-permute-start.4 = (f32[1280,128]{1,0:T(8,128)S(1)}, f32[1280,128]{1,0:T(8,128)S(1)}, u32[]{:S(2)}, u32[]{:S(2)}) collective-permute-start(f32[1280,128]{1,0:T(8,128)S(1)} %get-tuple-element.67), channel_id=1, source_target_pairs={{0,1},{1,0},{4,5},{5,4},{8,9},{9,8},{12,13},{13,12},{14,15},{15,14... | collective-permute-start | bytes 1966088 | tf_op jit(solution)/shard_map/ppermute | solution.py:595
  30.7 3.3 %collective-permute-start.8 = (f32[304,128]{1,0:T(8,128)S(1)}, f32[304,128]{1,0:T(8,128)S(1)}, u32[]{:S(2)}, u32[]{:S(2)}) collective-permute-start(f32[304,128]{1,0:T(8,128)S(1)} %get-tuple-element.75), channel_id=1, source_target_pairs={{0,5},{1,13},{2,11},{3,3},{4,4},{5,12},{6,10},{7,2},{8,1},{9,9},{1... | collective-permute-start | bytes 466952 | tf_op jit(solution)/shard_map/ppermute | solution.py:645
  34.3 2.3 %collective-permute-start.6 = (f32[304,128]{1,0:T(8,128)S(1)}, f32[304,128]{1,0:T(8,128)S(1)}, u32[]{:S(2)}, u32[]{:S(2)}) collective-permute-start(f32[304,128]{1,0:T(8,128)S(1)} %get-tuple-element.71), channel_id=1, source_target_pairs={{0,1},{1,9},{2,15},{3,7},{4,0},{5,8},{6,14},{7,6},{8,5},{9,13},{10... | collective-permute-start | bytes 466952 | tf_op jit(solution)/shard_map/ppermute | solution.py:645
  37.3 4.9 %shard_map.117 = (f32[2048,128]{1,0:T(8,128)S(1)}, f32[1280,128]{1,0:T(8,128)S(1)}, f32[1280,128]{1,0:T(8,128)S(1)}, f32[768,128]{1,0:T(8,128)S(1)}) custom-call(s32[33]{0:T(128)S(1)} %pad_add_fusion.1.ints, f32[1280,128]{1,0:T(8,128)S(1)} %get-tuple-element.80.state, f32[1280,128]{1,0:T(8,128)S(1)} %collective-permute-done.11.from_next, ...), custom_call_target="tpu_custom_call" | custom-call | flops 8000000 | bytes 8000000 | tf_op jit(solution)/shard_map/pallas_call | solution.py:84
  42.1 5.0 %collective-permute-done.8.refs_3_.refs_5_ = f32[304,128]{1,0:T(8,128)S(1)} collective-permute-done((f32[304,128]{1,0:T(8,128)S(1)}, f32[304,128]{1,0:T(8,128)S(1)}, u32[]{:S(2)}, u32[]{:S(2)}) %collective-permute-start.8) | collective-permute-done | bytes 155680 | tf_op jit(solution)/shard_map/ppermute | solution.py:645
  47.1 3.3 %collective-permute-done.6.refs_1_.refs_3_ = f32[304,128]{1,0:T(8,128)S(1)} collective-permute-done((f32[304,128]{1,0:T(8,128)S(1)}, f32[304,128]{1,0:T(8,128)S(1)}, u32[]{:S(2)}, u32[]{:S(2)}) %collective-permute-start.6) | collective-permute-done | bytes 155680 | tf_op jit(solution)/shard_map/ppermute | solution.py:645
  51.1 5.4 %collective-permute-start.13 = (f32[768,128]{1,0:T(8,128)S(1)}, f32[768,128]{1,0:T(8,128)S(1)}, u32[]{:S(2)}, u32[]{:S(2)}) collective-permute-start(f32[768,128]{1,0:T(8,128)S(1)} %get-tuple-element.88), channel_id=1, source_target_pairs={{0,1},{1,0},{4,5},{5,4},{8,9},{9,8},{12,13},{13,12},{14,15},{15,14... | collective-permute-start | bytes 1179656 | tf_op jit(solution)/shard_map/ppermute | solution.py:595
  58.0 4.8 %shard_map.118 = (f32[2048,128]{1,0:T(8,128)S(1)}, f32[1280,128]{1,0:T(8,128)S(1)}, f32[768,128]{1,0:T(8,128)S(1)}) custom-call(s32[33]{0:T(128)S(1)} %pad_add_fusion.1.ints, f32[1280,128]{1,0:T(8,128)S(1)} %get-tuple-element.86.state, f32[768,128]{1,0:T(8,128)S(1)} %collective-permute-done.12.from_next, f32[768,128]{1,0:T(8,128)S(1)} %collective-permute-done.13.from_twin, ...), custom_call_target="tpu_custom_call" | custom-call | flops 8000000 | bytes 8000000 | tf_op jit(solution)/shard_map/pallas_call | solution.py:84
  63.6 6.9 %collective-permute-start.15 = (f32[768,128]{1,0:T(8,128)S(1)}, f32[768,128]{1,0:T(8,128)S(1)}, u32[]{:S(2)}, u32[]{:S(2)}) collective-permute-start(f32[768,128]{1,0:T(8,128)S(1)} %get-tuple-element.90), channel_id=1, source_target_pairs={{0,1},{1,0},{4,5},{5,4},{8,9},{9,8},{12,13},{13,12},{14,15},{15,14... | collective-permute-start | bytes 1179656 | tf_op jit(solution)/shard_map/ppermute | solution.py:595
  73.4 4.7 %shard_map.119.history = f32[2048,128]{1,0:T(8,128)S(1)} custom-call(s32[33]{0:T(128)S(1)} %pad_add_fusion.1.ints, f32[1280,128]{1,0:T(8,128)S(1)} %get-tuple-element.89.state, f32[768,128]{1,0:T(8,128)S(1)} %collective-permute-done.14.from_next, f32[768,128]{1,0:T(8,128)S(1)} %collective-permute-done.15.from_twin, ...), custom_call_target="tpu_custom_call" | custom-call | flops 8000000 | bytes 8000000 | tf_op jit(solution)/shard_map/pallas_call | solution.py:84
  78.1 2.0 %shard_map.122.misfit = f32[56,512]{1,0:T(8,128)S(1)} custom-call(s32[2]{0:T(128)S(1)} %pad_add_fusion.where_ref, f32[2048,128]{1,0:T(8,128)S(1)} %shard_map.119.history, f32[4,512]{1,0:T(4,128)S(1)} %get-tuple-element.70.codes, f32[16,512]{1,0:T(8,128)S(1)} %shard_map.120.refs_0_, f32[16,512]{1,0:T(8,128)S(1)} %shard_map.121.refs_1_, ...), custom_call_target="tpu_custom_call" | custom-call | flops 4000000 | bytes 4000000 | tf_op jit(solution)/shard_map/pallas_call | solution.py:84
  80.8 5.4 %collective-permute-start.17 = (f32[56,512]{1,0:T(8,128)S(1)}, f32[56,512]{1,0:T(8,128)S(1)}, u32[]{:S(2)}, u32[]{:S(2)}) collective-permute-start(f32[56,512]{1,0:T(8,128)S(1)} %shard_map.122.misfit), channel_id=1, source_target_pairs={{0,1},{1,0},{4,5},{5,4},{8,9},{9,8},{12,13},{13,12},{14,15},{15,14... | collective-permute-start | bytes 344072 | tf_op jit(solution)/shard_map/ppermute | solution.py:595
  89.9 4.8 %shard_map.125 = (f32[2048,128]{1,0:T(8,128)S(1)}, f32[1280,128]{1,0:T(8,128)S(1)}, f32[768,128]{1,0:T(8,128)S(1)}) custom-call(s32[2]{0:T(128)S(1)} %pad_add_fusion.where_ref, f32[1280,128]{1,0:T(8,128)S(1)} %get-tuple-element.76.state, f32[896,128]{1,0:T(8,128)S(1)} %collective-permute-done.9.from_next, f32[896,128]{1,0:T(8,128)S(1)} %collective-permute-done.10.from_twin, ...), custom_call_target="tpu_custom_call" | custom-call | flops 8000000 | bytes 8000000 | tf_op jit(solution)/shard_map/pallas_call | solution.py:84
  95.7 3.6 %collective-permute-start.19 = (f32[768,128]{1,0:T(8,128)S(1)}, f32[768,128]{1,0:T(8,128)S(1)}, u32[]{:S(2)}, u32[]{:S(2)}) collective-permute-start(f32[768,128]{1,0:T(8,128)S(1)} %get-tuple-element.95), channel_id=1, source_target_pairs={{0,1},{1,0},{4,5},{5,4},{8,9},{9,8},{12,13},{13,12},{14,15},{15,14... | collective-permute-start | bytes 1179656 | tf_op jit(solution)/shard_map/ppermute | solution.py:595
  103.1 4.8 %shard_map.128 = (f32[2048,128]{1,0:T(8,128)S(1)}, f32[1280,128]{1,0:T(8,128)S(1)}, f32[768,128]{1,0:T(8,128)S(1)}) custom-call(s32[2]{0:T(128)S(1)} %pad_add_fusion.where_ref, f32[1280,128]{1,0:T(8,128)S(1)} %get-tuple-element.94.state, f32[768,128]{1,0:T(8,128)S(1)} %collective-permute-done.18.from_next, f32[768,128]{1,0:T(8,128)S(1)} %collective-permute-done.19.from_twin, ...), custom_call_target="tpu_custom_call" | custom-call | flops 8000000 | bytes 8000000 | tf_op jit(solution)/shard_map/pallas_call | solution.py:84
  108.6 4.4 %collective-permute-start.21 = (f32[768,128]{1,0:T(8,128)S(1)}, f32[768,128]{1,0:T(8,128)S(1)}, u32[]{:S(2)}, u32[]{:S(2)}) collective-permute-start(f32[768,128]{1,0:T(8,128)S(1)} %get-tuple-element.97), channel_id=1, source_target_pairs={{0,1},{1,0},{4,5},{5,4},{8,9},{9,8},{12,13},{13,12},{14,15},{15,14... | collective-permute-start | bytes 1179656 | tf_op jit(solution)/shard_map/ppermute | solution.py:595
  117.3 4.8 %shard_map.131.adjoint = f32[2048,128]{1,0:T(8,128)S(1)} custom-call(s32[2]{0:T(128)S(1)} %pad_add_fusion.where_ref, f32[1280,128]{1,0:T(8,128)S(1)} %get-tuple-element.96.state, f32[768,128]{1,0:T(8,128)S(1)} %collective-permute-done.20.from_next, f32[768,128]{1,0:T(8,128)S(1)} %collective-permute-done.21.from_twin, ...), custom_call_target="tpu_custom_call" | custom-call | flops 8000000 | bytes 8000000 | tf_op jit(solution)/shard_map/pallas_call | solution.py:84
  123.6 4.7 %collective-permute-start.23 = (f32[176,128]{1,0:T(8,128)S(1)}, f32[176,128]{1,0:T(8,128)S(1)}, u32[]{:S(2)}, u32[]{:S(2)}) collective-permute-start(f32[176,128]{1,0:T(8,128)S(1)} %get-tuple-element.101), channel_id=1, source_target_pairs={{1,0},{9,1},{15,2},{7,3},{0,4},{8,5},{14,6},{6,7},{5,8},{13,9},{11... | collective-permute-start | bytes 270344 | tf_op jit(solution)/shard_map/ppermute | solution.py:755
  128.4 3.3 %collective-permute-start.24 = (f32[176,128]{1,0:T(8,128)S(1)}, f32[176,128]{1,0:T(8,128)S(1)}, u32[]{:S(2)}, u32[]{:S(2)}) collective-permute-start(f32[176,128]{1,0:T(8,128)S(1)} %get-tuple-element.102), channel_id=1, source_target_pairs={{4,0},{12,1},{10,2},{2,3},{5,4},{13,5},{11,6},{3,7},{0,8},{8,9},{1... | collective-permute-start | bytes 270344 | tf_op jit(solution)/shard_map/ppermute | solution.py:755
  134.5 3.9 %collective-permute-done.25.refs_3_ = f32[176,128]{1,0:T(8,128)S(1)} collective-permute-done((f32[176,128]{1,0:T(8,128)S(1)}, f32[176,128]{1,0:T(8,128)S(1)}, u32[]{:S(2)}, u32[]{:S(2)}) %collective-permute-start.25) | collective-permute-done | bytes 90144 | tf_op jit(solution)/shard_map/ppermute | solution.py:755
  (72 shorter events, 35.3 us)
Async XLA Ops:
  3.7 15.5 %collective-permute-start = (f32[392,128]{1,0:T(8,128)}, f32[392,128]{1,0:T(8,128)S(1)}, u32[]{:S(2)}, u32[]{:S(2)}) collective-permute-start(f32[392,128]{1,0:T(8,128)} %get-tuple-element.54), channel_id=1, source_target_pairs={{0,0},{1,8},{2,14},{3,6},{4,1},{5,9},{6,15},{7,7},{8,4},{9,12},{10... | collective-permute-start | bytes 602120 | tf_op jit(solution)/shard_map/ppermute | solution.py:627
  5.3 14.0 %collective-permute-start.1 = (f32[392,128]{1,0:T(8,128)}, f32[392,128]{1,0:T(8,128)S(1)}, u32[]{:S(2)}, u32[]{:S(2)}) collective-permute-start(f32[392,128]{1,0:T(8,128)} %get-tuple-element.55), channel_id=1, source_target_pairs={{0,1},{1,9},{2,15},{3,7},{4,0},{5,8},{6,14},{7,6},{8,5},{9,13},{10... | collective-permute-start | bytes 602120 | tf_op jit(solution)/shard_map/ppermute | solution.py:627
  9.9 17.1 %collective-permute-start.2 = (f32[392,128]{1,0:T(8,128)}, f32[392,128]{1,0:T(8,128)S(1)}, u32[]{:S(2)}, u32[]{:S(2)}) collective-permute-start(f32[392,128]{1,0:T(8,128)} %get-tuple-element.56), channel_id=1, source_target_pairs={{0,4},{1,12},{2,10},{3,2},{4,5},{5,13},{6,11},{7,3},{8,0},{9,8},{1... | collective-permute-start | bytes 602120 | tf_op jit(solution)/shard_map/ppermute | solution.py:627
  9.9 17.1 %collective-permute-start.3 = (f32[392,128]{1,0:T(8,128)}, f32[392,128]{1,0:T(8,128)S(1)}, u32[]{:S(2)}, u32[]{:S(2)}) collective-permute-start(f32[392,128]{1,0:T(8,128)} %get-tuple-element.57), channel_id=1, source_target_pairs={{0,5},{1,13},{2,11},{3,3},{4,4},{5,12},{6,10},{7,2},{8,1},{9,9},{1... | collective-permute-start | bytes 602120 | tf_op jit(solution)/shard_map/ppermute | solution.py:627
  27.9 8.6 %collective-permute-start.4 = (f32[1280,128]{1,0:T(8,128)S(1)}, f32[1280,128]{1,0:T(8,128)S(1)}, u32[]{:S(2)}, u32[]{:S(2)}) collective-permute-start(f32[1280,128]{1,0:T(8,128)S(1)} %get-tuple-element.67), channel_id=1, source_target_pairs={{0,1},{1,0},{4,5},{5,4},{8,9},{9,8},{12,13},{13,12},{14,15},{15,14... | collective-permute-start | bytes 1966088 | tf_op jit(solution)/shard_map/ppermute | solution.py:595
  30.0 7.3 %collective-permute-start.11 = (f32[1280,128]{1,0:T(8,128)S(1)}, f32[1280,128]{1,0:T(8,128)S(1)}, u32[]{:S(2)}, u32[]{:S(2)}) collective-permute-start(f32[1280,128]{1,0:T(8,128)S(1)} %get-tuple-element.81), channel_id=1, source_target_pairs={{1,4},{4,1},{5,8},{8,5},{9,12},{12,9},{13,14},{14,13},{15,10},{10,... | collective-permute-start | bytes 1966088 | tf_op jit(solution)/shard_map/ppermute | solution.py:594
  30.7 16.5 %collective-permute-start.8 = (f32[304,128]{1,0:T(8,128)S(1)}, f32[304,128]{1,0:T(8,128)S(1)}, u32[]{:S(2)}, u32[]{:S(2)}) collective-permute-start(f32[304,128]{1,0:T(8,128)S(1)} %get-tuple-element.75), channel_id=1, source_target_pairs={{0,5},{1,13},{2,11},{3,3},{4,4},{5,12},{6,10},{7,2},{8,1},{9,9},{1... | collective-permute-start | bytes 466952 | tf_op jit(solution)/shard_map/ppermute | solution.py:645
  33.9 13.2 %collective-permute-start.7 = (f32[304,128]{1,0:T(8,128)S(1)}, f32[304,128]{1,0:T(8,128)S(1)}, u32[]{:S(2)}, u32[]{:S(2)}) collective-permute-start(f32[304,128]{1,0:T(8,128)S(1)} %get-tuple-element.73), channel_id=1, source_target_pairs={{0,4},{1,12},{2,10},{3,2},{4,5},{5,13},{6,11},{7,3},{8,0},{9,8},{1... | collective-permute-start | bytes 466952 | tf_op jit(solution)/shard_map/ppermute | solution.py:645
  34.3 16.1 %collective-permute-start.6 = (f32[304,128]{1,0:T(8,128)S(1)}, f32[304,128]{1,0:T(8,128)S(1)}, u32[]{:S(2)}, u32[]{:S(2)}) collective-permute-start(f32[304,128]{1,0:T(8,128)S(1)} %get-tuple-element.71), channel_id=1, source_target_pairs={{0,1},{1,9},{2,15},{3,7},{4,0},{5,8},{6,14},{7,6},{8,5},{9,13},{10... | collective-permute-start | bytes 466952 | tf_op jit(solution)/shard_map/ppermute | solution.py:645
  36.6 13.8 %collective-permute-start.5 = (f32[304,128]{1,0:T(8,128)S(1)}, f32[304,128]{1,0:T(8,128)S(1)}, u32[]{:S(2)}, u32[]{:S(2)}) collective-permute-start(f32[304,128]{1,0:T(8,128)S(1)} %get-tuple-element.68), channel_id=1, source_target_pairs={{0,0},{1,8},{2,14},{3,6},{4,1},{5,9},{6,15},{7,7},{8,4},{9,12},{10... | collective-permute-start | bytes 466952 | tf_op jit(solution)/shard_map/ppermute | solution.py:645
  50.4 7.5 %collective-permute-start.12 = (f32[768,128]{1,0:T(8,128)S(1)}, f32[768,128]{1,0:T(8,128)S(1)}, u32[]{:S(2)}, u32[]{:S(2)}) collective-permute-start(f32[768,128]{1,0:T(8,128)S(1)} %get-tuple-element.88), channel_id=1, source_target_pairs={{1,4},{4,1},{5,8},{8,5},{9,12},{12,9},{13,14},{14,13},{15,10},{10,... | collective-permute-start | bytes 1179656 | tf_op jit(solution)/shard_map/ppermute | solution.py:594
  51.1 6.9 %collective-permute-start.13 = (f32[768,128]{1,0:T(8,128)S(1)}, f32[768,128]{1,0:T(8,128)S(1)}, u32[]{:S(2)}, u32[]{:S(2)}) collective-permute-start(f32[768,128]{1,0:T(8,128)S(1)} %get-tuple-element.88), channel_id=1, source_target_pairs={{0,1},{1,0},{4,5},{5,4},{8,9},{9,8},{12,13},{13,12},{14,15},{15,14... | collective-permute-start | bytes 1179656 | tf_op jit(solution)/shard_map/ppermute | solution.py:595
  57.2 22.9 %collective-permute-start.10 = (f32[896,128]{1,0:T(8,128)S(1)}, f32[896,128]{1,0:T(8,128)S(1)}, u32[]{:S(2)}, u32[]{:S(2)}) collective-permute-start(f32[896,128]{1,0:T(8,128)S(1)} %get-tuple-element.78), channel_id=1, source_target_pairs={{0,1},{1,0},{4,5},{5,4},{8,9},{9,8},{12,13},{13,12},{14,15},{15,14... | collective-permute-start | bytes 1376264 | tf_op jit(solution)/shard_map/ppermute | solution.py:595
  57.2 22.8 %collective-permute-start.9 = (f32[896,128]{1,0:T(8,128)S(1)}, f32[896,128]{1,0:T(8,128)S(1)}, u32[]{:S(2)}, u32[]{:S(2)}) collective-permute-start(f32[896,128]{1,0:T(8,128)S(1)} %get-tuple-element.77), channel_id=1, source_target_pairs={{1,4},{4,1},{5,8},{8,5},{9,12},{12,9},{13,14},{14,13},{15,10},{10,... | collective-permute-start | bytes 1376264 | tf_op jit(solution)/shard_map/ppermute | solution.py:594
  62.8 10.6 %collective-permute-start.14 = (f32[768,128]{1,0:T(8,128)S(1)}, f32[768,128]{1,0:T(8,128)S(1)}, u32[]{:S(2)}, u32[]{:S(2)}) collective-permute-start(f32[768,128]{1,0:T(8,128)S(1)} %get-tuple-element.90), channel_id=1, source_target_pairs={{1,4},{4,1},{5,8},{8,5},{9,12},{12,9},{13,14},{14,13},{15,10},{10,... | collective-permute-start | bytes 1179656 | tf_op jit(solution)/shard_map/ppermute | solution.py:594
  63.6 9.7 %collective-permute-start.15 = (f32[768,128]{1,0:T(8,128)S(1)}, f32[768,128]{1,0:T(8,128)S(1)}, u32[]{:S(2)}, u32[]{:S(2)}) collective-permute-start(f32[768,128]{1,0:T(8,128)S(1)} %get-tuple-element.90), channel_id=1, source_target_pairs={{0,1},{1,0},{4,5},{5,4},{8,9},{9,8},{12,13},{13,12},{14,15},{15,14... | collective-permute-start | bytes 1179656 | tf_op jit(solution)/shard_map/ppermute | solution.py:595
  80.1 7.9 %collective-permute-start.16 = (f32[56,512]{1,0:T(8,128)S(1)}, f32[56,512]{1,0:T(8,128)S(1)}, u32[]{:S(2)}, u32[]{:S(2)}) collective-permute-start(f32[56,512]{1,0:T(8,128)S(1)} %shard_map.122.misfit), channel_id=1, source_target_pairs={{1,4},{4,1},{5,8},{8,5},{9,12},{12,9},{13,14},{14,13},{15,10},{10,... | collective-permute-start | bytes 344072 | tf_op jit(solution)/shard_map/ppermute | solution.py:594
  80.8 7.2 %collective-permute-start.17 = (f32[56,512]{1,0:T(8,128)S(1)}, f32[56,512]{1,0:T(8,128)S(1)}, u32[]{:S(2)}, u32[]{:S(2)}) collective-permute-start(f32[56,512]{1,0:T(8,128)S(1)} %shard_map.122.misfit), channel_id=1, source_target_pairs={{0,1},{1,0},{4,5},{5,4},{8,9},{9,8},{12,13},{13,12},{14,15},{15,14... | collective-permute-start | bytes 344072 | tf_op jit(solution)/shard_map/ppermute | solution.py:595
  94.8 8.3 %collective-permute-start.18 = (f32[768,128]{1,0:T(8,128)S(1)}, f32[768,128]{1,0:T(8,128)S(1)}, u32[]{:S(2)}, u32[]{:S(2)}) collective-permute-start(f32[768,128]{1,0:T(8,128)S(1)} %get-tuple-element.95), channel_id=1, source_target_pairs={{1,4},{4,1},{5,8},{8,5},{9,12},{12,9},{13,14},{14,13},{15,10},{10,... | collective-permute-start | bytes 1179656 | tf_op jit(solution)/shard_map/ppermute | solution.py:594
  95.7 7.4 %collective-permute-start.19 = (f32[768,128]{1,0:T(8,128)S(1)}, f32[768,128]{1,0:T(8,128)S(1)}, u32[]{:S(2)}, u32[]{:S(2)}) collective-permute-start(f32[768,128]{1,0:T(8,128)S(1)} %get-tuple-element.95), channel_id=1, source_target_pairs={{0,1},{1,0},{4,5},{5,4},{8,9},{9,8},{12,13},{13,12},{14,15},{15,14... | collective-permute-start | bytes 1179656 | tf_op jit(solution)/shard_map/ppermute | solution.py:595
  107.9 9.4 %collective-permute-start.20 = (f32[768,128]{1,0:T(8,128)S(1)}, f32[768,128]{1,0:T(8,128)S(1)}, u32[]{:S(2)}, u32[]{:S(2)}) collective-permute-start(f32[768,128]{1,0:T(8,128)S(1)} %get-tuple-element.97), channel_id=1, source_target_pairs={{1,4},{4,1},{5,8},{8,5},{9,12},{12,9},{13,14},{14,13},{15,10},{10,... | collective-permute-start | bytes 1179656 | tf_op jit(solution)/shard_map/ppermute | solution.py:594
  108.6 8.7 %collective-permute-start.21 = (f32[768,128]{1,0:T(8,128)S(1)}, f32[768,128]{1,0:T(8,128)S(1)}, u32[]{:S(2)}, u32[]{:S(2)}) collective-permute-start(f32[768,128]{1,0:T(8,128)S(1)} %get-tuple-element.97), channel_id=1, source_target_pairs={{0,1},{1,0},{4,5},{5,4},{8,9},{9,8},{12,13},{13,12},{14,15},{15,14... | collective-permute-start | bytes 1179656 | tf_op jit(solution)/shard_map/ppermute | solution.py:595
  123.0 10.7 %collective-permute-start.22 = (f32[176,128]{1,0:T(8,128)S(1)}, f32[176,128]{1,0:T(8,128)S(1)}, u32[]{:S(2)}, u32[]{:S(2)}) collective-permute-start(f32[176,128]{1,0:T(8,128)S(1)} %get-tuple-element.100), channel_id=1, source_target_pairs={{0,0},{8,1},{14,2},{6,3},{1,4},{9,5},{15,6},{7,7},{4,8},{12,9},{10... | collective-permute-start | bytes 270344 | tf_op jit(solution)/shard_map/ppermute | solution.py:755
  123.6 10.0 %collective-permute-start.23 = (f32[176,128]{1,0:T(8,128)S(1)}, f32[176,128]{1,0:T(8,128)S(1)}, u32[]{:S(2)}, u32[]{:S(2)}) collective-permute-start(f32[176,128]{1,0:T(8,128)S(1)} %get-tuple-element.101), channel_id=1, source_target_pairs={{1,0},{9,1},{15,2},{7,3},{0,4},{8,5},{14,6},{6,7},{5,8},{13,9},{11... | collective-permute-start | bytes 270344 | tf_op jit(solution)/shard_map/ppermute | solution.py:755
  (5 other events, 15.5 us)

commit v4 on v3

--- a/solution.py
+++ b/solution.py
@@ -13,6 +13,7 @@
 DEPTH = 4
 LANES = 128
 ROWS = 8
+LAYERS = (4, 2, 1)
 
 
 stencil = (-205.0 / 72.0, 8.0 / 5.0, -1.0 / 5.0, 8.0 / 315.0, -1.0 / 560.0)
@@ -56,6 +57,17 @@
     def to_slabs(self, turn):
         return [(target, source) for source, target in self.to_chunks(turn)]
 
+    def across(self):
+        far = self.count_x // 2
+        return [(self.at(place), self.at(place ^ far)) for place in range(self.count_x * self.count_y)]
+
+    def home(self):
+        moves = []
+        for strip in range(self.count_y):
+            for slot in range(self.count_x):
+                moves.append((self.at(strip * self.count_x + slot), slot * self.count_y + strip))
+        return moves
+
     def swaps(self, first):
         moves = []
         for place in range(first, self.count_x * self.count_y - 1, 2):
@@ -66,6 +78,7 @@
 def fits(count_x, count_y, width_x, width_y, depth_z):
     return (
         count_x & (count_x - 1) == 0
+        and count_x == 4
         and count_y % 2 == 0
         and width_x == ROWS
         and width_x * count_x == ROWS * REACH
@@ -257,9 +270,8 @@
     along_z[half : 2 * half, :] = found[:, LANES:]
 
 
-def sweep(lay, step, now, prev, following, half, gain, band, along_z, inject=None):
+def sweep(lay, step, group, now, prev, following, half, gain, band, along_z, inject=None):
     first_layer = REACH * (step + 1)
-    group = 8
     multiply_z(lay, first_layer, lay.extent - 2 * first_layer, now, band, along_z)
     row = lax.broadcasted_iota(jnp.int32, (ROWS, LANES), 0)
     top, bottom = row == 0, row == ROWS - 1
@@ -329,7 +341,7 @@
         pulse[source : source + 1, :] = scale * (half[flat, :] * gain[flat, :])
 
     for step in range(DEPTH):
-        sweep(lay, step, now, prev, following, half, gain, band, along_z)
+        sweep(lay, step, LAYERS[phase], now, prev, following, half, gain, band, along_z)
         added = pulse[...] * drive[phase * DEPTH + step]
         places = [pl.ds(ints[1 + source], 1) for source in range(sources)]
         lines = [following[place, :] for place in places]
@@ -468,7 +480,7 @@
     fill_band(band)
     load_state(lay, where_ref[1], first, now, prev, state, from_next, from_twin)
     for step in range(DEPTH):
-        sweep(lay, step, now, prev, following, half, gain, band, along_z, inject)
+        sweep(lay, step, LAYERS[phase], now, prev, following, half, gain, band, along_z, inject)
         keep_own(lay, step, following, history)
         now, prev, following = following, now, prev
     if not last:
@@ -501,34 +513,27 @@
     add_gradient(lay, before, adjoint, history, state, gradient)
 
 
-def gradient_last(lay, where_ref, adjoint, history, state, before, misfit, *refs):
+def gradient_last(lay, where_ref, adjoint, history, state, before, *refs):
     sends, (gradient, plain) = refs[: lay.count_x], refs[lay.count_x :]
     add_gradient(lay, before, adjoint, history, state, gradient)
     for y in range(lay.chunk):
         for tile in range(lay.tiles):
             row = y * lay.wide + tile * ROWS
             plain[pl.ds(y * lay.wide + tile, ROWS, stride=lay.tiles), :] = gradient[row : row + ROWS, :]
-    total = STEPS * lay.count_x
     for turn, send in enumerate(sends):
         other = where_ref[0] ^ turn
         for y in range(lay.chunk):
             source = pl.ds(aligned(y * lay.wide + other * ROWS), ROWS)
             send[y * ROWS : (y + 1) * ROWS, :] = plain[source, :]
-        tile = pl.ds(aligned(other * LANES, LANES), LANES)
-        send[lay.cells : lay.cells + total, :] = misfit[0:total, tile]
 
 
 def finish(lay, slab_ref, *refs):
-    pieces, (gradient, residual) = refs[: lay.count_x], refs[lay.count_x :]
-    total = None
+    pieces, gradient = refs[: lay.count_x], refs[lay.count_x]
     for turn, piece in enumerate(pieces):
         start = (slab_ref[0] ^ turn) * lay.chunk
         for x in range(ROWS):
             target = pl.ds(aligned(x * lay.width_y + start), lay.chunk)
             gradient[target, :] = piece[pl.ds(x, lay.chunk, stride=ROWS), :]
-        part = piece[lay.cells : lay.cells + residual.shape[0], :]
-        total = part if total is None else total + part
-    residual[...] = total
 
 
 def gain_rows(lay, first_y):
@@ -683,9 +688,8 @@
         if last:
             continue
         state, send = results
-        if first:
-            send = after(send, back_pieces)
-        from_next, from_twin = swap(send, send)
+        to_twin = after(send, back_pieces) if first else send
+        from_next, from_twin = swap(send, to_twin)
     for history in histories[:-1]:
         records += call(
             part(record_phase, lay),
@@ -714,6 +718,9 @@
 
     misfit = after(misfit, [back_from_next, back_from_twin])
     misfit_next, misfit_twin = swap(misfit, misfit)
+
+    total = STEPS * count
+    twins = after(misfit[:total] + misfit_twin[:total], state)
     state, from_next, from_twin = back_state, back_from_next, back_from_twin
     gradient = None
     inject_shape = f32(DEPTH, lay.inner * lay.wide, LANES)
@@ -741,24 +748,26 @@
             sends = call(
                 part(gradient_last, lay),
                 (where,),
-                arrays + [gradient, misfit],
-                [f32(lay.cells + traces.shape[0], LANES)] * count,
+                arrays + [gradient],
+                [f32(lay.cells, LANES)] * count,
                 [pltpu.VMEM((lay.rows, LANES), jnp.float32)] * 2,
             )
             continue
         _, state, send = results
         from_next, from_twin = swap(send, send)
+        if first:
+            others = lax.ppermute(after(twins, send), axes, lay.across())
+            state = after(state, others)
+        else:
+            tile = lax.dynamic_slice_in_dim(twins + others, where[0] * LANES, LANES, axis=1)
+            residual = lax.ppermute(tile, axes, lay.home())
+            state = after(state, residual)
         kernel = gradient_first if first else gradient_later
         (gradient,) = call(
             part(kernel, lay), (), arrays + ([] if first else [gradient]), [f32(lay.rows, LANES)], cost=side_cost
         )
     pieces = [lax.ppermute(send, axes, lay.to_slabs(turn)) for turn, send in enumerate(sends)]
-    gradient, residual = call(
-        part(finish, lay),
-        (slab_int,),
-        pieces,
-        [f32(lay.width_x * lay.width_y, LANES), f32(*traces.shape)],
-    )
+    (gradient,) = call(part(finish, lay), (slab_int,), pieces, [f32(lay.width_x * lay.width_y, LANES)])
     return gradient.reshape(courant.shape), residual.reshape(observed.shape)
 
 

time: 140 us -> 148 us (1.057)
  Pallas kernels: 51.8 us -> 55.3 us
  local copies, waits for them, and re-layouts: 3.07 us -> 6.38 us
  starting transfers between devices: 59.5 us -> 56.9 us
  waiting for transfers between devices: 20.7 us -> 23.2 us
    ppermute x7, starting transfers between devices: 27.8 us -> 20.2 us  [swap(): lax.ppermute(to_twin, axes, lay.swaps(0))]
    ppermute x0 -> x2, waiting for transfers between devices: none -> 3.67 us  [the longest x1 3.67 us: local_tiles(): others = lax.ppermute(after(twins, send), axes, lay.across())]
    pallas_call x23, Pallas kernels: 51.8 us -> 55.3 us  [call(): pl.pallas_call(kernel, out_shape=tuple(outs), in_specs=[pl.BlockSpec(memo...]
    unnamed x6 -> x47, local copies, waits for them, and re-layouts: 2.64 us -> 5.94 us
    ppermute x0 -> x2, starting transfers between devices: none -> 2.49 us  [the longest x1 1.69 us: local_tiles(): others = lax.ppermute(after(twins, send), axes, lay.across())]
    ppermute x4, starting transfers between devices: 10.6 us -> 12.4 us  [local_tiles(): lax.ppermute(send, axes, lay.to_slabs(turn))]
  transfers between devices with their start and end apart: 26 -> 28, of which waited for: 5 -> 5; matrix products, arithmetic and copies ran while one was open for 2% -> 3% of each run, Pallas kernels for 21% -> 21%
where the time goes in v4:
time: 148 us; the launch traced here: 147 us
  starting transfers between devices  56.9 us (38%)
  Pallas kernels  55.3 us (37%)
  waiting for transfers between devices  23.2 us (16%)
  local copies, waits for them, and re-layouts  6.38 us (4%)
  other arithmetic  3.8 us (3%)
    pallas_call x23, Pallas kernels, call(): pl.pallas_call(kernel, out_shape=tuple(outs), in_specs=[pl.BlockSpec(memo...  55.3 us
    ppermute x7, starting transfers between devices, swap(): lax.ppermute(to_twin, axes, lay.swaps(0))  20.2 us
    ppermute x4, starting transfers between devices, local_tiles(): lax.ppermute(send, axes, lay.to_slabs(turn))  12.4 us
    ppermute x4, starting transfers between devices, local_tiles(): lax.ppermute(cut, axes, lay.to_chunks(turn))  9.33 us
    ppermute x4, waiting for transfers between devices, local_tiles(): lax.ppermute(cut, axes, lay.to_chunks(turn))  7.62 us
    ppermute x4, waiting for transfers between devices, move_adjoint(): lax.ppermute(after(back_cuts[turn], earlier), axes, lay.to_chunks(turn))  7.56 us
    ppermute x4, starting transfers between devices, move_adjoint(): lax.ppermute(after(back_cuts[turn], earlier), axes, lay.to_chunks(turn))  6.57 us
    unnamed x47, local copies, waits for them, and re-layouts  5.94 us
  transfers between devices with their start and end apart: 28, of which 5 were waited for; matrix products, arithmetic and copies ran while one was open for 3% of the time, Pallas kernels for 21%

profile of v4, /device:TPU:0, one launch (start us, length us, event | category | flops | bytes accessed | tf_op | source)
XLA Modules:
  0.0 147.0 jit_solution(5167181044437029900)
XLA Ops:
  0.6 3.1 %shard_map.113 = (f32[392,128]{1,0:T(8,128)}, f32[392,128]{1,0:T(8,128)}, f32[392,128]{1,0:T(8,128)}, f32[392,128]{1,0:T(8,128)}) custom-call(s32[1]{0:T(128)} %bitcast.slab_ref, s32[4]{0:T(128)} %bitcast.24, f32[512,128]{1,0:T(8,128)} %bitcast.19, f32[512,128]{1,0:T(8,128)} %bitcast.20, f32[512,128]{1,0:T(8,128)} %bitcast.21, s32[4,128]{1,0:T(4,128)} %bitcast.23), custom_call_target="tpu_custom_call" | custom-call | flops 1000000 | bytes 1000000 | tf_op jit(solution)/shard_map/pallas_call | solution.py:97
  5.3 4.5 %collective-permute-start.1 = (f32[392,128]{1,0:T(8,128)}, f32[392,128]{1,0:T(8,128)S(1)}, u32[]{:S(2)}, u32[]{:S(2)}) collective-permute-start(f32[392,128]{1,0:T(8,128)} %get-tuple-element.57), channel_id=1, source_target_pairs={{0,1},{1,9},{2,15},{3,7},{4,0},{5,8},{6,14},{7,6},{8,5},{9,13},{10... | collective-permute-start | bytes 602120 | tf_op jit(solution)/shard_map/ppermute | solution.py:632
  9.9 3.2 %collective-permute-start.3 = (f32[392,128]{1,0:T(8,128)}, f32[392,128]{1,0:T(8,128)S(1)}, u32[]{:S(2)}, u32[]{:S(2)}) collective-permute-start(f32[392,128]{1,0:T(8,128)} %get-tuple-element.59), channel_id=1, source_target_pairs={{0,5},{1,13},{2,11},{3,3},{4,4},{5,12},{6,10},{7,2},{8,1},{9,9},{1... | collective-permute-start | bytes 602120 | tf_op jit(solution)/shard_map/ppermute | solution.py:632
  19.3 7.6 %collective-permute-done.2.refs_2_ = f32[392,128]{1,0:T(8,128)S(1)} collective-permute-done((f32[392,128]{1,0:T(8,128)}, f32[392,128]{1,0:T(8,128)S(1)}, u32[]{:S(2)}, u32[]{:S(2)}) %collective-permute-start.2) | collective-permute-done | bytes 200736 | tf_op jit(solution)/shard_map/ppermute | solution.py:632
  27.9 2.0 %collective-permute-start.4 = (f32[1280,128]{1,0:T(8,128)S(1)}, f32[1280,128]{1,0:T(8,128)S(1)}, u32[]{:S(2)}, u32[]{:S(2)}) collective-permute-start(f32[1280,128]{1,0:T(8,128)S(1)} %get-tuple-element.69), channel_id=1, source_target_pairs={{0,1},{1,0},{4,5},{5,4},{8,9},{9,8},{12,13},{13,12},{14,15},{15,14... | collective-permute-start | bytes 1966088 | tf_op jit(solution)/shard_map/ppermute | solution.py:600
  30.7 3.3 %collective-permute-start.8 = (f32[304,128]{1,0:T(8,128)S(1)}, f32[304,128]{1,0:T(8,128)S(1)}, u32[]{:S(2)}, u32[]{:S(2)}) collective-permute-start(f32[304,128]{1,0:T(8,128)S(1)} %get-tuple-element.77), channel_id=1, source_target_pairs={{0,5},{1,13},{2,11},{3,3},{4,4},{5,12},{6,10},{7,2},{8,1},{9,9},{1... | collective-permute-start | bytes 466952 | tf_op jit(solution)/shard_map/ppermute | solution.py:650
  34.3 2.3 %collective-permute-start.6 = (f32[304,128]{1,0:T(8,128)S(1)}, f32[304,128]{1,0:T(8,128)S(1)}, u32[]{:S(2)}, u32[]{:S(2)}) collective-permute-start(f32[304,128]{1,0:T(8,128)S(1)} %get-tuple-element.73), channel_id=1, source_target_pairs={{0,1},{1,9},{2,15},{3,7},{4,0},{5,8},{6,14},{7,6},{8,5},{9,13},{10... | collective-permute-start | bytes 466952 | tf_op jit(solution)/shard_map/ppermute | solution.py:650
  37.3 4.9 %shard_map.117 = (f32[2048,128]{1,0:T(8,128)S(1)}, f32[1280,128]{1,0:T(8,128)S(1)}, f32[1280,128]{1,0:T(8,128)S(1)}, f32[768,128]{1,0:T(8,128)S(1)}) custom-call(s32[33]{0:T(128)S(1)} %pad_add_fusion.1.ints, f32[1280,128]{1,0:T(8,128)S(1)} %get-tuple-element.82.state, f32[1280,128]{1,0:T(8,128)S(1)} %collective-permute-done.11.from_next, ...), custom_call_target="tpu_custom_call" | custom-call | flops 8000000 | bytes 8000000 | tf_op jit(solution)/shard_map/pallas_call | solution.py:97
  42.9 4.3 %collective-permute-done.8.refs_3_.refs_5_ = f32[304,128]{1,0:T(8,128)S(1)} collective-permute-done((f32[304,128]{1,0:T(8,128)S(1)}, f32[304,128]{1,0:T(8,128)S(1)}, u32[]{:S(2)}, u32[]{:S(2)}) %collective-permute-start.8) | collective-permute-done | bytes 155680 | tf_op jit(solution)/shard_map/ppermute | solution.py:650
  47.1 3.3 %collective-permute-done.6.refs_1_.refs_3_ = f32[304,128]{1,0:T(8,128)S(1)} collective-permute-done((f32[304,128]{1,0:T(8,128)S(1)}, f32[304,128]{1,0:T(8,128)S(1)}, u32[]{:S(2)}, u32[]{:S(2)}) %collective-permute-start.6) | collective-permute-done | bytes 155680 | tf_op jit(solution)/shard_map/ppermute | solution.py:650
  50.4 2.0 %collective-permute-start.13 = (f32[768,128]{1,0:T(8,128)S(1)}, f32[768,128]{1,0:T(8,128)S(1)}, u32[]{:S(2)}, u32[]{:S(2)}) collective-permute-start(f32[768,128]{1,0:T(8,128)S(1)} %get-tuple-element.90), channel_id=1, source_target_pairs={{0,1},{1,0},{4,5},{5,4},{8,9},{9,8},{12,13},{13,12},{14,15},{15,14... | collective-permute-start | bytes 1179656 | tf_op jit(solution)/shard_map/ppermute | solution.py:600
  54.0 5.1 %shard_map.118 = (f32[2048,128]{1,0:T(8,128)S(1)}, f32[1280,128]{1,0:T(8,128)S(1)}, f32[768,128]{1,0:T(8,128)S(1)}) custom-call(s32[33]{0:T(128)S(1)} %pad_add_fusion.1.ints, f32[1280,128]{1,0:T(8,128)S(1)} %get-tuple-element.88.state, f32[768,128]{1,0:T(8,128)S(1)} %collective-permute-done.12.from_next, f32[768,128]{1,0:T(8,128)S(1)} %collective-permute-done.13.from_twin, ...), custom_call_target="tpu_custom_call" | custom-call | flops 8000000 | bytes 8000000 | tf_op jit(solution)/shard_map/pallas_call | solution.py:97
  59.9 6.9 %collective-permute-start.15 = (f32[768,128]{1,0:T(8,128)S(1)}, f32[768,128]{1,0:T(8,128)S(1)}, u32[]{:S(2)}, u32[]{:S(2)}) collective-permute-start(f32[768,128]{1,0:T(8,128)S(1)} %get-tuple-element.92), channel_id=1, source_target_pairs={{0,1},{1,0},{4,5},{5,4},{8,9},{9,8},{12,13},{13,12},{14,15},{15,14... | collective-permute-start | bytes 1179656 | tf_op jit(solution)/shard_map/ppermute | solution.py:600
  69.6 5.5 %shard_map.119.history = f32[2048,128]{1,0:T(8,128)S(1)} custom-call(s32[33]{0:T(128)S(1)} %pad_add_fusion.1.ints, f32[1280,128]{1,0:T(8,128)S(1)} %get-tuple-element.91.state, f32[768,128]{1,0:T(8,128)S(1)} %collective-permute-done.14.from_next, f32[768,128]{1,0:T(8,128)S(1)} %collective-permute-done.15.from_twin, ...), custom_call_target="tpu_custom_call" | custom-call | flops 8000000 | bytes 8000000 | tf_op jit(solution)/shard_map/pallas_call | solution.py:97
  75.1 2.0 %shard_map.122.misfit = f32[56,512]{1,0:T(8,128)S(1)} custom-call(s32[2]{0:T(128)S(1)} %pad_add_fusion.where_ref, f32[2048,128]{1,0:T(8,128)S(1)} %shard_map.119.history, f32[4,512]{1,0:T(4,128)S(1)} %get-tuple-element.72.codes, f32[16,512]{1,0:T(8,128)S(1)} %shard_map.120.refs_0_, f32[16,512]{1,0:T(8,128)S(1)} %shard_map.121.refs_1_, ...), custom_call_target="tpu_custom_call" | custom-call | flops 4000000 | bytes 4000000 | tf_op jit(solution)/shard_map/pallas_call | solution.py:97
  77.8 5.4 %collective-permute-start.17 = (f32[56,512]{1,0:T(8,128)S(1)}, f32[56,512]{1,0:T(8,128)S(1)}, u32[]{:S(2)}, u32[]{:S(2)}) collective-permute-start(f32[56,512]{1,0:T(8,128)S(1)} %shard_map.122.misfit), channel_id=1, source_target_pairs={{0,1},{1,0},{4,5},{5,4},{8,9},{9,8},{12,13},{13,12},{14,15},{15,14... | collective-permute-start | bytes 344072 | tf_op jit(solution)/shard_map/ppermute | solution.py:600
  87.0 4.9 %shard_map.125 = (f32[2048,128]{1,0:T(8,128)S(1)}, f32[1280,128]{1,0:T(8,128)S(1)}, f32[768,128]{1,0:T(8,128)S(1)}) custom-call(s32[2]{0:T(128)S(1)} %pad_add_fusion.where_ref, f32[1280,128]{1,0:T(8,128)S(1)} %get-tuple-element.78.state, f32[896,128]{1,0:T(8,128)S(1)} %collective-permute-done.9.from_next, f32[896,128]{1,0:T(8,128)S(1)} %collective-permute-done.10.from_twin, ...), custom_call_target="tpu_custom_call" | custom-call | flops 8000000 | bytes 8000000 | tf_op jit(solution)/shard_map/pallas_call | solution.py:97
  92.8 3.6 %collective-permute-start.20 = (f32[768,128]{1,0:T(8,128)S(1)}, f32[768,128]{1,0:T(8,128)S(1)}, u32[]{:S(2)}, u32[]{:S(2)}) collective-permute-start(f32[768,128]{1,0:T(8,128)S(1)} %get-tuple-element.98), channel_id=1, source_target_pairs={{0,1},{1,0},{4,5},{5,4},{8,9},{9,8},{12,13},{13,12},{14,15},{15,14... | collective-permute-start | bytes 1179656 | tf_op jit(solution)/shard_map/ppermute | solution.py:600
  101.9 3.7 %collective-permute-done.18 = f32[48,512]{1,0:T(8,128)S(1)} collective-permute-done((f32[48,512]{1,0:T(8,128)S(1)}, f32[48,512]{1,0:T(8,128)S(1)}, u32[]{:S(2)}, u32[]{:S(2)}) %collective-permute-start.18) | collective-permute-done | bytes 98336 | tf_op jit(solution)/shard_map/ppermute | solution.py:759
  105.6 5.9 %shard_map.128 = (f32[2048,128]{1,0:T(8,128)S(1)}, f32[1280,128]{1,0:T(8,128)S(1)}, f32[768,128]{1,0:T(8,128)}) custom-call(s32[2]{0:T(128)S(1)} %pad_add_fusion.where_ref, f32[1280,128]{1,0:T(8,128)S(1)} %get-tuple-element.100.state, f32[768,128]{1,0:T(8,128)S(1)} %collective-permute-done.19.from_next, f32[768,128]{1,0:T(8,128)S(1)} %collective-permute-done.20.from_twin, ...), custom_call_target="tpu_custom_call" | custom-call | flops 8000000 | bytes 8000000 | tf_op jit(solution)/shard_map/pallas_call | solution.py:97
  121.8 6.2 %shard_map.131.adjoint = f32[2048,128]{1,0:T(8,128)S(1)} custom-call(s32[2]{0:T(128)S(1)} %pad_add_fusion.where_ref, f32[1280,128]{1,0:T(8,128)S(1)} %copy-done.17, f32[768,128]{1,0:T(8,128)} %collective-permute-done.22.from_next, f32[768,128]{1,0:T(8,128)} %collective-permute-done.23.from_twin, f32[1280,128]{1,0:T(8,128)S(1)} %get-tuple-element.87.courant.half, ...), custom_call_target="tpu_custom_call" | custom-call | flops 8000000 | bytes 8000000 | tf_op jit(solution)/shard_map/pallas_call | solution.py:97
  129.6 5.9 %collective-permute-start.25 = (f32[128,128]{1,0:T(8,128)S(1)}, f32[128,128]{1,0:T(8,128)S(1)}, u32[]{:S(2)}, u32[]{:S(2)}) collective-permute-start(f32[128,128]{1,0:T(8,128)S(1)} %get-tuple-element.107), channel_id=1, source_target_pairs={{1,0},{9,1},{15,2},{7,3},{0,4},{8,5},{14,6},{6,7},{5,8},{13,9},{11... | collective-permute-start | bytes 196616 | tf_op jit(solution)/shard_map/ppermute | solution.py:769
  135.5 3.9 %collective-permute-start.26 = (f32[128,128]{1,0:T(8,128)S(1)}, f32[128,128]{1,0:T(8,128)S(1)}, u32[]{:S(2)}, u32[]{:S(2)}) collective-permute-start(f32[128,128]{1,0:T(8,128)S(1)} %get-tuple-element.108), channel_id=1, source_target_pairs={{4,0},{12,1},{10,2},{2,3},{5,4},{13,5},{11,6},{3,7},{0,8},{8,9},{1... | collective-permute-start | bytes 196616 | tf_op jit(solution)/shard_map/ppermute | solution.py:769
  141.3 4.3 %collective-permute-done.27.refs_3_ = f32[128,128]{1,0:T(8,128)S(1)} collective-permute-done((f32[128,128]{1,0:T(8,128)S(1)}, f32[128,128]{1,0:T(8,128)S(1)}, u32[]{:S(2)}, u32[]{:S(2)}) %collective-permute-start.27) | collective-permute-done | bytes 65568 | tf_op jit(solution)/shard_map/ppermute | solution.py:769
  (119 shorter events, 42.0 us)
Async XLA Ops:
  3.7 15.5 %collective-permute-start = (f32[392,128]{1,0:T(8,128)}, f32[392,128]{1,0:T(8,128)S(1)}, u32[]{:S(2)}, u32[]{:S(2)}) collective-permute-start(f32[392,128]{1,0:T(8,128)} %get-tuple-element.56), channel_id=1, source_target_pairs={{0,0},{1,8},{2,14},{3,6},{4,1},{5,9},{6,15},{7,7},{8,4},{9,12},{10... | collective-permute-start | bytes 602120 | tf_op jit(solution)/shard_map/ppermute | solution.py:632
  5.3 14.0 %collective-permute-start.1 = (f32[392,128]{1,0:T(8,128)}, f32[392,128]{1,0:T(8,128)S(1)}, u32[]{:S(2)}, u32[]{:S(2)}) collective-permute-start(f32[392,128]{1,0:T(8,128)} %get-tuple-element.57), channel_id=1, source_target_pairs={{0,1},{1,9},{2,15},{3,7},{4,0},{5,8},{6,14},{7,6},{8,5},{9,13},{10... | collective-permute-start | bytes 602120 | tf_op jit(solution)/shard_map/ppermute | solution.py:632
  9.9 17.1 %collective-permute-start.2 = (f32[392,128]{1,0:T(8,128)}, f32[392,128]{1,0:T(8,128)S(1)}, u32[]{:S(2)}, u32[]{:S(2)}) collective-permute-start(f32[392,128]{1,0:T(8,128)} %get-tuple-element.58), channel_id=1, source_target_pairs={{0,4},{1,12},{2,10},{3,2},{4,5},{5,13},{6,11},{7,3},{8,0},{9,8},{1... | collective-permute-start | bytes 602120 | tf_op jit(solution)/shard_map/ppermute | solution.py:632
  9.9 17.1 %collective-permute-start.3 = (f32[392,128]{1,0:T(8,128)}, f32[392,128]{1,0:T(8,128)S(1)}, u32[]{:S(2)}, u32[]{:S(2)}) collective-permute-start(f32[392,128]{1,0:T(8,128)} %get-tuple-element.59), channel_id=1, source_target_pairs={{0,5},{1,13},{2,11},{3,3},{4,4},{5,12},{6,10},{7,2},{8,1},{9,9},{1... | collective-permute-start | bytes 602120 | tf_op jit(solution)/shard_map/ppermute | solution.py:632
  27.9 8.6 %collective-permute-start.4 = (f32[1280,128]{1,0:T(8,128)S(1)}, f32[1280,128]{1,0:T(8,128)S(1)}, u32[]{:S(2)}, u32[]{:S(2)}) collective-permute-start(f32[1280,128]{1,0:T(8,128)S(1)} %get-tuple-element.69), channel_id=1, source_target_pairs={{0,1},{1,0},{4,5},{5,4},{8,9},{9,8},{12,13},{13,12},{14,15},{15,14... | collective-permute-start | bytes 1966088 | tf_op jit(solution)/shard_map/ppermute | solution.py:600
  30.0 7.3 %collective-permute-start.11 = (f32[1280,128]{1,0:T(8,128)S(1)}, f32[1280,128]{1,0:T(8,128)S(1)}, u32[]{:S(2)}, u32[]{:S(2)}) collective-permute-start(f32[1280,128]{1,0:T(8,128)S(1)} %get-tuple-element.83), channel_id=1, source_target_pairs={{1,4},{4,1},{5,8},{8,5},{9,12},{12,9},{13,14},{14,13},{15,10},{10,... | collective-permute-start | bytes 1966088 | tf_op jit(solution)/shard_map/ppermute | solution.py:599
  30.7 16.5 %collective-permute-start.8 = (f32[304,128]{1,0:T(8,128)S(1)}, f32[304,128]{1,0:T(8,128)S(1)}, u32[]{:S(2)}, u32[]{:S(2)}) collective-permute-start(f32[304,128]{1,0:T(8,128)S(1)} %get-tuple-element.77), channel_id=1, source_target_pairs={{0,5},{1,13},{2,11},{3,3},{4,4},{5,12},{6,10},{7,2},{8,1},{9,9},{1... | collective-permute-start | bytes 466952 | tf_op jit(solution)/shard_map/ppermute | solution.py:650
  33.9 13.2 %collective-permute-start.7 = (f32[304,128]{1,0:T(8,128)S(1)}, f32[304,128]{1,0:T(8,128)S(1)}, u32[]{:S(2)}, u32[]{:S(2)}) collective-permute-start(f32[304,128]{1,0:T(8,128)S(1)} %get-tuple-element.75), channel_id=1, source_target_pairs={{0,4},{1,12},{2,10},{3,2},{4,5},{5,13},{6,11},{7,3},{8,0},{9,8},{1... | collective-permute-start | bytes 466952 | tf_op jit(solution)/shard_map/ppermute | solution.py:650
  34.3 16.1 %collective-permute-start.6 = (f32[304,128]{1,0:T(8,128)S(1)}, f32[304,128]{1,0:T(8,128)S(1)}, u32[]{:S(2)}, u32[]{:S(2)}) collective-permute-start(f32[304,128]{1,0:T(8,128)S(1)} %get-tuple-element.73), channel_id=1, source_target_pairs={{0,1},{1,9},{2,15},{3,7},{4,0},{5,8},{6,14},{7,6},{8,5},{9,13},{10... | collective-permute-start | bytes 466952 | tf_op jit(solution)/shard_map/ppermute | solution.py:650
  36.6 13.8 %collective-permute-start.5 = (f32[304,128]{1,0:T(8,128)S(1)}, f32[304,128]{1,0:T(8,128)S(1)}, u32[]{:S(2)}, u32[]{:S(2)}) collective-permute-start(f32[304,128]{1,0:T(8,128)S(1)} %get-tuple-element.70), channel_id=1, source_target_pairs={{0,0},{1,8},{2,14},{3,6},{4,1},{5,9},{6,15},{7,7},{8,4},{9,12},{10... | collective-permute-start | bytes 466952 | tf_op jit(solution)/shard_map/ppermute | solution.py:650
  42.2 11.8 %collective-permute-start.12 = (f32[768,128]{1,0:T(8,128)S(1)}, f32[768,128]{1,0:T(8,128)S(1)}, u32[]{:S(2)}, u32[]{:S(2)}) collective-permute-start(f32[768,128]{1,0:T(8,128)S(1)} %get-tuple-element.90), channel_id=1, source_target_pairs={{1,4},{4,1},{5,8},{8,5},{9,12},{12,9},{13,14},{14,13},{15,10},{10,... | collective-permute-start | bytes 1179656 | tf_op jit(solution)/shard_map/ppermute | solution.py:599
  53.2 24.0 %collective-permute-start.10 = (f32[896,128]{1,0:T(8,128)S(1)}, f32[896,128]{1,0:T(8,128)S(1)}, u32[]{:S(2)}, u32[]{:S(2)}) collective-permute-start(f32[896,128]{1,0:T(8,128)S(1)} %get-tuple-element.80), channel_id=1, source_target_pairs={{0,1},{1,0},{4,5},{5,4},{8,9},{9,8},{12,13},{13,12},{14,15},{15,14... | collective-permute-start | bytes 1376264 | tf_op jit(solution)/shard_map/ppermute | solution.py:600
  53.2 23.9 %collective-permute-start.9 = (f32[896,128]{1,0:T(8,128)S(1)}, f32[896,128]{1,0:T(8,128)S(1)}, u32[]{:S(2)}, u32[]{:S(2)}) collective-permute-start(f32[896,128]{1,0:T(8,128)S(1)} %get-tuple-element.79), channel_id=1, source_target_pairs={{1,4},{4,1},{5,8},{8,5},{9,12},{12,9},{13,14},{14,13},{15,10},{10,... | collective-permute-start | bytes 1376264 | tf_op jit(solution)/shard_map/ppermute | solution.py:599
  59.0 10.5 %collective-permute-start.14 = (f32[768,128]{1,0:T(8,128)S(1)}, f32[768,128]{1,0:T(8,128)S(1)}, u32[]{:S(2)}, u32[]{:S(2)}) collective-permute-start(f32[768,128]{1,0:T(8,128)S(1)} %get-tuple-element.92), channel_id=1, source_target_pairs={{1,4},{4,1},{5,8},{8,5},{9,12},{12,9},{13,14},{14,13},{15,10},{10,... | collective-permute-start | bytes 1179656 | tf_op jit(solution)/shard_map/ppermute | solution.py:599
  59.9 9.7 %collective-permute-start.15 = (f32[768,128]{1,0:T(8,128)S(1)}, f32[768,128]{1,0:T(8,128)S(1)}, u32[]{:S(2)}, u32[]{:S(2)}) collective-permute-start(f32[768,128]{1,0:T(8,128)S(1)} %get-tuple-element.92), channel_id=1, source_target_pairs={{0,1},{1,0},{4,5},{5,4},{8,9},{9,8},{12,13},{13,12},{14,15},{15,14... | collective-permute-start | bytes 1179656 | tf_op jit(solution)/shard_map/ppermute | solution.py:600
  77.1 7.9 %collective-permute-start.16 = (f32[56,512]{1,0:T(8,128)S(1)}, f32[56,512]{1,0:T(8,128)S(1)}, u32[]{:S(2)}, u32[]{:S(2)}) collective-permute-start(f32[56,512]{1,0:T(8,128)S(1)} %shard_map.122.misfit), channel_id=1, source_target_pairs={{1,4},{4,1},{5,8},{8,5},{9,12},{12,9},{13,14},{14,13},{15,10},{10,... | collective-permute-start | bytes 344072 | tf_op jit(solution)/shard_map/ppermute | solution.py:599
  77.8 7.2 %collective-permute-start.17 = (f32[56,512]{1,0:T(8,128)S(1)}, f32[56,512]{1,0:T(8,128)S(1)}, u32[]{:S(2)}, u32[]{:S(2)}) collective-permute-start(f32[56,512]{1,0:T(8,128)S(1)} %shard_map.122.misfit), channel_id=1, source_target_pairs={{0,1},{1,0},{4,5},{5,4},{8,9},{9,8},{12,13},{13,12},{14,15},{15,14... | collective-permute-start | bytes 344072 | tf_op jit(solution)/shard_map/ppermute | solution.py:600
  91.9 13.7 %collective-permute-start.19 = (f32[768,128]{1,0:T(8,128)S(1)}, f32[768,128]{1,0:T(8,128)S(1)}, u32[]{:S(2)}, u32[]{:S(2)}) collective-permute-start(f32[768,128]{1,0:T(8,128)S(1)} %get-tuple-element.98), channel_id=1, source_target_pairs={{1,4},{4,1},{5,8},{8,5},{9,12},{12,9},{13,14},{14,13},{15,10},{10,... | collective-permute-start | bytes 1179656 | tf_op jit(solution)/shard_map/ppermute | solution.py:599
  92.8 12.8 %collective-permute-start.20 = (f32[768,128]{1,0:T(8,128)S(1)}, f32[768,128]{1,0:T(8,128)S(1)}, u32[]{:S(2)}, u32[]{:S(2)}) collective-permute-start(f32[768,128]{1,0:T(8,128)S(1)} %get-tuple-element.98), channel_id=1, source_target_pairs={{0,1},{1,0},{4,5},{5,4},{8,9},{9,8},{12,13},{13,12},{14,15},{15,14... | collective-permute-start | bytes 1179656 | tf_op jit(solution)/shard_map/ppermute | solution.py:600
  96.4 9.1 %collective-permute-start.18 = (f32[48,512]{1,0:T(8,128)S(1)}, f32[48,512]{1,0:T(8,128)S(1)}, u32[]{:S(2)}, u32[]{:S(2)}) collective-permute-start(f32[48,512]{1,0:T(8,128)S(1)} %slice_add_fusion), channel_id=1, source_target_pairs={{0,4},{1,5},{4,0},{5,1},{8,12},{9,13},{12,8},{13,9},{14,10},{15,11... | collective-permute-start | bytes 294920 | tf_op jit(solution)/shard_map/ppermute | solution.py:759
  113.3 7.7 %collective-permute-start.22 = (f32[768,128]{1,0:T(8,128)}, f32[768,128]{1,0:T(8,128)}, u32[]{:S(2)}, u32[]{:S(2)}) collective-permute-start(f32[768,128]{1,0:T(8,128)} %get-tuple-element.103), channel_id=1, source_target_pairs={{1,4},{4,1},{5,8},{8,5},{9,12},{12,9},{13,14},{14,13},{15,10},{10,... | collective-permute-start | bytes 1179656 | tf_op jit(solution)/shard_map/ppermute | solution.py:599
  114.7 6.3 %collective-permute-start.23 = (f32[768,128]{1,0:T(8,128)}, f32[768,128]{1,0:T(8,128)}, u32[]{:S(2)}, u32[]{:S(2)}) collective-permute-start(f32[768,128]{1,0:T(8,128)} %get-tuple-element.103), channel_id=1, source_target_pairs={{0,1},{1,0},{4,5},{5,4},{8,9},{9,8},{12,13},{13,12},{14,15},{15,14... | collective-permute-start | bytes 1179656 | tf_op jit(solution)/shard_map/ppermute | solution.py:600
  128.9 12.4 %collective-permute-start.24 = (f32[128,128]{1,0:T(8,128)S(1)}, f32[128,128]{1,0:T(8,128)S(1)}, u32[]{:S(2)}, u32[]{:S(2)}) collective-permute-start(f32[128,128]{1,0:T(8,128)S(1)} %get-tuple-element.106), channel_id=1, source_target_pairs={{0,0},{8,1},{14,2},{6,3},{1,4},{9,5},{15,6},{7,7},{4,8},{12,9},{10... | collective-permute-start | bytes 196616 | tf_op jit(solution)/shard_map/ppermute | solution.py:769
  129.6 11.8 %collective-permute-start.25 = (f32[128,128]{1,0:T(8,128)S(1)}, f32[128,128]{1,0:T(8,128)S(1)}, u32[]{:S(2)}, u32[]{:S(2)}) collective-permute-start(f32[128,128]{1,0:T(8,128)S(1)} %get-tuple-element.107), channel_id=1, source_target_pairs={{1,0},{9,1},{15,2},{7,3},{0,4},{8,5},{14,6},{6,7},{5,8},{13,9},{11... | collective-permute-start | bytes 196616 | tf_op jit(solution)/shard_map/ppermute | solution.py:769
  (27 other events, 205.1 us)

commit v5 on v3

--- a/solution.py
+++ b/solution.py
@@ -13,6 +13,7 @@
 DEPTH = 4
 LANES = 128
 ROWS = 8
+LAYERS = 8
 
 
 stencil = (-205.0 / 72.0, 8.0 / 5.0, -1.0 / 5.0, 8.0 / 315.0, -1.0 / 560.0)
@@ -257,9 +258,8 @@
     along_z[half : 2 * half, :] = found[:, LANES:]
 
 
-def sweep(lay, step, now, prev, following, half, gain, band, along_z, inject=None):
+def sweep(lay, step, group, now, prev, following, half, gain, band, along_z, inject=None):
     first_layer = REACH * (step + 1)
-    group = 8
     multiply_z(lay, first_layer, lay.extent - 2 * first_layer, now, band, along_z)
     row = lax.broadcasted_iota(jnp.int32, (ROWS, LANES), 0)
     top, bottom = row == 0, row == ROWS - 1
@@ -329,7 +329,7 @@
         pulse[source : source + 1, :] = scale * (half[flat, :] * gain[flat, :])
 
     for step in range(DEPTH):
-        sweep(lay, step, now, prev, following, half, gain, band, along_z)
+        sweep(lay, step, LAYERS, now, prev, following, half, gain, band, along_z)
         added = pulse[...] * drive[phase * DEPTH + step]
         places = [pl.ds(ints[1 + source], 1) for source in range(sources)]
         lines = [following[place, :] for place in places]
@@ -468,7 +468,7 @@
     fill_band(band)
     load_state(lay, where_ref[1], first, now, prev, state, from_next, from_twin)
     for step in range(DEPTH):
-        sweep(lay, step, now, prev, following, half, gain, band, along_z, inject)
+        sweep(lay, step, LAYERS, now, prev, following, half, gain, band, along_z, inject)
         keep_own(lay, step, following, history)
         now, prev, following = following, now, prev
     if not last:
@@ -683,9 +683,8 @@
         if last:
             continue
         state, send = results
-        if first:
-            send = after(send, back_pieces)
-        from_next, from_twin = swap(send, send)
+        to_twin = after(send, back_pieces) if first else send
+        from_next, from_twin = swap(send, to_twin)
     for history in histories[:-1]:
         records += call(
             part(record_phase, lay),

time: 140 us -> 135 us (0.964)
  starting transfers between devices: 59.5 us -> 55.7 us
  waiting for transfers between devices: 20.7 us -> 19.1 us
    ppermute x7, starting transfers between devices: 27.8 us -> 24.4 us  [swap(): lax.ppermute(to_twin, axes, lay.swaps(0))]
  transfers between devices with their start and end apart: 26 -> 26, of which waited for: 5 -> 5; matrix products, arithmetic and copies ran while one was open for 2% -> 2% of each run, Pallas kernels for 21% -> 22%
where the time goes in v5:
time: 135 us; the launch traced here: 134 us
  starting transfers between devices  55.7 us (41%)
  Pallas kernels  51.8 us (38%)
  waiting for transfers between devices  19.1 us (14%)
  local copies, waits for them, and re-layouts  3.07 us (2%)
  other arithmetic  2.9 us (2%)
    pallas_call x23, Pallas kernels, call(): pl.pallas_call(kernel, out_shape=tuple(outs), in_specs=[pl.BlockSpec(memo...  51.8 us
    ppermute x7, starting transfers between devices, swap(): lax.ppermute(to_twin, axes, lay.swaps(0))  24.4 us
    ppermute x4, starting transfers between devices, local_tiles(): lax.ppermute(send, axes, lay.to_slabs(turn))  10.2 us
    ppermute x4, starting transfers between devices, local_tiles(): lax.ppermute(cut, axes, lay.to_chunks(turn))  9.33 us
    ppermute x4, waiting for transfers between devices, local_tiles(): lax.ppermute(cut, axes, lay.to_chunks(turn))  7.62 us
    ppermute x4, waiting for transfers between devices, move_adjoint(): lax.ppermute(after(back_cuts[turn], earlier), axes, lay.to_chunks(turn))  7.56 us
    ppermute x4, starting transfers between devices, move_adjoint(): lax.ppermute(after(back_cuts[turn], earlier), axes, lay.to_chunks(turn))  6.57 us
    ppermute x7, starting transfers between devices, swap(): lax.ppermute(to_next, axes, lay.swaps(1))  5.19 us
  transfers between devices with their start and end apart: 26, of which 5 were waited for; matrix products, arithmetic and copies ran while one was open for 2% of the time, Pallas kernels for 22%

profile of v5, /device:TPU:0, one launch (start us, length us, event | category | flops | bytes accessed | tf_op | source)
XLA Modules:
  0.0 133.8 jit_solution(517736431641346108)
XLA Ops:
  0.6 3.1 %shard_map.113 = (f32[392,128]{1,0:T(8,128)}, f32[392,128]{1,0:T(8,128)}, f32[392,128]{1,0:T(8,128)}, f32[392,128]{1,0:T(8,128)}) custom-call(s32[1]{0:T(128)} %bitcast.slab_ref, s32[4]{0:T(128)} %bitcast.22, f32[512,128]{1,0:T(8,128)} %bitcast.18, f32[512,128]{1,0:T(8,128)} %bitcast.19, f32[512,128]{1,0:T(8,128)} %bitcast.20, s32[4,128]{1,0:T(4,128)} %bitcast.21), custom_call_target="tpu_custom_call" | custom-call | flops 1000000 | bytes 1000000 | tf_op jit(solution)/shard_map/pallas_call | solution.py:85
  5.3 4.5 %collective-permute-start.1 = (f32[392,128]{1,0:T(8,128)}, f32[392,128]{1,0:T(8,128)S(1)}, u32[]{:S(2)}, u32[]{:S(2)}) collective-permute-start(f32[392,128]{1,0:T(8,128)} %get-tuple-element.55), channel_id=1, source_target_pairs={{0,1},{1,9},{2,15},{3,7},{4,0},{5,8},{6,14},{7,6},{8,5},{9,13},{10... | collective-permute-start | bytes 602120 | tf_op jit(solution)/shard_map/ppermute | solution.py:627
  9.9 3.2 %collective-permute-start.3 = (f32[392,128]{1,0:T(8,128)}, f32[392,128]{1,0:T(8,128)S(1)}, u32[]{:S(2)}, u32[]{:S(2)}) collective-permute-start(f32[392,128]{1,0:T(8,128)} %get-tuple-element.57), channel_id=1, source_target_pairs={{0,5},{1,13},{2,11},{3,3},{4,4},{5,12},{6,10},{7,2},{8,1},{9,9},{1... | collective-permute-start | bytes 602120 | tf_op jit(solution)/shard_map/ppermute | solution.py:627
  19.3 7.6 %collective-permute-done.2.refs_2_ = f32[392,128]{1,0:T(8,128)S(1)} collective-permute-done((f32[392,128]{1,0:T(8,128)}, f32[392,128]{1,0:T(8,128)S(1)}, u32[]{:S(2)}, u32[]{:S(2)}) %collective-permute-start.2) | collective-permute-done | bytes 200736 | tf_op jit(solution)/shard_map/ppermute | solution.py:627
  27.9 2.0 %collective-permute-start.4 = (f32[1280,128]{1,0:T(8,128)S(1)}, f32[1280,128]{1,0:T(8,128)S(1)}, u32[]{:S(2)}, u32[]{:S(2)}) collective-permute-start(f32[1280,128]{1,0:T(8,128)S(1)} %get-tuple-element.67), channel_id=1, source_target_pairs={{0,1},{1,0},{4,5},{5,4},{8,9},{9,8},{12,13},{13,12},{14,15},{15,14... | collective-permute-start | bytes 1966088 | tf_op jit(solution)/shard_map/ppermute | solution.py:595
  30.7 3.3 %collective-permute-start.8 = (f32[304,128]{1,0:T(8,128)S(1)}, f32[304,128]{1,0:T(8,128)S(1)}, u32[]{:S(2)}, u32[]{:S(2)}) collective-permute-start(f32[304,128]{1,0:T(8,128)S(1)} %get-tuple-element.75), channel_id=1, source_target_pairs={{0,5},{1,13},{2,11},{3,3},{4,4},{5,12},{6,10},{7,2},{8,1},{9,9},{1... | collective-permute-start | bytes 466952 | tf_op jit(solution)/shard_map/ppermute | solution.py:645
  34.3 2.3 %collective-permute-start.6 = (f32[304,128]{1,0:T(8,128)S(1)}, f32[304,128]{1,0:T(8,128)S(1)}, u32[]{:S(2)}, u32[]{:S(2)}) collective-permute-start(f32[304,128]{1,0:T(8,128)S(1)} %get-tuple-element.71), channel_id=1, source_target_pairs={{0,1},{1,9},{2,15},{3,7},{4,0},{5,8},{6,14},{7,6},{8,5},{9,13},{10... | collective-permute-start | bytes 466952 | tf_op jit(solution)/shard_map/ppermute | solution.py:645
  37.3 4.9 %shard_map.117 = (f32[2048,128]{1,0:T(8,128)S(1)}, f32[1280,128]{1,0:T(8,128)S(1)}, f32[1280,128]{1,0:T(8,128)S(1)}, f32[768,128]{1,0:T(8,128)S(1)}) custom-call(s32[33]{0:T(128)S(1)} %pad_add_fusion.1.ints, f32[1280,128]{1,0:T(8,128)S(1)} %get-tuple-element.80.state, f32[1280,128]{1,0:T(8,128)S(1)} %collective-permute-done.11.from_next, ...), custom_call_target="tpu_custom_call" | custom-call | flops 8000000 | bytes 8000000 | tf_op jit(solution)/shard_map/pallas_call | solution.py:85
  42.8 4.3 %collective-permute-done.8.refs_3_.refs_5_ = f32[304,128]{1,0:T(8,128)S(1)} collective-permute-done((f32[304,128]{1,0:T(8,128)S(1)}, f32[304,128]{1,0:T(8,128)S(1)}, u32[]{:S(2)}, u32[]{:S(2)}) %collective-permute-start.8) | collective-permute-done | bytes 155680 | tf_op jit(solution)/shard_map/ppermute | solution.py:645
  47.1 3.3 %collective-permute-done.6.refs_1_.refs_3_ = f32[304,128]{1,0:T(8,128)S(1)} collective-permute-done((f32[304,128]{1,0:T(8,128)S(1)}, f32[304,128]{1,0:T(8,128)S(1)}, u32[]{:S(2)}, u32[]{:S(2)}) %collective-permute-start.6) | collective-permute-done | bytes 155680 | tf_op jit(solution)/shard_map/ppermute | solution.py:645
  50.4 2.0 %collective-permute-start.13 = (f32[768,128]{1,0:T(8,128)S(1)}, f32[768,128]{1,0:T(8,128)S(1)}, u32[]{:S(2)}, u32[]{:S(2)}) collective-permute-start(f32[768,128]{1,0:T(8,128)S(1)} %get-tuple-element.88), channel_id=1, source_target_pairs={{0,1},{1,0},{4,5},{5,4},{8,9},{9,8},{12,13},{13,12},{14,15},{15,14... | collective-permute-start | bytes 1179656 | tf_op jit(solution)/shard_map/ppermute | solution.py:595
  53.9 4.8 %shard_map.118 = (f32[2048,128]{1,0:T(8,128)S(1)}, f32[1280,128]{1,0:T(8,128)S(1)}, f32[768,128]{1,0:T(8,128)S(1)}) custom-call(s32[33]{0:T(128)S(1)} %pad_add_fusion.1.ints, f32[1280,128]{1,0:T(8,128)S(1)} %get-tuple-element.86.state, f32[768,128]{1,0:T(8,128)S(1)} %collective-permute-done.12.from_next, f32[768,128]{1,0:T(8,128)S(1)} %collective-permute-done.13.from_twin, ...), custom_call_target="tpu_custom_call" | custom-call | flops 8000000 | bytes 8000000 | tf_op jit(solution)/shard_map/pallas_call | solution.py:85
  59.6 6.8 %collective-permute-start.15 = (f32[768,128]{1,0:T(8,128)S(1)}, f32[768,128]{1,0:T(8,128)S(1)}, u32[]{:S(2)}, u32[]{:S(2)}) collective-permute-start(f32[768,128]{1,0:T(8,128)S(1)} %get-tuple-element.90), channel_id=1, source_target_pairs={{0,1},{1,0},{4,5},{5,4},{8,9},{9,8},{12,13},{13,12},{14,15},{15,14... | collective-permute-start | bytes 1179656 | tf_op jit(solution)/shard_map/ppermute | solution.py:595
  69.3 4.7 %shard_map.119.history = f32[2048,128]{1,0:T(8,128)S(1)} custom-call(s32[33]{0:T(128)S(1)} %pad_add_fusion.1.ints, f32[1280,128]{1,0:T(8,128)S(1)} %get-tuple-element.89.state, f32[768,128]{1,0:T(8,128)S(1)} %collective-permute-done.14.from_next, f32[768,128]{1,0:T(8,128)S(1)} %collective-permute-done.15.from_twin, ...), custom_call_target="tpu_custom_call" | custom-call | flops 8000000 | bytes 8000000 | tf_op jit(solution)/shard_map/pallas_call | solution.py:85
  76.7 5.4 %collective-permute-start.17 = (f32[56,512]{1,0:T(8,128)S(1)}, f32[56,512]{1,0:T(8,128)S(1)}, u32[]{:S(2)}, u32[]{:S(2)}) collective-permute-start(f32[56,512]{1,0:T(8,128)S(1)} %shard_map.122.misfit), channel_id=1, source_target_pairs={{0,1},{1,0},{4,5},{5,4},{8,9},{9,8},{12,13},{13,12},{14,15},{15,14... | collective-permute-start | bytes 344072 | tf_op jit(solution)/shard_map/ppermute | solution.py:595
  85.9 4.8 %shard_map.125 = (f32[2048,128]{1,0:T(8,128)S(1)}, f32[1280,128]{1,0:T(8,128)S(1)}, f32[768,128]{1,0:T(8,128)S(1)}) custom-call(s32[2]{0:T(128)S(1)} %pad_add_fusion.where_ref, f32[1280,128]{1,0:T(8,128)S(1)} %get-tuple-element.76.state, f32[896,128]{1,0:T(8,128)S(1)} %collective-permute-done.9.from_next, f32[896,128]{1,0:T(8,128)S(1)} %collective-permute-done.10.from_twin, ...), custom_call_target="tpu_custom_call" | custom-call | flops 8000000 | bytes 8000000 | tf_op jit(solution)/shard_map/pallas_call | solution.py:85
  91.6 3.6 %collective-permute-start.19 = (f32[768,128]{1,0:T(8,128)S(1)}, f32[768,128]{1,0:T(8,128)S(1)}, u32[]{:S(2)}, u32[]{:S(2)}) collective-permute-start(f32[768,128]{1,0:T(8,128)S(1)} %get-tuple-element.95), channel_id=1, source_target_pairs={{0,1},{1,0},{4,5},{5,4},{8,9},{9,8},{12,13},{13,12},{14,15},{15,14... | collective-permute-start | bytes 1179656 | tf_op jit(solution)/shard_map/ppermute | solution.py:595
  99.0 4.8 %shard_map.128 = (f32[2048,128]{1,0:T(8,128)S(1)}, f32[1280,128]{1,0:T(8,128)S(1)}, f32[768,128]{1,0:T(8,128)S(1)}) custom-call(s32[2]{0:T(128)S(1)} %pad_add_fusion.where_ref, f32[1280,128]{1,0:T(8,128)S(1)} %get-tuple-element.94.state, f32[768,128]{1,0:T(8,128)S(1)} %collective-permute-done.18.from_next, f32[768,128]{1,0:T(8,128)S(1)} %collective-permute-done.19.from_twin, ...), custom_call_target="tpu_custom_call" | custom-call | flops 8000000 | bytes 8000000 | tf_op jit(solution)/shard_map/pallas_call | solution.py:85
  104.5 4.4 %collective-permute-start.21 = (f32[768,128]{1,0:T(8,128)S(1)}, f32[768,128]{1,0:T(8,128)S(1)}, u32[]{:S(2)}, u32[]{:S(2)}) collective-permute-start(f32[768,128]{1,0:T(8,128)S(1)} %get-tuple-element.97), channel_id=1, source_target_pairs={{0,1},{1,0},{4,5},{5,4},{8,9},{9,8},{12,13},{13,12},{14,15},{15,14... | collective-permute-start | bytes 1179656 | tf_op jit(solution)/shard_map/ppermute | solution.py:595
  113.2 4.8 %shard_map.131.adjoint = f32[2048,128]{1,0:T(8,128)S(1)} custom-call(s32[2]{0:T(128)S(1)} %pad_add_fusion.where_ref, f32[1280,128]{1,0:T(8,128)S(1)} %get-tuple-element.96.state, f32[768,128]{1,0:T(8,128)S(1)} %collective-permute-done.20.from_next, f32[768,128]{1,0:T(8,128)S(1)} %collective-permute-done.21.from_twin, ...), custom_call_target="tpu_custom_call" | custom-call | flops 8000000 | bytes 8000000 | tf_op jit(solution)/shard_map/pallas_call | solution.py:85
  119.6 4.5 %collective-permute-start.23 = (f32[176,128]{1,0:T(8,128)S(1)}, f32[176,128]{1,0:T(8,128)S(1)}, u32[]{:S(2)}, u32[]{:S(2)}) collective-permute-start(f32[176,128]{1,0:T(8,128)S(1)} %get-tuple-element.101), channel_id=1, source_target_pairs={{1,0},{9,1},{15,2},{7,3},{0,4},{8,5},{14,6},{6,7},{5,8},{13,9},{11... | collective-permute-start | bytes 270344 | tf_op jit(solution)/shard_map/ppermute | solution.py:754
  124.1 2.9 %collective-permute-start.24 = (f32[176,128]{1,0:T(8,128)S(1)}, f32[176,128]{1,0:T(8,128)S(1)}, u32[]{:S(2)}, u32[]{:S(2)}) collective-permute-start(f32[176,128]{1,0:T(8,128)S(1)} %get-tuple-element.102), channel_id=1, source_target_pairs={{4,0},{12,1},{10,2},{2,3},{5,4},{13,5},{11,6},{3,7},{0,8},{8,9},{1... | collective-permute-start | bytes 270344 | tf_op jit(solution)/shard_map/ppermute | solution.py:754
  126.9 2.2 %collective-permute-start.25 = (f32[176,128]{1,0:T(8,128)S(1)}, f32[176,128]{1,0:T(8,128)S(1)}, u32[]{:S(2)}, u32[]{:S(2)}) collective-permute-start(f32[176,128]{1,0:T(8,128)S(1)} %get-tuple-element.103), channel_id=1, source_target_pairs={{5,0},{13,1},{11,2},{3,3},{4,4},{12,5},{10,6},{2,7},{1,8},{9,9},{1... | collective-permute-start | bytes 270344 | tf_op jit(solution)/shard_map/ppermute | solution.py:754
  130.8 2.2 %collective-permute-done.25.refs_3_ = f32[176,128]{1,0:T(8,128)S(1)} collective-permute-done((f32[176,128]{1,0:T(8,128)S(1)}, f32[176,128]{1,0:T(8,128)S(1)}, u32[]{:S(2)}, u32[]{:S(2)}) %collective-permute-start.25) | collective-permute-done | bytes 90144 | tf_op jit(solution)/shard_map/ppermute | solution.py:754
  (72 shorter events, 36.1 us)
Async XLA Ops:
  3.7 15.5 %collective-permute-start = (f32[392,128]{1,0:T(8,128)}, f32[392,128]{1,0:T(8,128)S(1)}, u32[]{:S(2)}, u32[]{:S(2)}) collective-permute-start(f32[392,128]{1,0:T(8,128)} %get-tuple-element.54), channel_id=1, source_target_pairs={{0,0},{1,8},{2,14},{3,6},{4,1},{5,9},{6,15},{7,7},{8,4},{9,12},{10... | collective-permute-start | bytes 602120 | tf_op jit(solution)/shard_map/ppermute | solution.py:627
  5.3 14.0 %collective-permute-start.1 = (f32[392,128]{1,0:T(8,128)}, f32[392,128]{1,0:T(8,128)S(1)}, u32[]{:S(2)}, u32[]{:S(2)}) collective-permute-start(f32[392,128]{1,0:T(8,128)} %get-tuple-element.55), channel_id=1, source_target_pairs={{0,1},{1,9},{2,15},{3,7},{4,0},{5,8},{6,14},{7,6},{8,5},{9,13},{10... | collective-permute-start | bytes 602120 | tf_op jit(solution)/shard_map/ppermute | solution.py:627
  9.9 17.1 %collective-permute-start.2 = (f32[392,128]{1,0:T(8,128)}, f32[392,128]{1,0:T(8,128)S(1)}, u32[]{:S(2)}, u32[]{:S(2)}) collective-permute-start(f32[392,128]{1,0:T(8,128)} %get-tuple-element.56), channel_id=1, source_target_pairs={{0,4},{1,12},{2,10},{3,2},{4,5},{5,13},{6,11},{7,3},{8,0},{9,8},{1... | collective-permute-start | bytes 602120 | tf_op jit(solution)/shard_map/ppermute | solution.py:627
  9.9 17.1 %collective-permute-start.3 = (f32[392,128]{1,0:T(8,128)}, f32[392,128]{1,0:T(8,128)S(1)}, u32[]{:S(2)}, u32[]{:S(2)}) collective-permute-start(f32[392,128]{1,0:T(8,128)} %get-tuple-element.57), channel_id=1, source_target_pairs={{0,5},{1,13},{2,11},{3,3},{4,4},{5,12},{6,10},{7,2},{8,1},{9,9},{1... | collective-permute-start | bytes 602120 | tf_op jit(solution)/shard_map/ppermute | solution.py:627
  27.9 8.6 %collective-permute-start.4 = (f32[1280,128]{1,0:T(8,128)S(1)}, f32[1280,128]{1,0:T(8,128)S(1)}, u32[]{:S(2)}, u32[]{:S(2)}) collective-permute-start(f32[1280,128]{1,0:T(8,128)S(1)} %get-tuple-element.67), channel_id=1, source_target_pairs={{0,1},{1,0},{4,5},{5,4},{8,9},{9,8},{12,13},{13,12},{14,15},{15,14... | collective-permute-start | bytes 1966088 | tf_op jit(solution)/shard_map/ppermute | solution.py:595
  30.0 7.3 %collective-permute-start.11 = (f32[1280,128]{1,0:T(8,128)S(1)}, f32[1280,128]{1,0:T(8,128)S(1)}, u32[]{:S(2)}, u32[]{:S(2)}) collective-permute-start(f32[1280,128]{1,0:T(8,128)S(1)} %get-tuple-element.81), channel_id=1, source_target_pairs={{1,4},{4,1},{5,8},{8,5},{9,12},{12,9},{13,14},{14,13},{15,10},{10,... | collective-permute-start | bytes 1966088 | tf_op jit(solution)/shard_map/ppermute | solution.py:594
  30.7 16.5 %collective-permute-start.8 = (f32[304,128]{1,0:T(8,128)S(1)}, f32[304,128]{1,0:T(8,128)S(1)}, u32[]{:S(2)}, u32[]{:S(2)}) collective-permute-start(f32[304,128]{1,0:T(8,128)S(1)} %get-tuple-element.75), channel_id=1, source_target_pairs={{0,5},{1,13},{2,11},{3,3},{4,4},{5,12},{6,10},{7,2},{8,1},{9,9},{1... | collective-permute-start | bytes 466952 | tf_op jit(solution)/shard_map/ppermute | solution.py:645
  33.9 13.2 %collective-permute-start.7 = (f32[304,128]{1,0:T(8,128)S(1)}, f32[304,128]{1,0:T(8,128)S(1)}, u32[]{:S(2)}, u32[]{:S(2)}) collective-permute-start(f32[304,128]{1,0:T(8,128)S(1)} %get-tuple-element.73), channel_id=1, source_target_pairs={{0,4},{1,12},{2,10},{3,2},{4,5},{5,13},{6,11},{7,3},{8,0},{9,8},{1... | collective-permute-start | bytes 466952 | tf_op jit(solution)/shard_map/ppermute | solution.py:645
  34.3 16.1 %collective-permute-start.6 = (f32[304,128]{1,0:T(8,128)S(1)}, f32[304,128]{1,0:T(8,128)S(1)}, u32[]{:S(2)}, u32[]{:S(2)}) collective-permute-start(f32[304,128]{1,0:T(8,128)S(1)} %get-tuple-element.71), channel_id=1, source_target_pairs={{0,1},{1,9},{2,15},{3,7},{4,0},{5,8},{6,14},{7,6},{8,5},{9,13},{10... | collective-permute-start | bytes 466952 | tf_op jit(solution)/shard_map/ppermute | solution.py:645
  36.6 13.8 %collective-permute-start.5 = (f32[304,128]{1,0:T(8,128)S(1)}, f32[304,128]{1,0:T(8,128)S(1)}, u32[]{:S(2)}, u32[]{:S(2)}) collective-permute-start(f32[304,128]{1,0:T(8,128)S(1)} %get-tuple-element.68), channel_id=1, source_target_pairs={{0,0},{1,8},{2,14},{3,6},{4,1},{5,9},{6,15},{7,7},{8,4},{9,12},{10... | collective-permute-start | bytes 466952 | tf_op jit(solution)/shard_map/ppermute | solution.py:645
  42.2 11.8 %collective-permute-start.12 = (f32[768,128]{1,0:T(8,128)S(1)}, f32[768,128]{1,0:T(8,128)S(1)}, u32[]{:S(2)}, u32[]{:S(2)}) collective-permute-start(f32[768,128]{1,0:T(8,128)S(1)} %get-tuple-element.88), channel_id=1, source_target_pairs={{1,4},{4,1},{5,8},{8,5},{9,12},{12,9},{13,14},{14,13},{15,10},{10,... | collective-permute-start | bytes 1179656 | tf_op jit(solution)/shard_map/ppermute | solution.py:594
  53.1 22.9 %collective-permute-start.10 = (f32[896,128]{1,0:T(8,128)S(1)}, f32[896,128]{1,0:T(8,128)S(1)}, u32[]{:S(2)}, u32[]{:S(2)}) collective-permute-start(f32[896,128]{1,0:T(8,128)S(1)} %get-tuple-element.78), channel_id=1, source_target_pairs={{0,1},{1,0},{4,5},{5,4},{8,9},{9,8},{12,13},{13,12},{14,15},{15,14... | collective-permute-start | bytes 1376264 | tf_op jit(solution)/shard_map/ppermute | solution.py:595
  53.2 22.8 %collective-permute-start.9 = (f32[896,128]{1,0:T(8,128)S(1)}, f32[896,128]{1,0:T(8,128)S(1)}, u32[]{:S(2)}, u32[]{:S(2)}) collective-permute-start(f32[896,128]{1,0:T(8,128)S(1)} %get-tuple-element.77), channel_id=1, source_target_pairs={{1,4},{4,1},{5,8},{8,5},{9,12},{12,9},{13,14},{14,13},{15,10},{10,... | collective-permute-start | bytes 1376264 | tf_op jit(solution)/shard_map/ppermute | solution.py:594
  58.7 10.5 %collective-permute-start.14 = (f32[768,128]{1,0:T(8,128)S(1)}, f32[768,128]{1,0:T(8,128)S(1)}, u32[]{:S(2)}, u32[]{:S(2)}) collective-permute-start(f32[768,128]{1,0:T(8,128)S(1)} %get-tuple-element.90), channel_id=1, source_target_pairs={{1,4},{4,1},{5,8},{8,5},{9,12},{12,9},{13,14},{14,13},{15,10},{10,... | collective-permute-start | bytes 1179656 | tf_op jit(solution)/shard_map/ppermute | solution.py:594
  59.6 9.7 %collective-permute-start.15 = (f32[768,128]{1,0:T(8,128)S(1)}, f32[768,128]{1,0:T(8,128)S(1)}, u32[]{:S(2)}, u32[]{:S(2)}) collective-permute-start(f32[768,128]{1,0:T(8,128)S(1)} %get-tuple-element.90), channel_id=1, source_target_pairs={{0,1},{1,0},{4,5},{5,4},{8,9},{9,8},{12,13},{13,12},{14,15},{15,14... | collective-permute-start | bytes 1179656 | tf_op jit(solution)/shard_map/ppermute | solution.py:595
  76.0 7.9 %collective-permute-start.16 = (f32[56,512]{1,0:T(8,128)S(1)}, f32[56,512]{1,0:T(8,128)S(1)}, u32[]{:S(2)}, u32[]{:S(2)}) collective-permute-start(f32[56,512]{1,0:T(8,128)S(1)} %shard_map.122.misfit), channel_id=1, source_target_pairs={{1,4},{4,1},{5,8},{8,5},{9,12},{12,9},{13,14},{14,13},{15,10},{10,... | collective-permute-start | bytes 344072 | tf_op jit(solution)/shard_map/ppermute | solution.py:594
  76.7 7.2 %collective-permute-start.17 = (f32[56,512]{1,0:T(8,128)S(1)}, f32[56,512]{1,0:T(8,128)S(1)}, u32[]{:S(2)}, u32[]{:S(2)}) collective-permute-start(f32[56,512]{1,0:T(8,128)S(1)} %shard_map.122.misfit), channel_id=1, source_target_pairs={{0,1},{1,0},{4,5},{5,4},{8,9},{9,8},{12,13},{13,12},{14,15},{15,14... | collective-permute-start | bytes 344072 | tf_op jit(solution)/shard_map/ppermute | solution.py:595
  90.7 8.3 %collective-permute-start.18 = (f32[768,128]{1,0:T(8,128)S(1)}, f32[768,128]{1,0:T(8,128)S(1)}, u32[]{:S(2)}, u32[]{:S(2)}) collective-permute-start(f32[768,128]{1,0:T(8,128)S(1)} %get-tuple-element.95), channel_id=1, source_target_pairs={{1,4},{4,1},{5,8},{8,5},{9,12},{12,9},{13,14},{14,13},{15,10},{10,... | collective-permute-start | bytes 1179656 | tf_op jit(solution)/shard_map/ppermute | solution.py:594
  91.6 7.4 %collective-permute-start.19 = (f32[768,128]{1,0:T(8,128)S(1)}, f32[768,128]{1,0:T(8,128)S(1)}, u32[]{:S(2)}, u32[]{:S(2)}) collective-permute-start(f32[768,128]{1,0:T(8,128)S(1)} %get-tuple-element.95), channel_id=1, source_target_pairs={{0,1},{1,0},{4,5},{5,4},{8,9},{9,8},{12,13},{13,12},{14,15},{15,14... | collective-permute-start | bytes 1179656 | tf_op jit(solution)/shard_map/ppermute | solution.py:595
  103.8 9.4 %collective-permute-start.20 = (f32[768,128]{1,0:T(8,128)S(1)}, f32[768,128]{1,0:T(8,128)S(1)}, u32[]{:S(2)}, u32[]{:S(2)}) collective-permute-start(f32[768,128]{1,0:T(8,128)S(1)} %get-tuple-element.97), channel_id=1, source_target_pairs={{1,4},{4,1},{5,8},{8,5},{9,12},{12,9},{13,14},{14,13},{15,10},{10,... | collective-permute-start | bytes 1179656 | tf_op jit(solution)/shard_map/ppermute | solution.py:594
  104.5 8.7 %collective-permute-start.21 = (f32[768,128]{1,0:T(8,128)S(1)}, f32[768,128]{1,0:T(8,128)S(1)}, u32[]{:S(2)}, u32[]{:S(2)}) collective-permute-start(f32[768,128]{1,0:T(8,128)S(1)} %get-tuple-element.97), channel_id=1, source_target_pairs={{0,1},{1,0},{4,5},{5,4},{8,9},{9,8},{12,13},{13,12},{14,15},{15,14... | collective-permute-start | bytes 1179656 | tf_op jit(solution)/shard_map/ppermute | solution.py:595
  118.9 10.2 %collective-permute-start.22 = (f32[176,128]{1,0:T(8,128)S(1)}, f32[176,128]{1,0:T(8,128)S(1)}, u32[]{:S(2)}, u32[]{:S(2)}) collective-permute-start(f32[176,128]{1,0:T(8,128)S(1)} %get-tuple-element.100), channel_id=1, source_target_pairs={{0,0},{8,1},{14,2},{6,3},{1,4},{9,5},{15,6},{7,7},{4,8},{12,9},{10... | collective-permute-start | bytes 270344 | tf_op jit(solution)/shard_map/ppermute | solution.py:754
  119.6 9.5 %collective-permute-start.23 = (f32[176,128]{1,0:T(8,128)S(1)}, f32[176,128]{1,0:T(8,128)S(1)}, u32[]{:S(2)}, u32[]{:S(2)}) collective-permute-start(f32[176,128]{1,0:T(8,128)S(1)} %get-tuple-element.101), channel_id=1, source_target_pairs={{1,0},{9,1},{15,2},{7,3},{0,4},{8,5},{14,6},{6,7},{5,8},{13,9},{11... | collective-permute-start | bytes 270344 | tf_op jit(solution)/shard_map/ppermute | solution.py:754
  124.1 6.7 %collective-permute-start.24 = (f32[176,128]{1,0:T(8,128)S(1)}, f32[176,128]{1,0:T(8,128)S(1)}, u32[]{:S(2)}, u32[]{:S(2)}) collective-permute-start(f32[176,128]{1,0:T(8,128)S(1)} %get-tuple-element.102), channel_id=1, source_target_pairs={{4,0},{12,1},{10,2},{2,3},{5,4},{13,5},{11,6},{3,7},{0,8},{8,9},{1... | collective-permute-start | bytes 270344 | tf_op jit(solution)/shard_map/ppermute | solution.py:754
  (5 other events, 12.2 us)

commit v6 on v5

--- a/solution.py
+++ b/solution.py
@@ -501,34 +501,34 @@
     add_gradient(lay, before, adjoint, history, state, gradient)
 
 
-def gradient_last(lay, where_ref, adjoint, history, state, before, misfit, *refs):
+def gradient_last(lay, where_ref, adjoint, history, state, before, *refs):
     sends, (gradient, plain) = refs[: lay.count_x], refs[lay.count_x :]
     add_gradient(lay, before, adjoint, history, state, gradient)
     for y in range(lay.chunk):
         for tile in range(lay.tiles):
             row = y * lay.wide + tile * ROWS
             plain[pl.ds(y * lay.wide + tile, ROWS, stride=lay.tiles), :] = gradient[row : row + ROWS, :]
-    total = STEPS * lay.count_x
     for turn, send in enumerate(sends):
         other = where_ref[0] ^ turn
         for y in range(lay.chunk):
             source = pl.ds(aligned(y * lay.wide + other * ROWS), ROWS)
             send[y * ROWS : (y + 1) * ROWS, :] = plain[source, :]
-        tile = pl.ds(aligned(other * LANES, LANES), LANES)
-        send[lay.cells : lay.cells + total, :] = misfit[0:total, tile]
+
+
+def place_residual(lay, strip_ref, misfit, placed):
+    total = STEPS * lay.count_x
+    placed[...] = jnp.zeros_like(placed)
+    for tile in range(lay.count_x):
+        placed[tile, strip_ref[0]] = misfit[0:total, tile * LANES : (tile + 1) * LANES]
 
 
 def finish(lay, slab_ref, *refs):
-    pieces, (gradient, residual) = refs[: lay.count_x], refs[lay.count_x :]
-    total = None
+    pieces, gradient = refs[: lay.count_x], refs[lay.count_x]
     for turn, piece in enumerate(pieces):
         start = (slab_ref[0] ^ turn) * lay.chunk
         for x in range(ROWS):
             target = pl.ds(aligned(x * lay.width_y + start), lay.chunk)
             gradient[target, :] = piece[pl.ds(x, lay.chunk, stride=ROWS), :]
-        part = piece[lay.cells : lay.cells + residual.shape[0], :]
-        total = part if total is None else total + part
-    residual[...] = total
 
 
 def gain_rows(lay, first_y):
@@ -736,12 +736,22 @@
             cost=step_cost,
         )
         arrays = [results[0], histories[phases - 1 - phase], states[phases - 1 - phase]]
+        if first:
+            (placed,) = call(
+                part(place_residual, lay),
+                ((place // count).reshape(1).astype(jnp.int32),),
+                [after(misfit, results[0])],
+                [f32(count, lay.count_y, *traces.shape)],
+            )
+            placed = placed.reshape(-1, *traces.shape)
+            residual = lax.psum_scatter(placed, axes, scatter_dimension=0, tiled=False)
         if last:
+            arrays[0] = after(arrays[0], residual)
             sends = call(
                 part(gradient_last, lay),
                 (where,),
-                arrays + [gradient, misfit],
-                [f32(lay.cells + traces.shape[0], LANES)] * count,
+                arrays + [gradient],
+                [f32(lay.cells, LANES)] * count,
                 [pltpu.VMEM((lay.rows, LANES), jnp.float32)] * 2,
             )
             continue
@@ -752,12 +762,7 @@
             part(kernel, lay), (), arrays + ([] if first else [gradient]), [f32(lay.rows, LANES)], cost=side_cost
         )
     pieces = [lax.ppermute(send, axes, lay.to_slabs(turn)) for turn, send in enumerate(sends)]
-    gradient, residual = call(
-        part(finish, lay),
-        (slab_int,),
-        pieces,
-        [f32(lay.width_x * lay.width_y, LANES), f32(*traces.shape)],
-    )
+    (gradient,) = call(part(finish, lay), (slab_int,), pieces, [f32(lay.width_x * lay.width_y, LANES)])
     return gradient.reshape(courant.shape), residual.reshape(observed.shape)
 
 

time: 135 us -> 172 us (1.27)
  waiting for transfers between devices: 19.1 us -> 39.8 us
  between operations: 1.16 us -> 14.8 us
  local copies, waits for them, and re-layouts: 3.07 us -> 5.72 us
    reduce_scatter x0 -> x1, waiting for transfers between devices: none -> 20.9 us  [local_tiles(): residual = lax.psum_scatter(placed, axes, scatter_dimension=0, tiled=False)]
    unnamed x6 -> x40, local copies, waits for them, and re-layouts: 2.64 us -> 5.29 us
    pallas_call x23 -> x24, Pallas kernels: 51.8 us -> 52.6 us  [call(): pl.pallas_call(kernel, out_shape=tuple(outs), in_specs=[pl.BlockSpec(memo...]
  transfers between devices with their start and end apart: 26 -> 27, of which waited for: 5 -> 6; matrix products, arithmetic and copies ran while one was open for 2% -> 2% of each run, Pallas kernels for 22% -> 24%
where the time goes in v6:
time: 172 us; the launch traced here: 171 us
  starting transfers between devices  55.1 us (32%)
  Pallas kernels  52.6 us (31%)
  waiting for transfers between devices  39.8 us (23%)
  between operations  14.8 us (9%)
  local copies, waits for them, and re-layouts  5.72 us (3%)
  other arithmetic  2.9 us (2%)
    pallas_call x24, Pallas kernels, call(): pl.pallas_call(kernel, out_shape=tuple(outs), in_specs=[pl.BlockSpec(memo...  52.6 us
    ppermute x7, starting transfers between devices, swap(): lax.ppermute(to_twin, axes, lay.swaps(0))  23.2 us
    reduce_scatter x1, waiting for transfers between devices, local_tiles(): residual = lax.psum_scatter(placed, axes, scatter_dimension=0, tiled=False)  20.9 us
    ppermute x4, starting transfers between devices, local_tiles(): lax.ppermute(send, axes, lay.to_slabs(turn))  10.1 us
    ppermute x4, starting transfers between devices, local_tiles(): lax.ppermute(cut, axes, lay.to_chunks(turn))  9.33 us
    ppermute x4, waiting for transfers between devices, move_adjoint(): lax.ppermute(after(back_cuts[turn], earlier), axes, lay.to_chunks(turn))  7.68 us
    ppermute x4, waiting for transfers between devices, local_tiles(): lax.ppermute(cut, axes, lay.to_chunks(turn))  7.63 us
    ppermute x4, starting transfers between devices, move_adjoint(): lax.ppermute(after(back_cuts[turn], earlier), axes, lay.to_chunks(turn))  6.57 us
  transfers between devices with their start and end apart: 27, of which 6 were waited for; matrix products, arithmetic and copies ran while one was open for 2% of the time, Pallas kernels for 24%

profile of v6, /device:TPU:0, one launch (start us, length us, event | category | flops | bytes accessed | tf_op | source)
XLA Modules:
  0.0 170.9 jit_solution(1322413482813811335)
XLA Ops:
  7.2 3.1 %shard_map.113 = (f32[392,128]{1,0:T(8,128)}, f32[392,128]{1,0:T(8,128)}, f32[392,128]{1,0:T(8,128)}, f32[392,128]{1,0:T(8,128)}) custom-call(s32[1]{0:T(128)} %bitcast.slab_ref, s32[4]{0:T(128)} %bitcast.24, f32[512,128]{1,0:T(8,128)} %bitcast.20, f32[512,128]{1,0:T(8,128)} %bitcast.21, f32[512,128]{1,0:T(8,128)} %bitcast.22, s32[4,128]{1,0:T(4,128)} %bitcast.23), custom_call_target="tpu_custom_call" | custom-call | flops 1000000 | bytes 1000000 | tf_op jit(solution)/shard_map/pallas_call | solution.py:85
  11.9 4.5 %collective-permute-start.1 = (f32[392,128]{1,0:T(8,128)}, f32[392,128]{1,0:T(8,128)S(1)}, u32[]{:S(2)}, u32[]{:S(2)}) collective-permute-start(f32[392,128]{1,0:T(8,128)} %get-tuple-element.54), channel_id=1, source_target_pairs={{0,1},{1,9},{2,15},{3,7},{4,0},{5,8},{6,14},{7,6},{8,5},{9,13},{10... | collective-permute-start | bytes 602120 | tf_op jit(solution)/shard_map/ppermute | solution.py:627
  16.4 3.2 %collective-permute-start.3 = (f32[392,128]{1,0:T(8,128)}, f32[392,128]{1,0:T(8,128)S(1)}, u32[]{:S(2)}, u32[]{:S(2)}) collective-permute-start(f32[392,128]{1,0:T(8,128)} %get-tuple-element.56), channel_id=1, source_target_pairs={{0,5},{1,13},{2,11},{3,3},{4,4},{5,12},{6,10},{7,2},{8,1},{9,9},{1... | collective-permute-start | bytes 602120 | tf_op jit(solution)/shard_map/ppermute | solution.py:627
  25.9 7.6 %collective-permute-done.2.refs_2_ = f32[392,128]{1,0:T(8,128)S(1)} collective-permute-done((f32[392,128]{1,0:T(8,128)}, f32[392,128]{1,0:T(8,128)S(1)}, u32[]{:S(2)}, u32[]{:S(2)}) %collective-permute-start.2) | collective-permute-done | bytes 200736 | tf_op jit(solution)/shard_map/ppermute | solution.py:627
  34.5 2.0 %collective-permute-start.4 = (f32[1280,128]{1,0:T(8,128)S(1)}, f32[1280,128]{1,0:T(8,128)S(1)}, u32[]{:S(2)}, u32[]{:S(2)}) collective-permute-start(f32[1280,128]{1,0:T(8,128)S(1)} %get-tuple-element.66), channel_id=1, source_target_pairs={{0,1},{1,0},{4,5},{5,4},{8,9},{9,8},{12,13},{13,12},{14,15},{15,14... | collective-permute-start | bytes 1966088 | tf_op jit(solution)/shard_map/ppermute | solution.py:595
  37.3 3.3 %collective-permute-start.8 = (f32[304,128]{1,0:T(8,128)S(1)}, f32[304,128]{1,0:T(8,128)S(1)}, u32[]{:S(2)}, u32[]{:S(2)}) collective-permute-start(f32[304,128]{1,0:T(8,128)S(1)} %get-tuple-element.74), channel_id=1, source_target_pairs={{0,5},{1,13},{2,11},{3,3},{4,4},{5,12},{6,10},{7,2},{8,1},{9,9},{1... | collective-permute-start | bytes 466952 | tf_op jit(solution)/shard_map/ppermute | solution.py:645
  40.9 2.3 %collective-permute-start.6 = (f32[304,128]{1,0:T(8,128)S(1)}, f32[304,128]{1,0:T(8,128)S(1)}, u32[]{:S(2)}, u32[]{:S(2)}) collective-permute-start(f32[304,128]{1,0:T(8,128)S(1)} %get-tuple-element.70), channel_id=1, source_target_pairs={{0,1},{1,9},{2,15},{3,7},{4,0},{5,8},{6,14},{7,6},{8,5},{9,13},{10... | collective-permute-start | bytes 466952 | tf_op jit(solution)/shard_map/ppermute | solution.py:645
  43.9 4.8 %shard_map.117 = (f32[2048,128]{1,0:T(8,128)S(1)}, f32[1280,128]{1,0:T(8,128)S(1)}, f32[1280,128]{1,0:T(8,128)S(1)}, f32[768,128]{1,0:T(8,128)S(1)}) custom-call(s32[33]{0:T(128)S(1)} %pad_add_fusion.1.ints, f32[1280,128]{1,0:T(8,128)S(1)} %get-tuple-element.79.state, f32[1280,128]{1,0:T(8,128)S(1)} %collective-permute-done.11.from_next, ...), custom_call_target="tpu_custom_call" | custom-call | flops 8000000 | bytes 8000000 | tf_op jit(solution)/shard_map/pallas_call | solution.py:85
  49.3 4.4 %collective-permute-done.8.refs_3_.refs_5_ = f32[304,128]{1,0:T(8,128)S(1)} collective-permute-done((f32[304,128]{1,0:T(8,128)S(1)}, f32[304,128]{1,0:T(8,128)S(1)}, u32[]{:S(2)}, u32[]{:S(2)}) %collective-permute-start.8) | collective-permute-done | bytes 155680 | tf_op jit(solution)/shard_map/ppermute | solution.py:645
  53.7 3.3 %collective-permute-done.6.refs_1_.refs_3_ = f32[304,128]{1,0:T(8,128)S(1)} collective-permute-done((f32[304,128]{1,0:T(8,128)S(1)}, f32[304,128]{1,0:T(8,128)S(1)}, u32[]{:S(2)}, u32[]{:S(2)}) %collective-permute-start.6) | collective-permute-done | bytes 155680 | tf_op jit(solution)/shard_map/ppermute | solution.py:645
  60.4 4.7 %shard_map.118 = (f32[2048,128]{1,0:T(8,128)S(1)}, f32[1280,128]{1,0:T(8,128)S(1)}, f32[768,128]{1,0:T(8,128)S(1)}) custom-call(s32[33]{0:T(128)S(1)} %pad_add_fusion.1.ints, f32[1280,128]{1,0:T(8,128)S(1)} %get-tuple-element.85.state, f32[768,128]{1,0:T(8,128)S(1)} %collective-permute-done.12.from_next, f32[768,128]{1,0:T(8,128)S(1)} %collective-permute-done.13.from_twin, ...), custom_call_target="tpu_custom_call" | custom-call | flops 8000000 | bytes 8000000 | tf_op jit(solution)/shard_map/pallas_call | solution.py:85
  66.0 6.9 %collective-permute-start.15 = (f32[768,128]{1,0:T(8,128)S(1)}, f32[768,128]{1,0:T(8,128)S(1)}, u32[]{:S(2)}, u32[]{:S(2)}) collective-permute-start(f32[768,128]{1,0:T(8,128)S(1)} %get-tuple-element.89), channel_id=1, source_target_pairs={{0,1},{1,0},{4,5},{5,4},{8,9},{9,8},{12,13},{13,12},{14,15},{15,14... | collective-permute-start | bytes 1179656 | tf_op jit(solution)/shard_map/ppermute | solution.py:595
  75.7 4.6 %shard_map.119.history = f32[2048,128]{1,0:T(8,128)S(1)} custom-call(s32[33]{0:T(128)S(1)} %pad_add_fusion.1.ints, f32[1280,128]{1,0:T(8,128)S(1)} %get-tuple-element.88.state, f32[768,128]{1,0:T(8,128)S(1)} %collective-permute-done.14.from_next, f32[768,128]{1,0:T(8,128)S(1)} %collective-permute-done.15.from_twin, ...), custom_call_target="tpu_custom_call" | custom-call | flops 8000000 | bytes 8000000 | tf_op jit(solution)/shard_map/pallas_call | solution.py:85
  83.0 5.4 %collective-permute-start.17 = (f32[56,512]{1,0:T(8,128)S(1)}, f32[56,512]{1,0:T(8,128)S(1)}, u32[]{:S(2)}, u32[]{:S(2)}) collective-permute-start(f32[56,512]{1,0:T(8,128)S(1)} %shard_map.122.misfit), channel_id=1, source_target_pairs={{0,1},{1,0},{4,5},{5,4},{8,9},{9,8},{12,13},{13,12},{14,15},{15,14... | collective-permute-start | bytes 344072 | tf_op jit(solution)/shard_map/ppermute | solution.py:595
  92.2 5.5 %shard_map.125 = (f32[2048,128]{1,0:T(8,128)S(1)}, f32[1280,128]{1,0:T(8,128)S(1)}, f32[768,128]{1,0:T(8,128)}) custom-call(s32[2]{0:T(128)S(1)} %pad_add_fusion.where_ref, f32[1280,128]{1,0:T(8,128)S(1)} %get-tuple-element.75.state, f32[896,128]{1,0:T(8,128)S(1)} %collective-permute-done.9.from_next, f32[896,128]{1,0:T(8,128)S(1)} %collective-permute-done.10.from_twin, ...), custom_call_target="tpu_custom_call" | custom-call | flops 8000000 | bytes 8000000 | tf_op jit(solution)/shard_map/pallas_call | solution.py:85
  100.9 3.1 %collective-permute-start.19 = (f32[768,128]{1,0:T(8,128)}, f32[768,128]{1,0:T(8,128)}, u32[]{:S(2)}, u32[]{:S(2)}) collective-permute-start(f32[768,128]{1,0:T(8,128)} %get-tuple-element.94), channel_id=1, source_target_pairs={{0,1},{1,0},{4,5},{5,4},{8,9},{9,8},{12,13},{13,12},{14,15},{15,14... | collective-permute-start | bytes 1179656 | tf_op jit(solution)/shard_map/ppermute | solution.py:595
  108.7 5.4 %shard_map.128 = (f32[2048,128]{1,0:T(8,128)S(1)}, f32[1280,128]{1,0:T(8,128)S(1)}, f32[768,128]{1,0:T(8,128)S(1)}) custom-call(s32[2]{0:T(128)S(1)} %pad_add_fusion.where_ref, f32[1280,128]{1,0:T(8,128)S(1)} %copy-done.16, f32[768,128]{1,0:T(8,128)} %collective-permute-done.18.from_next, f32[768,128]{1,0:T(8,128)} %collective-permute-done.19.from_twin, ...), custom_call_target="tpu_custom_call" | custom-call | flops 8000000 | bytes 8000000 | tf_op jit(solution)/shard_map/pallas_call | solution.py:85
  114.9 3.9 %collective-permute-start.21 = (f32[768,128]{1,0:T(8,128)S(1)}, f32[768,128]{1,0:T(8,128)S(1)}, u32[]{:S(2)}, u32[]{:S(2)}) collective-permute-start(f32[768,128]{1,0:T(8,128)S(1)} %get-tuple-element.96), channel_id=1, source_target_pairs={{0,1},{1,0},{4,5},{5,4},{8,9},{9,8},{12,13},{13,12},{14,15},{15,14... | collective-permute-start | bytes 1179656 | tf_op jit(solution)/shard_map/ppermute | solution.py:595
  123.1 4.7 %shard_map.131.adjoint = f32[2048,128]{1,0:T(8,128)S(1)} custom-call(s32[2]{0:T(128)S(1)} %pad_add_fusion.where_ref, f32[1280,128]{1,0:T(8,128)S(1)} %get-tuple-element.95.state, f32[768,128]{1,0:T(8,128)S(1)} %collective-permute-done.20.from_next, f32[768,128]{1,0:T(8,128)S(1)} %collective-permute-done.21.from_twin, ...), custom_call_target="tpu_custom_call" | custom-call | flops 8000000 | bytes 8000000 | tf_op jit(solution)/shard_map/pallas_call | solution.py:85
  129.3 4.6 %collective-permute-start.23 = (f32[128,128]{1,0:T(8,128)S(1)}, f32[128,128]{1,0:T(8,128)S(1)}, u32[]{:S(2)}, u32[]{:S(2)}) collective-permute-start(f32[128,128]{1,0:T(8,128)S(1)} %get-tuple-element.100), channel_id=1, source_target_pairs={{1,0},{9,1},{15,2},{7,3},{0,4},{8,5},{14,6},{6,7},{5,8},{13,9},{11... | collective-permute-start | bytes 196616 | tf_op jit(solution)/shard_map/ppermute | solution.py:764
  133.9 2.9 %collective-permute-start.24 = (f32[128,128]{1,0:T(8,128)S(1)}, f32[128,128]{1,0:T(8,128)S(1)}, u32[]{:S(2)}, u32[]{:S(2)}) collective-permute-start(f32[128,128]{1,0:T(8,128)S(1)} %get-tuple-element.101), channel_id=1, source_target_pairs={{4,0},{12,1},{10,2},{2,3},{5,4},{13,5},{11,6},{3,7},{0,8},{8,9},{1... | collective-permute-start | bytes 196616 | tf_op jit(solution)/shard_map/ppermute | solution.py:764
  136.8 2.0 %collective-permute-start.25 = (f32[128,128]{1,0:T(8,128)S(1)}, f32[128,128]{1,0:T(8,128)S(1)}, u32[]{:S(2)}, u32[]{:S(2)}) collective-permute-start(f32[128,128]{1,0:T(8,128)S(1)} %get-tuple-element.102), channel_id=1, source_target_pairs={{5,0},{13,1},{11,2},{3,3},{4,4},{12,5},{10,6},{2,7},{1,8},{9,9},{1... | collective-permute-start | bytes 196616 | tf_op jit(solution)/shard_map/ppermute | solution.py:764
  140.1 2.3 %collective-permute-done.25.refs_3_ = f32[128,128]{1,0:T(8,128)S(1)} collective-permute-done((f32[128,128]{1,0:T(8,128)S(1)}, f32[128,128]{1,0:T(8,128)S(1)}, u32[]{:S(2)}, u32[]{:S(2)}) %collective-permute-start.25) | collective-permute-done | bytes 65568 | tf_op jit(solution)/shard_map/ppermute | solution.py:764
  143.2 20.9 %reduce-scatter.2.cloned.1.call-done = f32[1,48,128]{2,1,0:T(8,128)} async-done(((f32[16,48,128]{2,1,0:T(8,128)}), f32[1,48,128]{2,1,0:T(8,128)}) %reduce-scatter.2.cloned.1.call-update) | async-done | bytes 24592 | tf_op jit(solution)/shard_map/reduce_scatter | solution.py:747
  (110 shorter events, 40.9 us)
Async XLA Ops:
  7.2 156.9 %reduce-scatter.2.cloned.1.call-start = ((), (), s32[]{:S(2)}) async-start(), calls=%async_computation.1 | async-start | bytes 417792 | tf_op jit(solution)/shard_map/reduce_scatter | solution.py:747
  10.3 15.5 %collective-permute-start = (f32[392,128]{1,0:T(8,128)}, f32[392,128]{1,0:T(8,128)S(1)}, u32[]{:S(2)}, u32[]{:S(2)}) collective-permute-start(f32[392,128]{1,0:T(8,128)} %get-tuple-element.53), channel_id=1, source_target_pairs={{0,0},{1,8},{2,14},{3,6},{4,1},{5,9},{6,15},{7,7},{8,4},{9,12},{10... | collective-permute-start | bytes 602120 | tf_op jit(solution)/shard_map/ppermute | solution.py:627
  11.9 14.0 %collective-permute-start.1 = (f32[392,128]{1,0:T(8,128)}, f32[392,128]{1,0:T(8,128)S(1)}, u32[]{:S(2)}, u32[]{:S(2)}) collective-permute-start(f32[392,128]{1,0:T(8,128)} %get-tuple-element.54), channel_id=1, source_target_pairs={{0,1},{1,9},{2,15},{3,7},{4,0},{5,8},{6,14},{7,6},{8,5},{9,13},{10... | collective-permute-start | bytes 602120 | tf_op jit(solution)/shard_map/ppermute | solution.py:627
  16.4 17.1 %collective-permute-start.2 = (f32[392,128]{1,0:T(8,128)}, f32[392,128]{1,0:T(8,128)S(1)}, u32[]{:S(2)}, u32[]{:S(2)}) collective-permute-start(f32[392,128]{1,0:T(8,128)} %get-tuple-element.55), channel_id=1, source_target_pairs={{0,4},{1,12},{2,10},{3,2},{4,5},{5,13},{6,11},{7,3},{8,0},{9,8},{1... | collective-permute-start | bytes 602120 | tf_op jit(solution)/shard_map/ppermute | solution.py:627
  16.4 17.1 %collective-permute-start.3 = (f32[392,128]{1,0:T(8,128)}, f32[392,128]{1,0:T(8,128)S(1)}, u32[]{:S(2)}, u32[]{:S(2)}) collective-permute-start(f32[392,128]{1,0:T(8,128)} %get-tuple-element.56), channel_id=1, source_target_pairs={{0,5},{1,13},{2,11},{3,3},{4,4},{5,12},{6,10},{7,2},{8,1},{9,9},{1... | collective-permute-start | bytes 602120 | tf_op jit(solution)/shard_map/ppermute | solution.py:627
  34.5 8.6 %collective-permute-start.4 = (f32[1280,128]{1,0:T(8,128)S(1)}, f32[1280,128]{1,0:T(8,128)S(1)}, u32[]{:S(2)}, u32[]{:S(2)}) collective-permute-start(f32[1280,128]{1,0:T(8,128)S(1)} %get-tuple-element.66), channel_id=1, source_target_pairs={{0,1},{1,0},{4,5},{5,4},{8,9},{9,8},{12,13},{13,12},{14,15},{15,14... | collective-permute-start | bytes 1966088 | tf_op jit(solution)/shard_map/ppermute | solution.py:595
  36.6 7.3 %collective-permute-start.11 = (f32[1280,128]{1,0:T(8,128)S(1)}, f32[1280,128]{1,0:T(8,128)S(1)}, u32[]{:S(2)}, u32[]{:S(2)}) collective-permute-start(f32[1280,128]{1,0:T(8,128)S(1)} %get-tuple-element.80), channel_id=1, source_target_pairs={{1,4},{4,1},{5,8},{8,5},{9,12},{12,9},{13,14},{14,13},{15,10},{10,... | collective-permute-start | bytes 1966088 | tf_op jit(solution)/shard_map/ppermute | solution.py:594
  37.3 16.5 %collective-permute-start.8 = (f32[304,128]{1,0:T(8,128)S(1)}, f32[304,128]{1,0:T(8,128)S(1)}, u32[]{:S(2)}, u32[]{:S(2)}) collective-permute-start(f32[304,128]{1,0:T(8,128)S(1)} %get-tuple-element.74), channel_id=1, source_target_pairs={{0,5},{1,13},{2,11},{3,3},{4,4},{5,12},{6,10},{7,2},{8,1},{9,9},{1... | collective-permute-start | bytes 466952 | tf_op jit(solution)/shard_map/ppermute | solution.py:645
  40.5 13.2 %collective-permute-start.7 = (f32[304,128]{1,0:T(8,128)S(1)}, f32[304,128]{1,0:T(8,128)S(1)}, u32[]{:S(2)}, u32[]{:S(2)}) collective-permute-start(f32[304,128]{1,0:T(8,128)S(1)} %get-tuple-element.72), channel_id=1, source_target_pairs={{0,4},{1,12},{2,10},{3,2},{4,5},{5,13},{6,11},{7,3},{8,0},{9,8},{1... | collective-permute-start | bytes 466952 | tf_op jit(solution)/shard_map/ppermute | solution.py:645
  40.9 16.1 %collective-permute-start.6 = (f32[304,128]{1,0:T(8,128)S(1)}, f32[304,128]{1,0:T(8,128)S(1)}, u32[]{:S(2)}, u32[]{:S(2)}) collective-permute-start(f32[304,128]{1,0:T(8,128)S(1)} %get-tuple-element.70), channel_id=1, source_target_pairs={{0,1},{1,9},{2,15},{3,7},{4,0},{5,8},{6,14},{7,6},{8,5},{9,13},{10... | collective-permute-start | bytes 466952 | tf_op jit(solution)/shard_map/ppermute | solution.py:645
  43.2 13.8 %collective-permute-start.5 = (f32[304,128]{1,0:T(8,128)S(1)}, f32[304,128]{1,0:T(8,128)S(1)}, u32[]{:S(2)}, u32[]{:S(2)}) collective-permute-start(f32[304,128]{1,0:T(8,128)S(1)} %get-tuple-element.67), channel_id=1, source_target_pairs={{0,0},{1,8},{2,14},{3,6},{4,1},{5,9},{6,15},{7,7},{8,4},{9,12},{10... | collective-permute-start | bytes 466952 | tf_op jit(solution)/shard_map/ppermute | solution.py:645
  48.6 11.8 %collective-permute-start.12 = (f32[768,128]{1,0:T(8,128)S(1)}, f32[768,128]{1,0:T(8,128)S(1)}, u32[]{:S(2)}, u32[]{:S(2)}) collective-permute-start(f32[768,128]{1,0:T(8,128)S(1)} %get-tuple-element.87), channel_id=1, source_target_pairs={{1,4},{4,1},{5,8},{8,5},{9,12},{12,9},{13,14},{14,13},{15,10},{10,... | collective-permute-start | bytes 1179656 | tf_op jit(solution)/shard_map/ppermute | solution.py:594
  59.6 22.7 %collective-permute-start.10 = (f32[896,128]{1,0:T(8,128)S(1)}, f32[896,128]{1,0:T(8,128)S(1)}, u32[]{:S(2)}, u32[]{:S(2)}) collective-permute-start(f32[896,128]{1,0:T(8,128)S(1)} %get-tuple-element.77), channel_id=1, source_target_pairs={{0,1},{1,0},{4,5},{5,4},{8,9},{9,8},{12,13},{13,12},{14,15},{15,14... | collective-permute-start | bytes 1376264 | tf_op jit(solution)/shard_map/ppermute | solution.py:595
  59.7 22.6 %collective-permute-start.9 = (f32[896,128]{1,0:T(8,128)S(1)}, f32[896,128]{1,0:T(8,128)S(1)}, u32[]{:S(2)}, u32[]{:S(2)}) collective-permute-start(f32[896,128]{1,0:T(8,128)S(1)} %get-tuple-element.76), channel_id=1, source_target_pairs={{1,4},{4,1},{5,8},{8,5},{9,12},{12,9},{13,14},{14,13},{15,10},{10,... | collective-permute-start | bytes 1376264 | tf_op jit(solution)/shard_map/ppermute | solution.py:594
  65.1 10.5 %collective-permute-start.14 = (f32[768,128]{1,0:T(8,128)S(1)}, f32[768,128]{1,0:T(8,128)S(1)}, u32[]{:S(2)}, u32[]{:S(2)}) collective-permute-start(f32[768,128]{1,0:T(8,128)S(1)} %get-tuple-element.89), channel_id=1, source_target_pairs={{1,4},{4,1},{5,8},{8,5},{9,12},{12,9},{13,14},{14,13},{15,10},{10,... | collective-permute-start | bytes 1179656 | tf_op jit(solution)/shard_map/ppermute | solution.py:594
  66.0 9.7 %collective-permute-start.15 = (f32[768,128]{1,0:T(8,128)S(1)}, f32[768,128]{1,0:T(8,128)S(1)}, u32[]{:S(2)}, u32[]{:S(2)}) collective-permute-start(f32[768,128]{1,0:T(8,128)S(1)} %get-tuple-element.89), channel_id=1, source_target_pairs={{0,1},{1,0},{4,5},{5,4},{8,9},{9,8},{12,13},{13,12},{14,15},{15,14... | collective-permute-start | bytes 1179656 | tf_op jit(solution)/shard_map/ppermute | solution.py:595
  82.3 7.9 %collective-permute-start.16 = (f32[56,512]{1,0:T(8,128)S(1)}, f32[56,512]{1,0:T(8,128)S(1)}, u32[]{:S(2)}, u32[]{:S(2)}) collective-permute-start(f32[56,512]{1,0:T(8,128)S(1)} %shard_map.122.misfit), channel_id=1, source_target_pairs={{1,4},{4,1},{5,8},{8,5},{9,12},{12,9},{13,14},{14,13},{15,10},{10,... | collective-permute-start | bytes 344072 | tf_op jit(solution)/shard_map/ppermute | solution.py:594
  83.0 7.2 %collective-permute-start.17 = (f32[56,512]{1,0:T(8,128)S(1)}, f32[56,512]{1,0:T(8,128)S(1)}, u32[]{:S(2)}, u32[]{:S(2)}) collective-permute-start(f32[56,512]{1,0:T(8,128)S(1)} %shard_map.122.misfit), channel_id=1, source_target_pairs={{0,1},{1,0},{4,5},{5,4},{8,9},{9,8},{12,13},{13,12},{14,15},{15,14... | collective-permute-start | bytes 344072 | tf_op jit(solution)/shard_map/ppermute | solution.py:595
  99.5 9.1 %collective-permute-start.18 = (f32[768,128]{1,0:T(8,128)}, f32[768,128]{1,0:T(8,128)}, u32[]{:S(2)}, u32[]{:S(2)}) collective-permute-start(f32[768,128]{1,0:T(8,128)} %get-tuple-element.94), channel_id=1, source_target_pairs={{1,4},{4,1},{5,8},{8,5},{9,12},{12,9},{13,14},{14,13},{15,10},{10,... | collective-permute-start | bytes 1179656 | tf_op jit(solution)/shard_map/ppermute | solution.py:594
  100.9 7.7 %collective-permute-start.19 = (f32[768,128]{1,0:T(8,128)}, f32[768,128]{1,0:T(8,128)}, u32[]{:S(2)}, u32[]{:S(2)}) collective-permute-start(f32[768,128]{1,0:T(8,128)} %get-tuple-element.94), channel_id=1, source_target_pairs={{0,1},{1,0},{4,5},{5,4},{8,9},{9,8},{12,13},{13,12},{14,15},{15,14... | collective-permute-start | bytes 1179656 | tf_op jit(solution)/shard_map/ppermute | solution.py:595
  114.1 9.0 %collective-permute-start.20 = (f32[768,128]{1,0:T(8,128)S(1)}, f32[768,128]{1,0:T(8,128)S(1)}, u32[]{:S(2)}, u32[]{:S(2)}) collective-permute-start(f32[768,128]{1,0:T(8,128)S(1)} %get-tuple-element.96), channel_id=1, source_target_pairs={{1,4},{4,1},{5,8},{8,5},{9,12},{12,9},{13,14},{14,13},{15,10},{10,... | collective-permute-start | bytes 1179656 | tf_op jit(solution)/shard_map/ppermute | solution.py:594
  114.9 8.2 %collective-permute-start.21 = (f32[768,128]{1,0:T(8,128)S(1)}, f32[768,128]{1,0:T(8,128)S(1)}, u32[]{:S(2)}, u32[]{:S(2)}) collective-permute-start(f32[768,128]{1,0:T(8,128)S(1)} %get-tuple-element.96), channel_id=1, source_target_pairs={{0,1},{1,0},{4,5},{5,4},{8,9},{9,8},{12,13},{13,12},{14,15},{15,14... | collective-permute-start | bytes 1179656 | tf_op jit(solution)/shard_map/ppermute | solution.py:595
  128.7 10.2 %collective-permute-start.22 = (f32[128,128]{1,0:T(8,128)S(1)}, f32[128,128]{1,0:T(8,128)S(1)}, u32[]{:S(2)}, u32[]{:S(2)}) collective-permute-start(f32[128,128]{1,0:T(8,128)S(1)} %get-tuple-element.99), channel_id=1, source_target_pairs={{0,0},{8,1},{14,2},{6,3},{1,4},{9,5},{15,6},{7,7},{4,8},{12,9},{10... | collective-permute-start | bytes 196616 | tf_op jit(solution)/shard_map/ppermute | solution.py:764
  129.3 9.5 %collective-permute-start.23 = (f32[128,128]{1,0:T(8,128)S(1)}, f32[128,128]{1,0:T(8,128)S(1)}, u32[]{:S(2)}, u32[]{:S(2)}) collective-permute-start(f32[128,128]{1,0:T(8,128)S(1)} %get-tuple-element.100), channel_id=1, source_target_pairs={{1,0},{9,1},{15,2},{7,3},{0,4},{8,5},{14,6},{6,7},{5,8},{13,9},{11... | collective-permute-start | bytes 196616 | tf_op jit(solution)/shard_map/ppermute | solution.py:764
  (23 other events, 139.7 us)
Sparse Core Ops, SparseCore 0:
  105.0 59.0 reduce-scatter.1

commit v7 on v5

--- a/solution.py
+++ b/solution.py
@@ -99,12 +99,11 @@
     return pl.multiple_of(value, to)
 
 
-def cut_chunk(lay, slab, turn, fields, target):
+def cut_field(lay, slab, turn, index, field, target):
     start = (slab ^ turn) * lay.chunk
-    for index, field in enumerate(fields):
-        for y in range(lay.chunk):
-            row = (index * lay.chunk + y) * ROWS
-            target[row : row + ROWS, :] = field[pl.ds(start + y, ROWS, stride=lay.width_y), :]
+    for y in range(lay.chunk):
+        row = (index * lay.chunk + y) * ROWS
+        target[row : row + ROWS, :] = field[pl.ds(start + y, ROWS, stride=lay.width_y), :]
 
 
 def cut_forward(lay, slab_ref, count_ref, *refs):
@@ -116,15 +115,17 @@
     ]
     for copy in copies:
         copy.start()
-    for copy in copies:
+    for index, (copy, field) in enumerate(zip(copies, fields)):
         copy.wait()
+        for turn, send in enumerate(sends):
+            cut_field(lay, slab_ref[0], turn, index, field, send)
+    copies[-1].wait()
     slots = lax.broadcasted_iota(jnp.int32, (1, LANES), 1)
     used = []
     for tile in range(lay.count_x):
         cell = jnp.where(slots < count_ref[tile], held_cell[tile : tile + 1, :], -1)
         used.append(cell.astype(jnp.float32))
-    for turn, send in enumerate(sends):
-        cut_chunk(lay, slab_ref[0], turn, fields, send)
+    for send in sends:
         for tile in range(lay.count_x):
             row = 3 * lay.cells + tile
             send[row : row + 1, :] = used[tile]
@@ -132,7 +133,8 @@
 
 def cut_adjoint(lay, slab_ref, now, prev, observed, *sends):
     for turn, send in enumerate(sends):
-        cut_chunk(lay, slab_ref[0], turn, (now, prev), send)
+        for index, field in enumerate((now, prev)):
+            cut_field(lay, slab_ref[0], turn, index, field, send)
         row = 2 * lay.cells
         send[row : row + observed.shape[0], :] = observed[...]
 
@@ -475,7 +477,7 @@
         store_state(lay, now, prev, state_out, send)
 
 
-def add_gradient(lay, before, adjoint, history, state, gradient):
+def add_gradient(lay, before, adjoint, history, state, gradient, natural=False):
     def layer(y, carry):
         place = aligned(y * lay.wide)
         own = pl.ds(place, lay.wide)
@@ -487,7 +489,12 @@
             accel = (fields[index + 2] - fields[index + 1]) - (fields[index + 1] - fields[index])
             term = adjoint[pl.ds(aligned(place + step * lay.rows), lay.wide), :] * accel
             total = term if total is None else total + term
-        gradient[own, :] = total
+        if natural:
+            for tile in range(lay.tiles):
+                rows = pl.ds(place + tile, ROWS, stride=lay.tiles)
+                gradient[rows, :] = total[tile * ROWS : (tile + 1) * ROWS, :]
+        else:
+            gradient[own, :] = total
         return carry
 
     lax.fori_loop(0, lay.chunk, layer, 0)
@@ -502,12 +509,8 @@
 
 
 def gradient_last(lay, where_ref, adjoint, history, state, before, misfit, *refs):
-    sends, (gradient, plain) = refs[: lay.count_x], refs[lay.count_x :]
-    add_gradient(lay, before, adjoint, history, state, gradient)
-    for y in range(lay.chunk):
-        for tile in range(lay.tiles):
-            row = y * lay.wide + tile * ROWS
-            plain[pl.ds(y * lay.wide + tile, ROWS, stride=lay.tiles), :] = gradient[row : row + ROWS, :]
+    sends, plain = refs[: lay.count_x], refs[lay.count_x]
+    add_gradient(lay, before, adjoint, history, state, plain, natural=True)
     total = STEPS * lay.count_x
     for turn, send in enumerate(sends):
         other = where_ref[0] ^ turn
@@ -742,7 +745,7 @@
                 (where,),
                 arrays + [gradient, misfit],
                 [f32(lay.cells + traces.shape[0], LANES)] * count,
-                [pltpu.VMEM((lay.rows, LANES), jnp.float32)] * 2,
+                [pltpu.VMEM((lay.rows, LANES), jnp.float32)],
             )
             continue
         _, state, send = results

time: 135 us -> 135 us (level)
  no operation moved by 1% of the time
where the time goes in v7:
time: 135 us; the launch traced here: 134 us
  starting transfers between devices  55.7 us (41%)
  Pallas kernels  51.7 us (38%)
  waiting for transfers between devices  19.1 us (14%)
  local copies, waits for them, and re-layouts  3.07 us (2%)
  other arithmetic  2.9 us (2%)
    pallas_call x23, Pallas kernels, call(): pl.pallas_call(kernel, out_shape=tuple(outs), in_specs=[pl.BlockSpec(memo...  51.7 us
    ppermute x7, starting transfers between devices, swap(): lax.ppermute(to_twin, axes, lay.swaps(0))  24.4 us
    ppermute x4, starting transfers between devices, local_tiles(): lax.ppermute(send, axes, lay.to_slabs(turn))  10.2 us
    ppermute x4, starting transfers between devices, local_tiles(): lax.ppermute(cut, axes, lay.to_chunks(turn))  9.33 us
    ppermute x4, waiting for transfers between devices, local_tiles(): lax.ppermute(cut, axes, lay.to_chunks(turn))  7.62 us
    ppermute x4, waiting for transfers between devices, move_adjoint(): lax.ppermute(after(back_cuts[turn], earlier), axes, lay.to_chunks(turn))  7.56 us
    ppermute x4, starting transfers between devices, move_adjoint(): lax.ppermute(after(back_cuts[turn], earlier), axes, lay.to_chunks(turn))  6.57 us
    ppermute x7, starting transfers between devices, swap(): lax.ppermute(to_next, axes, lay.swaps(1))  5.19 us
  transfers between devices with their start and end apart: 26, of which 5 were waited for; matrix products, arithmetic and copies ran while one was open for 2% of the time, Pallas kernels for 22%

profile of v7, /device:TPU:0, one launch (start us, length us, event | category | flops | bytes accessed | tf_op | source)
XLA Modules:
  0.0 133.7 jit_solution(16927560160550367119)
XLA Ops:
  0.6 3.0 %shard_map.113 = (f32[392,128]{1,0:T(8,128)}, f32[392,128]{1,0:T(8,128)}, f32[392,128]{1,0:T(8,128)}, f32[392,128]{1,0:T(8,128)}) custom-call(s32[1]{0:T(128)} %bitcast.slab_ref, s32[4]{0:T(128)} %bitcast.22, f32[512,128]{1,0:T(8,128)} %bitcast.18, f32[512,128]{1,0:T(8,128)} %bitcast.19, f32[512,128]{1,0:T(8,128)} %bitcast.20, s32[4,128]{1,0:T(4,128)} %bitcast.21), custom_call_target="tpu_custom_call" | custom-call | flops 1000000 | bytes 1000000 | tf_op jit(solution)/shard_map/pallas_call | solution.py:85
  5.2 4.5 %collective-permute-start.1 = (f32[392,128]{1,0:T(8,128)}, f32[392,128]{1,0:T(8,128)S(1)}, u32[]{:S(2)}, u32[]{:S(2)}) collective-permute-start(f32[392,128]{1,0:T(8,128)} %get-tuple-element.55), channel_id=1, source_target_pairs={{0,1},{1,9},{2,15},{3,7},{4,0},{5,8},{6,14},{7,6},{8,5},{9,13},{10... | collective-permute-start | bytes 602120 | tf_op jit(solution)/shard_map/ppermute | solution.py:630
  9.8 3.2 %collective-permute-start.3 = (f32[392,128]{1,0:T(8,128)}, f32[392,128]{1,0:T(8,128)S(1)}, u32[]{:S(2)}, u32[]{:S(2)}) collective-permute-start(f32[392,128]{1,0:T(8,128)} %get-tuple-element.57), channel_id=1, source_target_pairs={{0,5},{1,13},{2,11},{3,3},{4,4},{5,12},{6,10},{7,2},{8,1},{9,9},{1... | collective-permute-start | bytes 602120 | tf_op jit(solution)/shard_map/ppermute | solution.py:630
  19.2 7.6 %collective-permute-done.2.refs_2_ = f32[392,128]{1,0:T(8,128)S(1)} collective-permute-done((f32[392,128]{1,0:T(8,128)}, f32[392,128]{1,0:T(8,128)S(1)}, u32[]{:S(2)}, u32[]{:S(2)}) %collective-permute-start.2) | collective-permute-done | bytes 200736 | tf_op jit(solution)/shard_map/ppermute | solution.py:630
  27.9 2.0 %collective-permute-start.4 = (f32[1280,128]{1,0:T(8,128)S(1)}, f32[1280,128]{1,0:T(8,128)S(1)}, u32[]{:S(2)}, u32[]{:S(2)}) collective-permute-start(f32[1280,128]{1,0:T(8,128)S(1)} %get-tuple-element.67), channel_id=1, source_target_pairs={{0,1},{1,0},{4,5},{5,4},{8,9},{9,8},{12,13},{13,12},{14,15},{15,14... | collective-permute-start | bytes 1966088 | tf_op jit(solution)/shard_map/ppermute | solution.py:598
  30.6 3.3 %collective-permute-start.8 = (f32[304,128]{1,0:T(8,128)S(1)}, f32[304,128]{1,0:T(8,128)S(1)}, u32[]{:S(2)}, u32[]{:S(2)}) collective-permute-start(f32[304,128]{1,0:T(8,128)S(1)} %get-tuple-element.75), channel_id=1, source_target_pairs={{0,5},{1,13},{2,11},{3,3},{4,4},{5,12},{6,10},{7,2},{8,1},{9,9},{1... | collective-permute-start | bytes 466952 | tf_op jit(solution)/shard_map/ppermute | solution.py:648
  34.2 2.3 %collective-permute-start.6 = (f32[304,128]{1,0:T(8,128)S(1)}, f32[304,128]{1,0:T(8,128)S(1)}, u32[]{:S(2)}, u32[]{:S(2)}) collective-permute-start(f32[304,128]{1,0:T(8,128)S(1)} %get-tuple-element.71), channel_id=1, source_target_pairs={{0,1},{1,9},{2,15},{3,7},{4,0},{5,8},{6,14},{7,6},{8,5},{9,13},{10... | collective-permute-start | bytes 466952 | tf_op jit(solution)/shard_map/ppermute | solution.py:648
  37.2 4.9 %shard_map.117 = (f32[2048,128]{1,0:T(8,128)S(1)}, f32[1280,128]{1,0:T(8,128)S(1)}, f32[1280,128]{1,0:T(8,128)S(1)}, f32[768,128]{1,0:T(8,128)S(1)}) custom-call(s32[33]{0:T(128)S(1)} %pad_add_fusion.1.ints, f32[1280,128]{1,0:T(8,128)S(1)} %get-tuple-element.80.state, f32[1280,128]{1,0:T(8,128)S(1)} %collective-permute-done.11.from_next, ...), custom_call_target="tpu_custom_call" | custom-call | flops 8000000 | bytes 8000000 | tf_op jit(solution)/shard_map/pallas_call | solution.py:85
  42.8 4.3 %collective-permute-done.8.refs_3_.refs_5_ = f32[304,128]{1,0:T(8,128)S(1)} collective-permute-done((f32[304,128]{1,0:T(8,128)S(1)}, f32[304,128]{1,0:T(8,128)S(1)}, u32[]{:S(2)}, u32[]{:S(2)}) %collective-permute-start.8) | collective-permute-done | bytes 155680 | tf_op jit(solution)/shard_map/ppermute | solution.py:648
  47.1 3.3 %collective-permute-done.6.refs_1_.refs_3_ = f32[304,128]{1,0:T(8,128)S(1)} collective-permute-done((f32[304,128]{1,0:T(8,128)S(1)}, f32[304,128]{1,0:T(8,128)S(1)}, u32[]{:S(2)}, u32[]{:S(2)}) %collective-permute-start.6) | collective-permute-done | bytes 155680 | tf_op jit(solution)/shard_map/ppermute | solution.py:648
  50.3 2.0 %collective-permute-start.13 = (f32[768,128]{1,0:T(8,128)S(1)}, f32[768,128]{1,0:T(8,128)S(1)}, u32[]{:S(2)}, u32[]{:S(2)}) collective-permute-start(f32[768,128]{1,0:T(8,128)S(1)} %get-tuple-element.88), channel_id=1, source_target_pairs={{0,1},{1,0},{4,5},{5,4},{8,9},{9,8},{12,13},{13,12},{14,15},{15,14... | collective-permute-start | bytes 1179656 | tf_op jit(solution)/shard_map/ppermute | solution.py:598
  53.9 4.8 %shard_map.118 = (f32[2048,128]{1,0:T(8,128)S(1)}, f32[1280,128]{1,0:T(8,128)S(1)}, f32[768,128]{1,0:T(8,128)S(1)}) custom-call(s32[33]{0:T(128)S(1)} %pad_add_fusion.1.ints, f32[1280,128]{1,0:T(8,128)S(1)} %get-tuple-element.86.state, f32[768,128]{1,0:T(8,128)S(1)} %collective-permute-done.12.from_next, f32[768,128]{1,0:T(8,128)S(1)} %collective-permute-done.13.from_twin, ...), custom_call_target="tpu_custom_call" | custom-call | flops 8000000 | bytes 8000000 | tf_op jit(solution)/shard_map/pallas_call | solution.py:85
  59.5 6.8 %collective-permute-start.15 = (f32[768,128]{1,0:T(8,128)S(1)}, f32[768,128]{1,0:T(8,128)S(1)}, u32[]{:S(2)}, u32[]{:S(2)}) collective-permute-start(f32[768,128]{1,0:T(8,128)S(1)} %get-tuple-element.90), channel_id=1, source_target_pairs={{0,1},{1,0},{4,5},{5,4},{8,9},{9,8},{12,13},{13,12},{14,15},{15,14... | collective-permute-start | bytes 1179656 | tf_op jit(solution)/shard_map/ppermute | solution.py:598
  69.2 4.7 %shard_map.119.history = f32[2048,128]{1,0:T(8,128)S(1)} custom-call(s32[33]{0:T(128)S(1)} %pad_add_fusion.1.ints, f32[1280,128]{1,0:T(8,128)S(1)} %get-tuple-element.89.state, f32[768,128]{1,0:T(8,128)S(1)} %collective-permute-done.14.from_next, f32[768,128]{1,0:T(8,128)S(1)} %collective-permute-done.15.from_twin, ...), custom_call_target="tpu_custom_call" | custom-call | flops 8000000 | bytes 8000000 | tf_op jit(solution)/shard_map/pallas_call | solution.py:85
  76.6 5.4 %collective-permute-start.17 = (f32[56,512]{1,0:T(8,128)S(1)}, f32[56,512]{1,0:T(8,128)S(1)}, u32[]{:S(2)}, u32[]{:S(2)}) collective-permute-start(f32[56,512]{1,0:T(8,128)S(1)} %shard_map.122.misfit), channel_id=1, source_target_pairs={{0,1},{1,0},{4,5},{5,4},{8,9},{9,8},{12,13},{13,12},{14,15},{15,14... | collective-permute-start | bytes 344072 | tf_op jit(solution)/shard_map/ppermute | solution.py:598
  85.8 4.8 %shard_map.125 = (f32[2048,128]{1,0:T(8,128)S(1)}, f32[1280,128]{1,0:T(8,128)S(1)}, f32[768,128]{1,0:T(8,128)S(1)}) custom-call(s32[2]{0:T(128)S(1)} %pad_add_fusion.where_ref, f32[1280,128]{1,0:T(8,128)S(1)} %get-tuple-element.76.state, f32[896,128]{1,0:T(8,128)S(1)} %collective-permute-done.9.from_next, f32[896,128]{1,0:T(8,128)S(1)} %collective-permute-done.10.from_twin, ...), custom_call_target="tpu_custom_call" | custom-call | flops 8000000 | bytes 8000000 | tf_op jit(solution)/shard_map/pallas_call | solution.py:85
  91.6 3.6 %collective-permute-start.19 = (f32[768,128]{1,0:T(8,128)S(1)}, f32[768,128]{1,0:T(8,128)S(1)}, u32[]{:S(2)}, u32[]{:S(2)}) collective-permute-start(f32[768,128]{1,0:T(8,128)S(1)} %get-tuple-element.95), channel_id=1, source_target_pairs={{0,1},{1,0},{4,5},{5,4},{8,9},{9,8},{12,13},{13,12},{14,15},{15,14... | collective-permute-start | bytes 1179656 | tf_op jit(solution)/shard_map/ppermute | solution.py:598
  98.9 4.8 %shard_map.128 = (f32[2048,128]{1,0:T(8,128)S(1)}, f32[1280,128]{1,0:T(8,128)S(1)}, f32[768,128]{1,0:T(8,128)S(1)}) custom-call(s32[2]{0:T(128)S(1)} %pad_add_fusion.where_ref, f32[1280,128]{1,0:T(8,128)S(1)} %get-tuple-element.94.state, f32[768,128]{1,0:T(8,128)S(1)} %collective-permute-done.18.from_next, f32[768,128]{1,0:T(8,128)S(1)} %collective-permute-done.19.from_twin, ...), custom_call_target="tpu_custom_call" | custom-call | flops 8000000 | bytes 8000000 | tf_op jit(solution)/shard_map/pallas_call | solution.py:85
  104.5 4.4 %collective-permute-start.21 = (f32[768,128]{1,0:T(8,128)S(1)}, f32[768,128]{1,0:T(8,128)S(1)}, u32[]{:S(2)}, u32[]{:S(2)}) collective-permute-start(f32[768,128]{1,0:T(8,128)S(1)} %get-tuple-element.97), channel_id=1, source_target_pairs={{0,1},{1,0},{4,5},{5,4},{8,9},{9,8},{12,13},{13,12},{14,15},{15,14... | collective-permute-start | bytes 1179656 | tf_op jit(solution)/shard_map/ppermute | solution.py:598
  113.2 4.8 %shard_map.131.adjoint = f32[2048,128]{1,0:T(8,128)S(1)} custom-call(s32[2]{0:T(128)S(1)} %pad_add_fusion.where_ref, f32[1280,128]{1,0:T(8,128)S(1)} %get-tuple-element.96.state, f32[768,128]{1,0:T(8,128)S(1)} %collective-permute-done.20.from_next, f32[768,128]{1,0:T(8,128)S(1)} %collective-permute-done.21.from_twin, ...), custom_call_target="tpu_custom_call" | custom-call | flops 8000000 | bytes 8000000 | tf_op jit(solution)/shard_map/pallas_call | solution.py:85
  119.5 4.5 %collective-permute-start.23 = (f32[176,128]{1,0:T(8,128)S(1)}, f32[176,128]{1,0:T(8,128)S(1)}, u32[]{:S(2)}, u32[]{:S(2)}) collective-permute-start(f32[176,128]{1,0:T(8,128)S(1)} %get-tuple-element.101), channel_id=1, source_target_pairs={{1,0},{9,1},{15,2},{7,3},{0,4},{8,5},{14,6},{6,7},{5,8},{13,9},{11... | collective-permute-start | bytes 270344 | tf_op jit(solution)/shard_map/ppermute | solution.py:757
  124.0 2.9 %collective-permute-start.24 = (f32[176,128]{1,0:T(8,128)S(1)}, f32[176,128]{1,0:T(8,128)S(1)}, u32[]{:S(2)}, u32[]{:S(2)}) collective-permute-start(f32[176,128]{1,0:T(8,128)S(1)} %get-tuple-element.102), channel_id=1, source_target_pairs={{4,0},{12,1},{10,2},{2,3},{5,4},{13,5},{11,6},{3,7},{0,8},{8,9},{1... | collective-permute-start | bytes 270344 | tf_op jit(solution)/shard_map/ppermute | solution.py:757
  126.8 2.2 %collective-permute-start.25 = (f32[176,128]{1,0:T(8,128)S(1)}, f32[176,128]{1,0:T(8,128)S(1)}, u32[]{:S(2)}, u32[]{:S(2)}) collective-permute-start(f32[176,128]{1,0:T(8,128)S(1)} %get-tuple-element.103), channel_id=1, source_target_pairs={{5,0},{13,1},{11,2},{3,3},{4,4},{12,5},{10,6},{2,7},{1,8},{9,9},{1... | collective-permute-start | bytes 270344 | tf_op jit(solution)/shard_map/ppermute | solution.py:757
  130.7 2.2 %collective-permute-done.25.refs_3_ = f32[176,128]{1,0:T(8,128)S(1)} collective-permute-done((f32[176,128]{1,0:T(8,128)S(1)}, f32[176,128]{1,0:T(8,128)S(1)}, u32[]{:S(2)}, u32[]{:S(2)}) %collective-permute-start.25) | collective-permute-done | bytes 90144 | tf_op jit(solution)/shard_map/ppermute | solution.py:757
  (72 shorter events, 36.1 us)
Async XLA Ops:
  3.7 15.5 %collective-permute-start = (f32[392,128]{1,0:T(8,128)}, f32[392,128]{1,0:T(8,128)S(1)}, u32[]{:S(2)}, u32[]{:S(2)}) collective-permute-start(f32[392,128]{1,0:T(8,128)} %get-tuple-element.54), channel_id=1, source_target_pairs={{0,0},{1,8},{2,14},{3,6},{4,1},{5,9},{6,15},{7,7},{8,4},{9,12},{10... | collective-permute-start | bytes 602120 | tf_op jit(solution)/shard_map/ppermute | solution.py:630
  5.2 14.0 %collective-permute-start.1 = (f32[392,128]{1,0:T(8,128)}, f32[392,128]{1,0:T(8,128)S(1)}, u32[]{:S(2)}, u32[]{:S(2)}) collective-permute-start(f32[392,128]{1,0:T(8,128)} %get-tuple-element.55), channel_id=1, source_target_pairs={{0,1},{1,9},{2,15},{3,7},{4,0},{5,8},{6,14},{7,6},{8,5},{9,13},{10... | collective-permute-start | bytes 602120 | tf_op jit(solution)/shard_map/ppermute | solution.py:630
  9.8 17.1 %collective-permute-start.2 = (f32[392,128]{1,0:T(8,128)}, f32[392,128]{1,0:T(8,128)S(1)}, u32[]{:S(2)}, u32[]{:S(2)}) collective-permute-start(f32[392,128]{1,0:T(8,128)} %get-tuple-element.56), channel_id=1, source_target_pairs={{0,4},{1,12},{2,10},{3,2},{4,5},{5,13},{6,11},{7,3},{8,0},{9,8},{1... | collective-permute-start | bytes 602120 | tf_op jit(solution)/shard_map/ppermute | solution.py:630
  9.8 17.1 %collective-permute-start.3 = (f32[392,128]{1,0:T(8,128)}, f32[392,128]{1,0:T(8,128)S(1)}, u32[]{:S(2)}, u32[]{:S(2)}) collective-permute-start(f32[392,128]{1,0:T(8,128)} %get-tuple-element.57), channel_id=1, source_target_pairs={{0,5},{1,13},{2,11},{3,3},{4,4},{5,12},{6,10},{7,2},{8,1},{9,9},{1... | collective-permute-start | bytes 602120 | tf_op jit(solution)/shard_map/ppermute | solution.py:630
  27.9 8.6 %collective-permute-start.4 = (f32[1280,128]{1,0:T(8,128)S(1)}, f32[1280,128]{1,0:T(8,128)S(1)}, u32[]{:S(2)}, u32[]{:S(2)}) collective-permute-start(f32[1280,128]{1,0:T(8,128)S(1)} %get-tuple-element.67), channel_id=1, source_target_pairs={{0,1},{1,0},{4,5},{5,4},{8,9},{9,8},{12,13},{13,12},{14,15},{15,14... | collective-permute-start | bytes 1966088 | tf_op jit(solution)/shard_map/ppermute | solution.py:598
  29.9 7.3 %collective-permute-start.11 = (f32[1280,128]{1,0:T(8,128)S(1)}, f32[1280,128]{1,0:T(8,128)S(1)}, u32[]{:S(2)}, u32[]{:S(2)}) collective-permute-start(f32[1280,128]{1,0:T(8,128)S(1)} %get-tuple-element.81), channel_id=1, source_target_pairs={{1,4},{4,1},{5,8},{8,5},{9,12},{12,9},{13,14},{14,13},{15,10},{10,... | collective-permute-start | bytes 1966088 | tf_op jit(solution)/shard_map/ppermute | solution.py:597
  30.6 16.5 %collective-permute-start.8 = (f32[304,128]{1,0:T(8,128)S(1)}, f32[304,128]{1,0:T(8,128)S(1)}, u32[]{:S(2)}, u32[]{:S(2)}) collective-permute-start(f32[304,128]{1,0:T(8,128)S(1)} %get-tuple-element.75), channel_id=1, source_target_pairs={{0,5},{1,13},{2,11},{3,3},{4,4},{5,12},{6,10},{7,2},{8,1},{9,9},{1... | collective-permute-start | bytes 466952 | tf_op jit(solution)/shard_map/ppermute | solution.py:648
  33.9 13.2 %collective-permute-start.7 = (f32[304,128]{1,0:T(8,128)S(1)}, f32[304,128]{1,0:T(8,128)S(1)}, u32[]{:S(2)}, u32[]{:S(2)}) collective-permute-start(f32[304,128]{1,0:T(8,128)S(1)} %get-tuple-element.73), channel_id=1, source_target_pairs={{0,4},{1,12},{2,10},{3,2},{4,5},{5,13},{6,11},{7,3},{8,0},{9,8},{1... | collective-permute-start | bytes 466952 | tf_op jit(solution)/shard_map/ppermute | solution.py:648
  34.2 16.1 %collective-permute-start.6 = (f32[304,128]{1,0:T(8,128)S(1)}, f32[304,128]{1,0:T(8,128)S(1)}, u32[]{:S(2)}, u32[]{:S(2)}) collective-permute-start(f32[304,128]{1,0:T(8,128)S(1)} %get-tuple-element.71), channel_id=1, source_target_pairs={{0,1},{1,9},{2,15},{3,7},{4,0},{5,8},{6,14},{7,6},{8,5},{9,13},{10... | collective-permute-start | bytes 466952 | tf_op jit(solution)/shard_map/ppermute | solution.py:648
  36.5 13.8 %collective-permute-start.5 = (f32[304,128]{1,0:T(8,128)S(1)}, f32[304,128]{1,0:T(8,128)S(1)}, u32[]{:S(2)}, u32[]{:S(2)}) collective-permute-start(f32[304,128]{1,0:T(8,128)S(1)} %get-tuple-element.68), channel_id=1, source_target_pairs={{0,0},{1,8},{2,14},{3,6},{4,1},{5,9},{6,15},{7,7},{8,4},{9,12},{10... | collective-permute-start | bytes 466952 | tf_op jit(solution)/shard_map/ppermute | solution.py:648
  42.1 11.8 %collective-permute-start.12 = (f32[768,128]{1,0:T(8,128)S(1)}, f32[768,128]{1,0:T(8,128)S(1)}, u32[]{:S(2)}, u32[]{:S(2)}) collective-permute-start(f32[768,128]{1,0:T(8,128)S(1)} %get-tuple-element.88), channel_id=1, source_target_pairs={{1,4},{4,1},{5,8},{8,5},{9,12},{12,9},{13,14},{14,13},{15,10},{10,... | collective-permute-start | bytes 1179656 | tf_op jit(solution)/shard_map/ppermute | solution.py:597
  53.1 22.9 %collective-permute-start.10 = (f32[896,128]{1,0:T(8,128)S(1)}, f32[896,128]{1,0:T(8,128)S(1)}, u32[]{:S(2)}, u32[]{:S(2)}) collective-permute-start(f32[896,128]{1,0:T(8,128)S(1)} %get-tuple-element.78), channel_id=1, source_target_pairs={{0,1},{1,0},{4,5},{5,4},{8,9},{9,8},{12,13},{13,12},{14,15},{15,14... | collective-permute-start | bytes 1376264 | tf_op jit(solution)/shard_map/ppermute | solution.py:598
  53.1 22.8 %collective-permute-start.9 = (f32[896,128]{1,0:T(8,128)S(1)}, f32[896,128]{1,0:T(8,128)S(1)}, u32[]{:S(2)}, u32[]{:S(2)}) collective-permute-start(f32[896,128]{1,0:T(8,128)S(1)} %get-tuple-element.77), channel_id=1, source_target_pairs={{1,4},{4,1},{5,8},{8,5},{9,12},{12,9},{13,14},{14,13},{15,10},{10,... | collective-permute-start | bytes 1376264 | tf_op jit(solution)/shard_map/ppermute | solution.py:597
  58.7 10.5 %collective-permute-start.14 = (f32[768,128]{1,0:T(8,128)S(1)}, f32[768,128]{1,0:T(8,128)S(1)}, u32[]{:S(2)}, u32[]{:S(2)}) collective-permute-start(f32[768,128]{1,0:T(8,128)S(1)} %get-tuple-element.90), channel_id=1, source_target_pairs={{1,4},{4,1},{5,8},{8,5},{9,12},{12,9},{13,14},{14,13},{15,10},{10,... | collective-permute-start | bytes 1179656 | tf_op jit(solution)/shard_map/ppermute | solution.py:597
  59.5 9.7 %collective-permute-start.15 = (f32[768,128]{1,0:T(8,128)S(1)}, f32[768,128]{1,0:T(8,128)S(1)}, u32[]{:S(2)}, u32[]{:S(2)}) collective-permute-start(f32[768,128]{1,0:T(8,128)S(1)} %get-tuple-element.90), channel_id=1, source_target_pairs={{0,1},{1,0},{4,5},{5,4},{8,9},{9,8},{12,13},{13,12},{14,15},{15,14... | collective-permute-start | bytes 1179656 | tf_op jit(solution)/shard_map/ppermute | solution.py:598
  76.0 7.9 %collective-permute-start.16 = (f32[56,512]{1,0:T(8,128)S(1)}, f32[56,512]{1,0:T(8,128)S(1)}, u32[]{:S(2)}, u32[]{:S(2)}) collective-permute-start(f32[56,512]{1,0:T(8,128)S(1)} %shard_map.122.misfit), channel_id=1, source_target_pairs={{1,4},{4,1},{5,8},{8,5},{9,12},{12,9},{13,14},{14,13},{15,10},{10,... | collective-permute-start | bytes 344072 | tf_op jit(solution)/shard_map/ppermute | solution.py:597
  76.6 7.2 %collective-permute-start.17 = (f32[56,512]{1,0:T(8,128)S(1)}, f32[56,512]{1,0:T(8,128)S(1)}, u32[]{:S(2)}, u32[]{:S(2)}) collective-permute-start(f32[56,512]{1,0:T(8,128)S(1)} %shard_map.122.misfit), channel_id=1, source_target_pairs={{0,1},{1,0},{4,5},{5,4},{8,9},{9,8},{12,13},{13,12},{14,15},{15,14... | collective-permute-start | bytes 344072 | tf_op jit(solution)/shard_map/ppermute | solution.py:598
  90.6 8.3 %collective-permute-start.18 = (f32[768,128]{1,0:T(8,128)S(1)}, f32[768,128]{1,0:T(8,128)S(1)}, u32[]{:S(2)}, u32[]{:S(2)}) collective-permute-start(f32[768,128]{1,0:T(8,128)S(1)} %get-tuple-element.95), channel_id=1, source_target_pairs={{1,4},{4,1},{5,8},{8,5},{9,12},{12,9},{13,14},{14,13},{15,10},{10,... | collective-permute-start | bytes 1179656 | tf_op jit(solution)/shard_map/ppermute | solution.py:597
  91.6 7.4 %collective-permute-start.19 = (f32[768,128]{1,0:T(8,128)S(1)}, f32[768,128]{1,0:T(8,128)S(1)}, u32[]{:S(2)}, u32[]{:S(2)}) collective-permute-start(f32[768,128]{1,0:T(8,128)S(1)} %get-tuple-element.95), channel_id=1, source_target_pairs={{0,1},{1,0},{4,5},{5,4},{8,9},{9,8},{12,13},{13,12},{14,15},{15,14... | collective-permute-start | bytes 1179656 | tf_op jit(solution)/shard_map/ppermute | solution.py:598
  103.8 9.4 %collective-permute-start.20 = (f32[768,128]{1,0:T(8,128)S(1)}, f32[768,128]{1,0:T(8,128)S(1)}, u32[]{:S(2)}, u32[]{:S(2)}) collective-permute-start(f32[768,128]{1,0:T(8,128)S(1)} %get-tuple-element.97), channel_id=1, source_target_pairs={{1,4},{4,1},{5,8},{8,5},{9,12},{12,9},{13,14},{14,13},{15,10},{10,... | collective-permute-start | bytes 1179656 | tf_op jit(solution)/shard_map/ppermute | solution.py:597
  104.5 8.7 %collective-permute-start.21 = (f32[768,128]{1,0:T(8,128)S(1)}, f32[768,128]{1,0:T(8,128)S(1)}, u32[]{:S(2)}, u32[]{:S(2)}) collective-permute-start(f32[768,128]{1,0:T(8,128)S(1)} %get-tuple-element.97), channel_id=1, source_target_pairs={{0,1},{1,0},{4,5},{5,4},{8,9},{9,8},{12,13},{13,12},{14,15},{15,14... | collective-permute-start | bytes 1179656 | tf_op jit(solution)/shard_map/ppermute | solution.py:598
  118.8 10.2 %collective-permute-start.22 = (f32[176,128]{1,0:T(8,128)S(1)}, f32[176,128]{1,0:T(8,128)S(1)}, u32[]{:S(2)}, u32[]{:S(2)}) collective-permute-start(f32[176,128]{1,0:T(8,128)S(1)} %get-tuple-element.100), channel_id=1, source_target_pairs={{0,0},{8,1},{14,2},{6,3},{1,4},{9,5},{15,6},{7,7},{4,8},{12,9},{10... | collective-permute-start | bytes 270344 | tf_op jit(solution)/shard_map/ppermute | solution.py:757
  119.5 9.6 %collective-permute-start.23 = (f32[176,128]{1,0:T(8,128)S(1)}, f32[176,128]{1,0:T(8,128)S(1)}, u32[]{:S(2)}, u32[]{:S(2)}) collective-permute-start(f32[176,128]{1,0:T(8,128)S(1)} %get-tuple-element.101), channel_id=1, source_target_pairs={{1,0},{9,1},{15,2},{7,3},{0,4},{8,5},{14,6},{6,7},{5,8},{13,9},{11... | collective-permute-start | bytes 270344 | tf_op jit(solution)/shard_map/ppermute | solution.py:757
  124.0 6.7 %collective-permute-start.24 = (f32[176,128]{1,0:T(8,128)S(1)}, f32[176,128]{1,0:T(8,128)S(1)}, u32[]{:S(2)}, u32[]{:S(2)}) collective-permute-start(f32[176,128]{1,0:T(8,128)S(1)} %get-tuple-element.102), channel_id=1, source_target_pairs={{4,0},{12,1},{10,2},{2,3},{5,4},{13,5},{11,6},{3,7},{0,8},{8,9},{1... | collective-permute-start | bytes 270344 | tf_op jit(solution)/shard_map/ppermute | solution.py:757
  (5 other events, 12.2 us)
